TPU v7x, 512 devices: a whole 4x8x8 slice. The times are simulated.
512 devices in a mesh: gx: 8 (over y_lo, x), gy: 16 (over z, core), col: 4 (over y_hi).
Axes of the slice: x: 4, y: 8 (y_hi: 4, y_lo: 2; y = y_hi * 2 + y_lo), z: 8, core: 2. Of those that a mesh axis runs over, the one named last changes fastest.
Arguments:
- permeability: float32 [64, 128, 512], P('gx', 'gy', 'col'), may hold values from 0.1 to 10
- source: float32 [64, 128, 512], P('gx', 'gy', 'col'), may hold values from -2400 to 2400
- ownership: int32 [64, 128, 512], P('gx', 'gy', 'col'), may hold values from 0 to 63, as said below
- assignment: int32 [8, 16, 4, 64], P('gx', 'gy', 'col'), may hold values from 0 to 1023, as said below
- layer_flags: int32 [512], replicated, may hold values 0 or 1
Outputs:
- pressure: float32 [64, 128, 512], P('gx', 'gy', 'col')
- coarse_pressure: float32 [8, 1024], P('gx', ('gy', 'col'))
Inputs may be any that keep to these rules, and one draw needn't show every extreme that they name: `ownership`: every brick of 8 x 8 x 128 cells holds cells of every subdomain. `assignment`: in every slab every coarse cell is named by some subdomain; coarse cells hold unequal numbers of subdomains.
All inputs are finite; a program needn't handle non-finite values.
Results may differ from a plain program's by a relative error of at most 0.00013.
Values sent between devices are 32-bit elements; how exact they have to be, the bound alone decides.
No kernel may reach another device: no remote copies, remote signals or barrier semaphores. Data moves between devices by JAX's collectives and lax.ppermute only.
A program may use at most 64 MiB of HBM per device.

v0:
```python
import jax
import jax.numpy as jnp
from jax import lax
from jax.sharding import PartitionSpec as P

NSUB = 64
SWEEPS = 4


fine_relax = 0.6666667
coarse_relax = 0.7
rim_width = 5


def with_halo(block, sides, width):
    for axis, dim in sides:
        count = lax.axis_size(axis)
        forward = [(i, i + 1) for i in range(count - 1)]
        forward.append((count - 1, 0))
        backward = [(target, source) for source, target in forward]
        low = lax.ppermute(
            lax.slice_in_dim(block, block.shape[dim] - width, None, axis=dim), axis, forward
        )
        high = lax.ppermute(lax.slice_in_dim(block, 0, width, axis=dim), axis, backward)
        block = jnp.concatenate([low, block, high], axis=dim)
    return block


def harmonic(lower_value, upper_value):
    return 2.0 * lower_value * upper_value / (lower_value + upper_value)


def trim_edges(values, margin):
    return values[
        margin : values.shape[0] - margin,
        margin : values.shape[1] - margin,
        margin : values.shape[2] - margin,
    ]


def operator_local(values, terms, margin):
    plus_x, minus_x, plus_y, minus_y, plus_z, minus_z, diagonal = [
        trim_edges(one_term, rim_width - margin) for one_term in terms
    ]
    return diagonal * values[1:-1, 1:-1, 1:-1] - (
        plus_x * values[2:, 1:-1, 1:-1]
        + minus_x * values[:-2, 1:-1, 1:-1]
        + plus_y * values[1:-1, 2:, 1:-1]
        + minus_y * values[1:-1, :-2, 1:-1]
        + plus_z * values[1:-1, 1:-1, 2:]
        + minus_z * values[1:-1, 1:-1, :-2]
    )


def on_device(permeability, source, ownership, assignment, layer_flags):
    size_x, size_y, size_z = permeability.shape
    top_margin = rim_width - 1
    index_x = lax.axis_index("gx")
    index_y = lax.axis_index("gy")
    index_z = lax.axis_index("col")
    total_x = size_x * lax.axis_size("gx")
    total_y = size_y * lax.axis_size("gy")
    total_z = size_z * lax.axis_size("col")
    widened = with_halo(permeability, (("gx", 0), ("gy", 1), ("col", 2)), rim_width)
    spots_x = index_x * size_x + jnp.arange(-rim_width, size_x + rim_width)
    inside_x = (spots_x >= 0) & (spots_x < total_x)
    spots_z = index_z * size_z + jnp.arange(-rim_width, size_z + rim_width)
    inside_z = (spots_z >= 0) & (spots_z < total_z)
    spots_y = jnp.mod(index_y * size_y + jnp.arange(-rim_width, size_y + rim_width), total_y)
    inside = inside_x[:, None, None] & inside_z[None, None, :]
    widened = jnp.where(inside, widened, 1.0)
    padded_flags = jnp.pad(layer_flags, (rim_width, rim_width))
    local_flags = lax.dynamic_slice_in_dim(
        padded_flags, index_z * size_z, size_z + 2 * rim_width
    ).astype(jnp.float32)
    both_x = (inside_x[:-1] & inside_x[1:])[:, None, None]
    lower_x = inside_x[:-1][:, None, None]
    upper_x = inside_x[1:][:, None, None]
    faces_x = jnp.where(
        both_x,
        harmonic(widened[:-1], widened[1:]),
        jnp.where(lower_x, widened[:-1], jnp.where(upper_x, widened[1:], 0.0)),
    )
    faces_y = harmonic(widened[:, :-1], widened[:, 1:])
    edge_rows = (spots_y[:-1] == total_y - 1)[None, :, None]
    faces_y = jnp.where(edge_rows, faces_y * local_flags[None, None, :], faces_y)
    both_z = (inside_z[:-1] & inside_z[1:])[None, None, :]
    faces_z = jnp.where(both_z, harmonic(widened[:, :, :-1], widened[:, :, 1:]), 0.0)
    plus_x = faces_x[1:, 1:-1, 1:-1]
    minus_x = faces_x[:-1, 1:-1, 1:-1]
    plus_y = faces_y[1:-1, 1:, 1:-1]
    minus_y = faces_y[1:-1, :-1, 1:-1]
    plus_z = faces_z[1:-1, 1:-1, 1:]
    minus_z = faces_z[1:-1, 1:-1, :-1]
    diagonal = plus_x + minus_x + plus_y + minus_y + plus_z + minus_z
    terms = (plus_x, minus_x, plus_y, minus_y, plus_z, minus_z, diagonal)
    keep_mask = jnp.broadcast_to(inside, widened.shape).astype(jnp.float32)[1:-1, 1:-1, 1:-1]

    def restrict_step(values, margin):
        scaled = values / trim_edges(diagonal, top_margin - margin)
        moved = values[1:-1, 1:-1, 1:-1] - fine_relax * operator_local(scaled, terms, margin)
        return moved * trim_edges(keep_mask, rim_width - margin)

    def prolong_step(values, margin):
        moved = values[1:-1, 1:-1, 1:-1] - fine_relax * operator_local(
            values, terms, margin
        ) / trim_edges(diagonal, rim_width - margin)
        return moved * trim_edges(keep_mask, rim_width - margin)

    def sweeps(field, step_rule):
        for sweep_turn in range(SWEEPS):
            widened_field = with_halo(field, (("gx", 0), ("gy", 1), ("col", 2)), 1) * trim_edges(
                keep_mask, top_margin - 1
            )
            field = step_rule(widened_field, 1)
        return field

    sub_labels = jnp.arange(NSUB)
    shares = lax.axis_size("gy") * lax.axis_size("col")
    coarse_count = shares * NSUB // 4
    share_length = coarse_count // shares
    picks = (assignment.reshape(NSUB, 1) == jnp.arange(coarse_count)[None, :]).astype(jnp.float32)

    def subdomain_sums(field):

        def add_slice(running, pieces):
            slice_values, slice_owner = pieces
            hits = (slice_owner[None, :, :] == sub_labels[:, None, None]).astype(jnp.float32)
            return (
                running
                + jnp.einsum("yz,syz->s", slice_values, hits, precision=lax.Precision.HIGHEST),
                None,
            )

        running, unused = lax.scan(add_slice, jnp.zeros((NSUB,), jnp.float32), (field, ownership))
        return running

    def coarse_terms(field):
        return jnp.dot(subdomain_sums(field), picks, precision=lax.Precision.HIGHEST)

    def expand(coarse):
        per_subdomain = jnp.dot(picks, coarse, precision=lax.Precision.HIGHEST)
        return jnp.take(per_subdomain, ownership)

    diag_inner = trim_edges(diagonal, top_margin)
    weighted = sweeps(source, restrict_step)

    def slab_sums(pair):
        return lax.psum(pair, ("gy", "col"))

    coarse_rhs, coarse_diag = slab_sums((coarse_terms(weighted), coarse_terms(diag_inner)))
    first_guess = coarse_relax * coarse_rhs / coarse_diag
    widened_field = with_halo(
        sweeps(expand(first_guess), prolong_step), (("gx", 0), ("gy", 1), ("col", 2)), 1
    ) * trim_edges(keep_mask, top_margin - 1)
    image_field = sweeps(operator_local(widened_field, terms, 1), restrict_step)
    (image_total,) = slab_sums((coarse_terms(image_field),))
    second_guess = first_guess + coarse_relax * (coarse_rhs - image_total) / coarse_diag
    pressure = sweeps(expand(second_guess), prolong_step)
    coarse_out = lax.dynamic_slice_in_dim(
        second_guess, (index_y * lax.axis_size("col") + index_z) * share_length, share_length
    )
    return (pressure, coarse_out.reshape(1, share_length))


def solution(mesh):
    placed = (
        P("gx", "gy", "col"),
        P("gx", "gy", "col"),
        P("gx", "gy", "col"),
        P("gx", "gy", "col", None),
        P(),
    )
    return jax.shard_map(
        on_device,
        mesh=mesh,
        in_specs=placed,
        out_specs=(P("gx", "gy", "col"), P("gx", ("gy", "col"))),
        check_vma=False,
    )
```

profile of v0, /device:TPU:1, one launch (start us, length us, event | category | flops | bytes accessed | tf_op | source)
XLA Modules:
  0.0 868.5 jit_solution(677472225446875596)
XLA Ops:
  5.4 4.2 collective-permute-start.7
  11.6 5.5 collective-permute-start.1
  33.0 4.2 collective-permute-start.11
  40.4 4.2 collective-permute-start.5
  51.4 6.5 collective-permute-start.13
  65.0 5.8 collective-permute-start.16
  72.7 4.4 collective-permute-done.17
  81.4 4.1 collective-permute-start.19
  88.6 4.1 collective-permute-start.21
  96.5 4.5 collective-permute-start.23
  103.0 4.7 collective-permute-start.24
  112.4 4.8 collective-permute-start.26
  122.8 5.9 collective-permute-start.29
  136.8 146.2 %all-reduce.1 = (f32[1024]{0:T(1024)S(1)}, f32[1024]{0:T(1024)S(1)}) all-reduce(f32[1024]{0:T(1024)S(1)} %bitcast.92, f32[1024]{0:T(1024)S(1)} %bitcast.91), channel_id=1, replica_groups=mesh['gx'=8,'gy'=16,'col'=4] {'gy','col'}, use_global_device_ids=true, to_apply=%region_5.6 | all-reduce | flops 2048 | bytes 16384 | tf_op jit(solution)/shard_map/psum | solution.py:149
  283.2 48.9 %gather_fusion = f32[8192]{0:T(1024)S(1)} fusion(f32[64]{0:T(128)S(1)} %convolution_bitcast_fusion.4, s32[8192]{0:T(1024)S(1)} %bitcast_clamp_fusion), kind=kCustom, calls=%fused_computation.clone | custom fusion | bytes 98304 | tf_op jit(solution)/shard_map/jit(_take)/gather | solution.py:143
  340.4 5.6 collective-permute-start.33
  348.8 5.5 collective-permute-start.35
  356.2 4.8 collective-permute-start.36
  365.3 5.8 collective-permute-start.39
  375.8 4.4 collective-permute-start.41
  385.7 4.2 collective-permute-start.43
  390.7 6.0 collective-permute-start.45
  397.7 4.6 collective-permute-start.46
  424.5 5.6 collective-permute-start.52
  436.7 4.1 collective-permute-start.54
  455.8 4.0 collective-permute-start.59
  466.3 4.2 collective-permute-start.61
  492.1 4.6 collective-permute-start.67
  497.5 4.3 collective-permute-start.68
  505.0 4.6 collective-permute-start.70
  518.3 6.1 collective-permute-start.73
  525.1 4.0 collective-permute-start.74
  535.1 5.0 collective-permute-start.77
  546.1 5.1 collective-permute-start.79
  561.8 4.2 collective-permute-start.83
  572.2 141.7 %psum.23 = f32[1024]{0:T(1024)S(1)} all-reduce(f32[1024]{0:T(1024)S(1)} %bitcast.93), channel_id=1, replica_groups=mesh['gx'=8,'gy'=16,'col'=4] {'gy','col'}, use_global_device_ids=true, to_apply=%region_8.10 | all-reduce | flops 1024 | bytes 8192 | tf_op jit(solution)/shard_map/psum | solution.py:149
  714.1 48.9 %gather_fusion.1 = f32[8192]{0:T(1024)S(1)} fusion(f32[64]{0:T(128)S(1)} %convolution_bitcast_fusion.3, s32[8192]{0:T(1024)S(1)} %bitcast_clamp_fusion), kind=kCustom, calls=%fused_computation.1.clone | custom fusion | bytes 98304 | tf_op jit(solution)/shard_map/jit(_take)/gather | solution.py:143
  763.1 4.0 collective-permute-start.84
  767.1 4.3 collective-permute-start.85
  772.2 5.2 collective-permute-start.87
  780.3 5.5 collective-permute-start.89
  787.7 4.4 collective-permute-start.90
  796.7 5.5 collective-permute-start.93
  806.9 4.4 collective-permute-start.95
  817.3 4.2 collective-permute-start.97
  822.3 5.9 collective-permute-start.99
  829.1 4.6 collective-permute-start.100
  856.0 5.2 collective-permute-start.106
  (422 shorter events, 273.3 us)
Async XLA Ops:
  1.4 24.2 %collective-permute-start.6 = (f32[5,8,128]{2,1,0:T(8,128)S(1)}, f32[5,8,128]{2,1,0:T(8,128)S(1)}, u32[]{:S(2)}, u32[]{:S(2)}) collective-permute-start(f32[5,8,128]{2,1,0:T(8,128)S(1)} %get-tuple-element.291), channel_id=1, source_target_pairs={{0,64},{64,128},{128,192},{192,256},{256,320},{320,384},{384,448},... | collective-permute-start | bytes 61448 | tf_op jit(solution)/shard_map/ppermute | solution.py:21
  5.4 20.3 %collective-permute-start.7 = (f32[5,8,128]{2,1,0:T(8,128)S(1)}, f32[5,8,128]{2,1,0:T(8,128)S(1)}, u32[]{:S(2)}, u32[]{:S(2)}) collective-permute-start(f32[5,8,128]{2,1,0:T(8,128)S(1)} %get-tuple-element.290), channel_id=1, source_target_pairs={{64,0},{128,64},{192,128},{256,192},{320,256},{384,320},{448,384},... | collective-permute-start | bytes 61448 | tf_op jit(solution)/shard_map/ppermute | solution.py:24
  9.6 8.6 collective-permute-start
  18.3 10.4 %collective-permute-start.2 = (f32[10,1,128]{2,1,0:T(1,128)S(1)}, f32[10,1,128]{2,1,0:T(1,128)S(1)}, u32[]{:S(2)}, u32[]{:S(2)}) collective-permute-start(f32[10,1,128]{2,1,0:T(1,128)S(1)} %get-tuple-element.254), channel_id=1, source_target_pairs={{0,4},{4,8},{8,12},{12,16},{16,20},{20,24},{24,28},{28,32},{32,36}... | collective-permute-start | bytes 15368 | tf_op jit(solution)/shard_map/ppermute | solution.py:21
  29.7 14.9 %collective-permute-start.10 = (f32[18,18,5]{2,1,0:T(8,128)S(1)}, f32[18,18,5]{2,1,0:T(8,128)S(1)}, u32[]{:S(2)}, u32[]{:S(2)}) collective-permute-start(f32[18,18,5]{2,1,0:T(8,128)S(1)} %get-tuple-element.184), channel_id=1, source_target_pairs={{0,1},{1,2},{2,3},{3,0},{4,5},{5,6},{6,7},{7,4},{8,9},{9,10},{10,1... | collective-permute-start | bytes 19448 | tf_op jit(solution)/shard_map/ppermute | solution.py:21
  33.0 12.1 %collective-permute-start.11 = (f32[18,18,5]{2,1,0:T(8,128)S(1)}, f32[18,18,5]{2,1,0:T(8,128)S(1)}, u32[]{:S(2)}, u32[]{:S(2)}) collective-permute-start(f32[18,18,5]{2,1,0:T(8,128)S(1)} %get-tuple-element.185), channel_id=1, source_target_pairs={{1,0},{2,1},{3,2},{0,3},{5,4},{6,5},{7,6},{4,7},{9,8},{10,9},{11,1... | collective-permute-start | bytes 19448 | tf_op jit(solution)/shard_map/ppermute | solution.py:24
  37.2 10.6 %collective-permute-start.4 = (f32[10,10,1]{2,1,0:T(8,128)S(1)}, f32[10,10,1]{2,1,0:T(8,128)S(1)}, u32[]{:S(2)}, u32[]{:S(2)}) collective-permute-start(f32[10,10,1]{2,1,0:T(8,128)S(1)} %get-tuple-element.218), channel_id=1, source_target_pairs={{0,1},{1,2},{2,3},{3,0},{4,5},{5,6},{6,7},{7,4},{8,9},{9,10},{10,1... | collective-permute-start | bytes 1208 | tf_op jit(solution)/shard_map/ppermute | solution.py:21
  40.4 8.6 collective-permute-start.5
  49.5 8.5 collective-permute-start.12
  51.4 7.3 collective-permute-start.13
  65.0 7.7 collective-permute-start.16
  77.6 8.0 collective-permute-start.18
  86.3 7.0 collective-permute-start.20
  93.6 7.4 collective-permute-start.22
  103.0 8.0 collective-permute-start.24
  120.3 9.2 %collective-permute-start.28 = (f32[10,10,1]{2,1,0:T(8,128)S(1)}, f32[10,10,1]{2,1,0:T(8,128)S(1)}, u32[]{:S(2)}, u32[]{:S(2)}) collective-permute-start(f32[10,10,1]{2,1,0:T(8,128)S(1)} %get-tuple-element.212), channel_id=1, source_target_pairs={{0,1},{1,2},{2,3},{3,0},{4,5},{5,6},{6,7},{7,4},{8,9},{9,10},{10,1... | collective-permute-start | bytes 1208 | tf_op jit(solution)/shard_map/ppermute | solution.py:21
  122.8 7.4 collective-permute-start.29
  332.2 7.4 collective-permute-start.30
  346.9 7.4 collective-permute-start.34
  348.8 6.9 collective-permute-start.35
  356.2 8.1 collective-permute-start.36
  372.1 8.1 collective-permute-start.40
  382.3 7.7 collective-permute-start.42
  397.7 7.4 collective-permute-start.46
  409.1 7.6 collective-permute-start.48
  424.5 7.9 collective-permute-start.52
  436.7 7.9 collective-permute-start.54
  452.5 7.4 collective-permute-start.58
  463.1 7.4 collective-permute-start.60
  478.0 7.4 collective-permute-start.64
  481.7 7.3 collective-permute-start.65
  489.4 7.4 collective-permute-start.66
  505.0 7.8 collective-permute-start.70
  516.3 8.0 collective-permute-start.72
  532.5 7.6 collective-permute-start.76
  535.1 7.2 collective-permute-start.77
  542.7 8.5 collective-permute-start.78
  558.6 8.0 collective-permute-start.82
  561.8 7.3 collective-permute-start.83
  763.1 8.4 collective-permute-start.84
  778.4 7.4 collective-permute-start.88
  780.3 6.9 collective-permute-start.89
  787.7 8.1 collective-permute-start.90
  803.1 8.1 collective-permute-start.94
  813.4 8.2 collective-permute-start.96
  829.1 7.4 collective-permute-start.100
  840.5 7.6 collective-permute-start.102
  856.0 8.0 collective-permute-start.106
  (65 other events, 350.2 us)
where the time goes:
time: 876 us; the launch traced here: 868 us
  starting transfers between devices  377 us (43%)
  blocking collectives  288 us (33%)
  local copies, waits for them, and re-layouts  103 us (12%)
  waiting for transfers between devices  80.5 us (9%)
  other arithmetic  10.7 us (1%)
    psum x2, blocking collectives, slab_sums(): return lax.psum(pair, ('gy', 'col'))  288 us
    ppermute x54, starting transfers between devices, with_halo(): lax.ppermute(lax.slice_in_dim(block, 0, width, axis=dim), axis, backward)  208 us
    ppermute x54, starting transfers between devices, with_halo(): lax.ppermute(lax.slice_in_dim(block, block.shape[dim] - width, None, axis...  169 us
    gather x2, local copies, waits for them, and re-layouts, expand(): return jnp.take(per_subdomain, ownership)  97.8 us
    ppermute x54, waiting for transfers between devices, with_halo(): lax.ppermute(lax.slice_in_dim(block, 0, width, axis=dim), axis, backward)  65.9 us
  transfers between devices with their start and end apart: 108, of which 73 were waited for; matrix products, arithmetic and copies ran while one was open for 0% of the time, Pallas kernels for 0%

commit v1 on v0

v1 whole, which is shorter than its diff:
```python
import functools

import jax
import jax.numpy as jnp
from jax import lax
from jax.experimental import pallas as pl
from jax.experimental.pallas import tpu as pltpu
from jax.sharding import PartitionSpec as P

f32 = jnp.float32
i32 = jnp.int32
bf16 = jnp.bfloat16
NSUB = 64
B = 8
LZ = 128
NP = 3 * B
W = 9
fine_relax = 0.6666667
coarse_relax = 0.7
VMEM_LIMIT = 48 * 1024 * 1024

PERM, OWN, HZ, ASG, SRC = 0, 8, 16, 24, 25
STACK = 33
BASE = (0, 29, 62)
LINE = 91


def lanes(shape):
    return lax.broadcasted_iota(i32, shape, len(shape) - 1)


def rows(shape):
    return lax.broadcasted_iota(i32, shape, len(shape) - 2)


def call(kernel, outs, scratch=(), n_vmem=0, smem_first=False):
    specs = [pl.BlockSpec(memory_space=pltpu.VMEM)] * n_vmem
    if smem_first:
        specs = [pl.BlockSpec(memory_space=pltpu.SMEM)] + specs
    single = not isinstance(outs, (list, tuple))
    vm = pl.BlockSpec(memory_space=pltpu.VMEM)
    return pl.pallas_call(
        kernel,
        out_shape=outs,
        in_specs=specs,
        out_specs=vm if single else [vm] * len(outs),
        scratch_shapes=list(scratch),
        compiler_params=pltpu.CompilerParams(vmem_limit_bytes=VMEM_LIMIT),
    )


def sds(*shape, dtype=f32):
    return jax.ShapeDtypeStruct(shape, dtype)


def z_messages(perm, src, own, asg, mr, ml, xa, xb, ya, yb):
    lane = lanes((B, LZ))
    tile = jnp.concatenate([asg[...].astype(f32), jnp.zeros((1, LZ - NSUB), f32)], axis=1)
    tile = jnp.where(rows((B, LZ)) == 0, jnp.broadcast_to(tile, (B, LZ)), 0.0)
    for p in range(B):
        k, s, o = perm[p], src[p], own[p].astype(f32)
        mr[p] = jnp.where(
            lane < 16, k, jnp.where(lane < 32, pltpu.roll(o, 16, 1), pltpu.roll(s, 32, 1))
        )
        ml[p] = jnp.where(
            lane >= 112, k, jnp.where(lane >= 96, pltpu.roll(o, 112, 1), pltpu.roll(s, 96, 1))
        )
    for out in (mr, ml):
        out[B] = tile
    for out, at in ((xa, B - 1), (xb, 0)):
        out[0] = perm[at]
        out[1] = own[at].astype(f32)
        out[2] = tile
    for out, at in ((ya, B - 1), (yb, 0)):
        out[0] = perm[:, at, :]
        out[1] = own[:, at, :].astype(f32)
        out[2] = tile


def stack_up(perm, src, own, mr, ml, asg, stack):
    lane = lanes((B, LZ))
    for p in range(B):
        stack[PERM + p] = perm[p]
        stack[OWN + p] = own[p].astype(f32)
        stack[HZ + p] = jnp.where(lane < 64, mr[p], ml[p])
        stack[SRC + p] = src[p]
    tile = jnp.concatenate([asg[...].astype(f32), jnp.zeros((1, LZ - NSUB), f32)], axis=1)
    row = rows((B, LZ))
    stack[ASG] = jnp.where(
        row == 0,
        jnp.broadcast_to(tile, (B, LZ)),
        jnp.where(
            row == 1,
            jnp.broadcast_to(mr[B, 0:1, :], (B, LZ)),
            jnp.where(row == 2, jnp.broadcast_to(ml[B, 0:1, :], (B, LZ)), 0.0),
        ),
    )


def shifted(u):
    return (
        pltpu.roll(u, NP - 1, 0),
        pltpu.roll(u, 1, 0),
        pltpu.roll(u, 2 * LZ - 1, 1),
        pltpu.roll(u, 1, 1),
    )


def around(u_ref, w_ref, p, edge=None):
    u = u_ref[p + 1]
    up, down, right, left = shifted(u)
    if edge is not None:
        up, down = edge(up, down)
    return u, (
        (w_ref[0, p] * u_ref[p + 2] + w_ref[1, p] * u_ref[p])
        + (w_ref[2, p] * up + w_ref[3, p] * down)
        + (w_ref[4, p] * right + w_ref[5, p] * left)
    )


def sweep(src, dst, w_ref, first, last):
    def one(p, carry):
        u, near = around(src, w_ref, p)
        dst[p + 1] = (1.0 - fine_relax) * u + near
        return carry

    lax.fori_loop(first, last + 1, one, 0)


def label_sums(label_tiles, field_sets, sums):
    def one(s, carry):
        hits = [tile == s for tile in label_tiles]
        for k, tiles in enumerate(field_sets):
            parts = [jnp.where(hit, tile, 0.0) for hit, tile in zip(hits, tiles)]
            while len(parts) > 1:
                parts = [a + b for a, b in zip(parts[::2], parts[1::2])]
            sums[pl.ds(k * NSUB + s, 1), :] = jnp.sum(parts[0], axis=0, keepdims=True)
        return carry

    lax.fori_loop(0, NSUB, one, 0, unroll=4)


def lane_sums(sums):
    ones = jnp.ones((B, LZ), f32)
    return lax.dot_general(
        ones, sums, (((1,), (1,)), ((), ())),
        precision=lax.Precision.HIGHEST, preferred_element_type=f32,
    )


def harmonic(a, b):
    return 2.0 * a * b / (a + b)


def first_sums(n_gx, n_gy, n_col, idx, y_lo, y_mid, y_hi, xl, xr, yl, yr, flags,
               weights, labels, chunk, kext, fx, va, vb, fmul, zmul, dvals, sums):
    gx, gy, col = idx[0], idx[1], idx[2]
    lines = (y_lo, y_mid, y_hi)
    lane = lanes((B, LZ))
    halo = (lane < W) | (lane >= LZ - W)
    near_side = lane < 64

    def positive(t):
        return jnp.where(t > 0.0, t, 1.0)

    ones = jnp.ones((NP, 2 * LZ), f32)
    for at, plane in ((0, xl), (NP + 1, xr)):
        kext[at] = ones
        kext[at, B : 2 * B, 0:LZ] = positive(plane[0])

    for b in range(3):

        def fill(q, carry, b=b):
            p = b * B + q
            for ty in range(3):
                line = lines[ty]
                r = slice(ty * B, (ty + 1) * B)
                packed = line[BASE[b] + HZ + q]
                kext[p + 1, r, 0:LZ] = positive(line[BASE[b] + PERM + q])
                kext[p + 1, r, LZ:] = positive(jnp.where(halo, packed, 1.0))
                own = line[BASE[b] + OWN + q]
                labels[p, r, 0:LZ] = own.astype(i32)
                own_z = jnp.where(near_side, pltpu.roll(packed, LZ - 16, 1), pltpu.roll(packed, 16, 1))
                labels[p, r, LZ:] = jnp.where(halo, own_z, 0.0).astype(i32)
            return carry

        lax.fori_loop(0, B, fill, 0)

    flag_row = jnp.concatenate(
        [flags[1:2, :], jnp.where(lane[0:1] < 64, flags[2:3, :], flags[0:1, :])], axis=1
    )
    row_all, lane_all = rows((NP, 2 * LZ)), lanes((NP, 2 * LZ))
    wrap_row = jnp.where(
        gy == 0, B - 1, jnp.where(gy == n_gy - 1, 2 * B - 1, jnp.where(gy == n_gy - 2, NP - 1, -1))
    )
    fmul[...] = jnp.where(row_all == wrap_row, jnp.broadcast_to(flag_row, (NP, 2 * LZ)), 1.0)
    low_flag = jnp.where(gy == 1, flag_row, 1.0)
    closed = ((lane_all == LZ - 1) & (col == n_col - 1)) | ((lane_all == 2 * LZ - 1) & (col == 0))
    zmul[...] = jnp.where(closed, 0.0, 1.0)

    def x_face(p, carry):
        fx[p] = harmonic(kext[p], kext[p + 1])
        return carry

    lax.fori_loop(0, NP + 1, x_face, 0)

    @pl.when(gx == 0)
    def _():
        fx[B] = kext[B + 1]

    @pl.when(gx == n_gx - 1)
    def _():
        fx[2 * B] = kext[2 * B]

    for b in range(3):
        if b == 0:
            inside = jnp.where(gx > 0, 1.0, 0.0)
        elif b == 2:
            inside = jnp.where(gx < n_gx - 1, 1.0, 0.0)
        else:
            inside = 1.0

        def terms(q, carry, b=b, inside=inside):
            p = b * B + q
            k = kext[p + 1]
            k_up = pltpu.roll(k, NP - 1, 0)
            if b == 1:
                one = jnp.ones((1, LZ), f32)
                high = jnp.concatenate([positive(yr[0, pl.ds(q, 1), :]), one], axis=1)
                k_up = jnp.where(row_all == NP - 1, jnp.broadcast_to(high, k.shape), k_up)
            fy_up = harmonic(k, k_up) * fmul[...]
            fy_down = pltpu.roll(fy_up, 1, 0)
            if b == 1:
                low = jnp.concatenate([positive(yl[0, pl.ds(q, 1), :]), one], axis=1)
                edge = harmonic(low, k[0:1]) * low_flag
                fy_down = jnp.where(row_all == 0, jnp.broadcast_to(edge, k.shape), fy_down)
            fz_right = harmonic(k, pltpu.roll(k, 2 * LZ - 1, 1)) * zmul[...]
            fz_left = pltpu.roll(fz_right, 1, 1)
            fx_up, fx_down = fx[p + 1], fx[p]
            diag = fx_up + fx_down + fy_up + fy_down + fz_right + fz_left
            scale = (fine_relax * inside) / diag
            for i, face in enumerate((fx_up, fx_down, fy_up, fy_down, fz_right, fz_left)):
                weights[i, p] = face * scale
            if b == 1:
                dvals[q] = diag[B : 2 * B, 0:LZ]
            if b == 1:
                source_field(p, BASE[1] + SRC + q, diag)
            else:

                @pl.when((q >= 4) if b == 0 else (q < 4))
                def _():
                    source_field(p, (BASE[0] + SRC - 4 if b == 0 else BASE[2] + SRC) + q, diag)

            return carry

        def source_field(p, at, diag, b=b):
            hz = BASE[b] + HZ + (p - b * B)
            for ty in range(3):
                line = lines[ty]
                r = slice(ty * B, (ty + 1) * B)
                packed = line[hz]
                src_z = jnp.where(near_side, pltpu.roll(packed, LZ - 32, 1), pltpu.roll(packed, 32, 1))
                va[p + 1, r, 0:LZ] = line[at] / diag[r, 0:LZ]
                va[p + 1, r, LZ:] = jnp.where(halo, src_z, 0.0) / diag[r, LZ:]

        lax.fori_loop(0, B, terms, 0)

    sweep(va, vb, weights, 5, 18)
    sweep(vb, va, weights, 6, 17)
    sweep(va, vb, weights, 7, 16)
    sweep(vb, va, weights, 8, 15)
    tiles = [va[B + 1 + q, B : 2 * B, 0:LZ] * dvals[q] for q in range(B)]
    diag_tiles = [dvals[q] for q in range(B)]
    label_tiles = [labels[B + q, B : 2 * B, 0:LZ] for q in range(B)]
    label_sums(label_tiles, (tiles, diag_tiles), sums)
    totals = lane_sums(sums[...])
    asg = y_mid[BASE[1] + ASG]
    twice = jnp.where(lane < NSUB, asg, pltpu.roll(asg, NSUB, 1))
    row = rows((B, LZ))
    tile = jnp.where(
        row == 0, totals, jnp.where(row == 1, jnp.broadcast_to(twice[0:1], (B, LZ)), 0.0)
    )
    for d in range(n_gy):
        chunk[d] = tile


def coarse_partial(n_gy, n_out, sets, values, assigned, out):
    sub = rows((B, LZ))
    lane = lanes((B, LZ))
    wide = rows((LZ, LZ))
    total = None
    for g in range(n_gy):
        value = jnp.broadcast_to(values[g, 0:1, :], (B, LZ))
        a = jnp.broadcast_to(assigned[g, 1:2, :], (B, LZ)).astype(i32)
        high = (a >> 7) == sub
        parts = [
            jnp.where(high & ((lane >= NSUB * i) & (lane < NSUB * (i + 1))), value, 0.0)
            for i in range(sets)
        ]
        left = jnp.concatenate(parts, axis=0)
        l1 = left.astype(bf16)
        rest = left - l1.astype(f32)
        l2 = rest.astype(bf16)
        l3 = (rest - l2.astype(f32)).astype(bf16)
        low = jnp.broadcast_to((a & 127)[0:1], (LZ, LZ)) == wide
        right = jnp.where(low, 1.0, 0.0).astype(bf16)
        for part in (l1, l2, l3):
            more = lax.dot_general(
                part, right, (((1,), (1,)), ((), ())), preferred_element_type=f32
            )
            total = more if total is None else total + more
    for d in range(n_out):
        out[d] = total


def lookup(table, index):
    low, high = index & 127, index >> 7
    result = jnp.zeros((B, LZ), f32)
    for h in range(B):
        got = jnp.take_along_axis(jnp.broadcast_to(table[h : h + 1], (B, LZ)), low, axis=1)
        result = jnp.where(high == h, got, result)
    return result


def pick(row, index):
    return jnp.take_along_axis(jnp.broadcast_to(row, (B, LZ)), index, axis=1)


def slab_totals(parts, g, n_gx, n_col):
    exists = (g >= 0) & (g < n_gx)
    at = jnp.clip(g, 0, n_gx - 1) * n_col
    total = parts[at]
    for c in range(1, n_col):
        total = total + parts[at + c]
    return total, exists


def guess(parts, g, n_gx, n_col):
    total, exists = slab_totals(parts, g, n_gx, n_col)
    rhs, diag = total[0:B], total[B : 2 * B]
    return rhs, diag, jnp.where(exists, coarse_relax * rhs / diag, 0.0)


def expand(coarse, lines, labels, u, first, last):
    near_side = lanes((B, LZ)) < 64
    for b in range(3):
        tables = [
            lookup(coarse[b], lines[ty][BASE[b] + ASG].astype(i32)) for ty in range(3)
        ]

        def one(p, carry, tables=tables):
            for ty in range(3):
                r = slice(ty * B, (ty + 1) * B)
                t = tables[ty]
                u[p + 1, r, 0:LZ] = pick(t[0:1], labels[p, r, 0:LZ])
                lab = labels[p, r, LZ:]
                u[p + 1, r, LZ:] = jnp.where(near_side, pick(t[1:2], lab), pick(t[2:3], lab))
            return carry

        lax.fori_loop(max(first, b * B), min(last + 1, (b + 1) * B), one, 0)


def second_sums(n_gx, n_gy, n_col, idx, parts, weights, labels, y_lo, y_mid, y_hi,
                xl, xr, yl, yr, dvals, chunk, ua, ub, ends, sums):
    gx = idx[0]
    lines = (y_lo, y_mid, y_hi)
    coarse = [guess(parts, gx + s, n_gx, n_col)[2] for s in (-2, -1, 0, 1, 2)]
    expand(coarse[1:4], lines, labels, ua, 0, NP - 1)
    zero = jnp.zeros((NP, 2 * LZ), f32)
    for at, plane, c in ((0, xl, coarse[0]), (NP + 1, xr, coarse[4])):
        ua[at] = zero
        table = lookup(c, plane[2].astype(i32))
        ua[at, B : 2 * B, 0:LZ] = pick(table[0:1], plane[1].astype(i32))
    for at, line in ((0, yl), (1, yr)):
        table = lookup(coarse[2], line[2].astype(i32))
        ends[at] = pick(table[0:1], line[1].astype(i32))
    row_all = rows((NP, 2 * LZ))
    blank = jnp.zeros((1, LZ), f32)
    for b in range(3):

        def one(q, carry, b=b):
            p = b * B + q

            def edge(up, down):
                high = jnp.concatenate([ends[1, pl.ds(q, 1), :], blank], axis=1)
                low = jnp.concatenate([ends[0, pl.ds(q, 1), :], blank], axis=1)
                return (
                    jnp.where(row_all == NP - 1, jnp.broadcast_to(high, up.shape), up),
                    jnp.where(row_all == 0, jnp.broadcast_to(low, down.shape), down),
                )

            u, near = around(ua, weights, p, edge if b == 1 else None)
            ub[p + 1] = (1.0 - fine_relax) * u + near
            return carry

        lax.fori_loop(0, B, one, 0)
    sweep(ub, ua, weights, 1, 22)
    sweep(ua, ub, weights, 2, 21)
    sweep(ub, ua, weights, 3, 20)

    def operator(p, carry):
        u, near = around(ua, weights, p)
        ub[p + 1] = u - near * (1.0 / fine_relax)
        return carry

    lax.fori_loop(4, 20, operator, 0)
    sweep(ub, ua, weights, 5, 18)
    sweep(ua, ub, weights, 6, 17)
    sweep(ub, ua, weights, 7, 16)
    sweep(ua, ub, weights, 8, 15)
    tiles = [ub[B + 1 + q, B : 2 * B, 0:LZ] * dvals[q] for q in range(B)]
    label_tiles = [labels[B + q, B : 2 * B, 0:LZ] for q in range(B)]
    label_sums(label_tiles, (tiles,), sums)
    totals = lane_sums(sums[...])
    tile = jnp.concatenate([totals, jnp.zeros((B, LZ - NSUB), f32)], axis=1)
    for d in range(n_gy):
        chunk[d] = tile


def last_sweeps(n_gx, n_gy, n_col, idx, parts, images, weights, labels, y_lo, y_mid, y_hi,
                pressure, coarse_out, ua, ub, held):
    gx, gy, col = idx[0], idx[1], idx[2]
    lines = (y_lo, y_mid, y_hi)
    coarse = []
    for s in (-1, 0, 1):
        rhs, diag, start = guess(parts, gx + s, n_gx, n_col)
        image, exists = slab_totals(images, gx + s, n_gx, n_col)
        coarse.append(
            jnp.where(exists, start + coarse_relax * (rhs - image) / diag, 0.0)
        )
    held[...] = coarse[1]
    share = B * LZ // (n_gy * n_col)
    per_row = LZ // share
    mine = gy * n_col + col
    row = held[pl.ds(mine // per_row, 1), :]
    turned = pltpu.roll(
        jnp.broadcast_to(row, (B, LZ)), lax.rem(LZ - lax.rem(mine, per_row) * share, LZ), 1
    )
    coarse_out[...] = turned[0:1, 0:share]
    expand(coarse, lines, labels, ua, 4, 19)
    sweep(ua, ub, weights, 5, 18)
    sweep(ub, ua, weights, 6, 17)
    sweep(ua, ub, weights, 7, 16)

    def one(q, carry):
        u, near = around(ub, weights, B + q)
        moved = (1.0 - fine_relax) * u + near
        pressure[q] = moved[B : 2 * B, 0:LZ]
        return carry

    lax.fori_loop(0, B, one, 0)


def steps(count, by, wrap):
    return [
        (i, (i + by) % count) for i in range(count) if wrap or 0 <= i + by < count
    ]


def on_device(n_gx, n_gy, n_col, permeability, source, ownership, assignment, layer_flags):
    idx = jnp.stack([lax.axis_index(a) for a in ("gx", "gy", "col")]).astype(i32)
    asg = assignment.reshape(1, NSUB)
    flags = layer_flags.astype(f32)
    flags = lax.dynamic_slice_in_dim(
        jnp.pad(flags, (LZ, LZ)), lax.axis_index("col") * LZ, 3 * LZ
    ).reshape(3, LZ)
    n_out = n_gx * n_col

    def send(x, axis, by, wrap=False):
        return lax.ppermute(x, axis, steps({"gx": n_gx, "gy": n_gy, "col": n_col}[axis], by, wrap))

    mr, ml, xa, xb, ya, yb = call(
        z_messages, [sds(B + 1, B, LZ)] * 2 + [sds(3, B, LZ)] * 4, n_vmem=4
    )(permeability, source, ownership, asg)
    mr, ml = send(mr, "col", -1), send(ml, "col", 1)
    stack = call(stack_up, sds(STACK, B, LZ), n_vmem=6)(
        permeability, source, ownership, mr, ml, asg
    )
    low, high = send(stack, "gx", 1), send(stack, "gx", -1)
    xl, xr = send(xa, "gx", 2), send(xb, "gx", -2)
    line = jnp.concatenate([low[:SRC], low[SRC + 4 :], stack, high[: SRC + 4]], axis=0)
    y_lo, y_hi = send(line, "gy", 1, True), send(line, "gy", -1, True)
    yl, yr = send(ya, "gy", 2, True), send(yb, "gy", -2, True)

    full = (NP, 2 * LZ)
    weights, labels, chunk, dvals = call(
        functools.partial(drop_dvals, functools.partial(first_sums, n_gx, n_gy, n_col)),
        [sds(6, NP, *full), sds(NP, *full, dtype=i32), sds(n_gy, B, LZ), sds(B, B, LZ)],
        scratch=[
            pltpu.VMEM((NP + 2, *full), f32),
            pltpu.VMEM((NP + 1, *full), f32),
            pltpu.VMEM((NP + 2, *full), f32),
            pltpu.VMEM((NP + 2, *full), f32),
            pltpu.VMEM(full, f32),
            pltpu.VMEM(full, f32),
            pltpu.VMEM((2 * NSUB, LZ), f32),
        ],
        n_vmem=8,
        smem_first=True,
    )(idx, y_lo, line, y_hi, xl, xr, yl, yr, flags)
    bricks = lax.all_to_all(chunk, "gy", 0, 0, tiled=True)
    parts = call(
        functools.partial(coarse_partial, n_gy, n_out, 2), sds(n_out, 2 * B, LZ), n_vmem=2
    )(bricks, bricks)
    parts = lax.all_to_all(parts, ("gx", "col"), 0, 0, tiled=True)
    chunk = call(
        functools.partial(second_sums, n_gx, n_gy, n_col),
        sds(n_gy, B, LZ),
        scratch=[
            pltpu.VMEM((NP + 2, *full), f32),
            pltpu.VMEM((NP + 2, *full), f32),
            pltpu.VMEM((2, B, LZ), f32),
            pltpu.VMEM((NSUB, LZ), f32),
        ],
        n_vmem=11,
        smem_first=True,
    )(idx, parts, weights, labels, y_lo, line, y_hi, xl, xr, yl, yr, dvals)
    images = lax.all_to_all(chunk, "gy", 0, 0, tiled=True)
    images = call(
        functools.partial(coarse_partial, n_gy, n_out, 1), sds(n_out, B, LZ), n_vmem=2
    )(images, bricks)
    images = lax.all_to_all(images, ("gx", "col"), 0, 0, tiled=True)
    share = B * LZ // (n_gy * n_col)
    pressure, coarse = call(
        functools.partial(last_sweeps, n_gx, n_gy, n_col),
        [sds(B, B, LZ), sds(1, share)],
        scratch=[
            pltpu.VMEM((NP + 2, *full), f32),
            pltpu.VMEM((NP + 2, *full), f32),
            pltpu.VMEM((B, LZ), f32),
        ],
        n_vmem=7,
        smem_first=True,
    )(idx, parts, images, weights, labels, y_lo, line, y_hi)
    return pressure, coarse


def drop_dvals(kernel, idx, y_lo, y_mid, y_hi, xl, xr, yl, yr, flags,
               weights, labels, chunk, dvals, kext, fx, va, vb, fmul, zmul, sums):
    kernel(idx, y_lo, y_mid, y_hi, xl, xr, yl, yr, flags,
           weights, labels, chunk, kext, fx, va, vb, fmul, zmul, dvals, sums)


def solution(mesh):
    placed = (
        P("gx", "gy", "col"),
        P("gx", "gy", "col"),
        P("gx", "gy", "col"),
        P("gx", "gy", "col", None),
        P(),
    )
    sizes = mesh.shape
    return jax.shard_map(
        functools.partial(on_device, sizes["gx"], sizes["gy"], sizes["col"]),
        mesh=mesh,
        in_specs=placed,
        out_specs=(P("gx", "gy", "col"), P("gx", ("gy", "col"))),
        check_vma=False,
    )
```

time: 876 us -> 147 us (0.17)
  starting transfers between devices: 377 us -> 32.9 us
  blocking collectives: 288 us -> 65.9 us
  local copies, waits for them, and re-layouts: 103 us -> 3.02 us
  waiting for transfers between devices: 80.5 us -> 6.21 us
  Pallas kernels: 0 us -> 36.9 us
  other arithmetic: 10.7 us -> 0.79 us
    ppermute x108 -> x10, starting transfers between devices: 377 us -> 32.9 us  [send(): lax.ppermute(x, axis, steps({'gx': n_gx, 'gy': n_gy, 'col': n_col}[axis],...]
    psum x2 -> x0, blocking collectives: 288 us -> none  [slab_sums(): return lax.psum(pair, ('gy', 'col'))]
    gather x2 -> x0, local copies, waits for them, and re-layouts: 97.8 us -> none  [expand(): return jnp.take(per_subdomain, ownership)]
    ppermute x108 -> x10, waiting for transfers between devices: 80.5 us -> 6.21 us  [send(): lax.ppermute(x, axis, steps({'gx': n_gx, 'gy': n_gy, 'col': n_col}[axis],...]
    all_to_all x0 -> x4, blocking collectives: none -> 65.9 us  [the longest x1 26 us: on_device(): parts = lax.all_to_all(parts, ('gx', 'col'), 0, 0, tiled=True)]
    pallas_call x0 -> x7, Pallas kernels: none -> 36.9 us  [the longest x1 16.4 us: on_device(): call(functools.partial(second_sums, n_gx, n_gy, n_col), sds(n_gy, B, LZ),...]
  transfers between devices with their start and end apart: 108 -> 10, of which waited for: 73 -> 4; matrix products, arithmetic and copies ran while one was open for 0% -> 1% of each run, Pallas kernels for 0% -> 0%
where the time goes in v1:
time: 147 us
  blocking collectives  65.9 us (45%)
  Pallas kernels  36.9 us (25%)
  starting transfers between devices  32.9 us (22%)
  waiting for transfers between devices  6.21 us (4%)
  local copies, waits for them, and re-layouts  3.02 us (2%)
    ppermute x10, starting transfers between devices, send(): lax.ppermute(x, axis, steps({'gx': n_gx, 'gy': n_gy, 'col': n_col}[axis],...  32.9 us
    all_to_all x1, blocking collectives, on_device(): parts = lax.all_to_all(parts, ('gx', 'col'), 0, 0, tiled=True)  26 us
    pallas_call x1, Pallas kernels, on_device(): call(functools.partial(second_sums, n_gx, n_gy, n_col), sds(n_gy, B, LZ),...  16.4 us
    all_to_all x1, blocking collectives, on_device(): bricks = lax.all_to_all(chunk, 'gy', 0, 0, tiled=True)  14.6 us
    all_to_all x1, blocking collectives, on_device(): images = lax.all_to_all(images, ('gx', 'col'), 0, 0, tiled=True)  12.7 us
    all_to_all x1, blocking collectives, on_device(): images = lax.all_to_all(chunk, 'gy', 0, 0, tiled=True)  12.6 us
    pallas_call x1, Pallas kernels, on_device(): call(functools.partial(drop_dvals, functools.partial(first_sums, n_gx, n_...  12 us
    pallas_call x1, Pallas kernels, on_device(): call(functools.partial(last_sweeps, n_gx, n_gy, n_col), [sds(B, B, LZ), s...  6.57 us
  transfers between devices with their start and end apart: 10, of which 4 were waited for; matrix products, arithmetic and copies ran while one was open for 1% of the time, Pallas kernels for 0%

profile of v1, /device:TPU:1, one launch (start us, length us, event | category | flops | bytes accessed | tf_op | source)
XLA Modules:
  0.0 146.5 jit_solution(15880824823912342214)
XLA Ops:
  0.6 0.0 copy-start
  0.6 0.7 copy-done
  1.4 0.0 copy-start.1
  1.4 0.8 copy-done.1
  2.1 0.0 copy-start.2
  2.1 0.8 copy-done.2
  2.9 0.0 copy-start.3
  2.9 0.7 copy-done.3
  3.6 0.1 shard_map.68
  3.7 1.3 collective-permute-start
  5.0 5.7 %collective-permute-start.1 = (f32[9,8,128]{2,1,0:T(8,128)S(1)}, f32[9,8,128]{2,1,0:T(8,128)S(1)}, u32[]{:S(2)}, u32[]{:S(2)}) collective-permute-start(f32[9,8,128]{2,1,0:T(8,128)S(1)} %get-tuple-element.13), channel_id=1, source_target_pairs={{0,1},{1,2},{2,3},{4,5},{5,6},{6,7},{8,9},{9,10},{10,11},{12,13},{... | collective-permute-start | bytes 110600 | tf_op jit(solution)/shard_map/ppermute | solution.py:470
  10.6 0.0 collective-permute-done.mr
  10.7 1.0 collective-permute-done.1.ml
  11.7 3.2 %collective-permute-start.2 = (f32[33,8,128]{2,1,0:T(8,128)S(1)}, f32[33,8,128]{2,1,0:T(8,128)S(1)}, u32[]{:S(2)}, u32[]{:S(2)}) collective-permute-start(f32[33,8,128]{2,1,0:T(8,128)S(1)} %shard_map.69), channel_id=1, source_target_pairs={{0,64},{64,128},{128,192},{192,256},{256,320},{320,384},{384,448},... | collective-permute-start | bytes 405512 | tf_op jit(solution)/shard_map/ppermute | solution.py:470
  14.9 1.3 collective-permute-start.3
  16.2 0.7 collective-permute-done.2
  16.9 3.8 %collective-permute-done.3 = f32[33,8,128]{2,1,0:T(8,128)S(1)} collective-permute-done((f32[33,8,128]{2,1,0:T(8,128)S(1)}, f32[33,8,128]{2,1,0:T(8,128)S(1)}, u32[]{:S(2)}, u32[]{:S(2)}) %collective-permute-start.3) | collective-permute-done | bytes 135200 | tf_op jit(solution)/shard_map/ppermute | solution.py:470
  20.7 6.5 %collective-permute-start.5 = (f32[91,8,128]{2,1,0:T(8,128)S(1)}, f32[91,8,128]{2,1,0:T(8,128)S(1)}, u32[]{:S(2)}, u32[]{:S(2)}) collective-permute-start(f32[91,8,128]{2,1,0:T(8,128)S(1)} %pad_maximum_fusion.y_mid), channel_id=1, source_target_pairs={{0,60},{4,0},{8,4},{12,8},{16,12},{20,16},{24,20},{28,24},{32,28},... | collective-permute-start | bytes 1118216 | tf_op jit(solution)/shard_map/ppermute | solution.py:470
  27.2 0.0 collective-permute-start.4
  27.2 3.1 %collective-permute-start.6 = (f32[3,8,128]{2,1,0:T(8,128)S(1)}, f32[3,8,128]{2,1,0:T(8,128)S(1)}, u32[]{:S(2)}, u32[]{:S(2)}) collective-permute-start(f32[3,8,128]{2,1,0:T(8,128)S(1)} %get-tuple-element.14), channel_id=1, source_target_pairs={{0,128},{64,192},{128,256},{192,320},{256,384},{320,448},{1,129},{... | collective-permute-start | bytes 36872 | tf_op jit(solution)/shard_map/ppermute | solution.py:470
  30.3 1.3 collective-permute-start.7
  31.6 4.0 %collective-permute-start.8 = (f32[3,8,128]{2,1,0:T(8,128)S(1)}, f32[3,8,128]{2,1,0:T(8,128)S(1)}, u32[]{:S(2)}, u32[]{:S(2)}) collective-permute-start(f32[3,8,128]{2,1,0:T(8,128)S(1)} %get-tuple-element.16), channel_id=1, source_target_pairs={{0,8},{4,12},{8,16},{12,20},{16,24},{20,28},{24,32},{28,36},{32,40... | collective-permute-start | bytes 36872 | tf_op jit(solution)/shard_map/ppermute | solution.py:470
  35.6 0.7 convert_element_type.5
  36.3 0.1 fusion.flags
  36.4 0.0 collective-permute-done.6.xl
  36.4 6.6 %collective-permute-start.9 = (f32[3,8,128]{2,1,0:T(8,128)S(1)}, f32[3,8,128]{2,1,0:T(8,128)S(1)}, u32[]{:S(2)}, u32[]{:S(2)}) collective-permute-start(f32[3,8,128]{2,1,0:T(8,128)S(1)} %get-tuple-element.17), channel_id=1, source_target_pairs={{0,56},{4,60},{8,0},{12,4},{16,8},{20,12},{24,16},{28,20},{32,24},... | collective-permute-start | bytes 36872 | tf_op jit(solution)/shard_map/ppermute | solution.py:470
  43.0 0.1 pad_add_fusion.idx
  43.0 0.0 collective-permute-done.7.xr
  43.0 0.0 collective-permute-done.8.yl
  43.0 0.7 collective-permute-done.9.yr
  43.8 0.0 collective-permute-done.5.y_hi
  43.8 0.0 collective-permute-done.4.y_lo
  43.8 12.0 %shard_map.70 = (f32[6,24,24,256]{3,2,1,0:T(8,128)S(1)}, s32[24,24,256]{2,1,0:T(8,128)S(1)}, f32[16,8,128]{2,1,0:T(8,128)S(1)}, f32[8,8,128]{2,1,0:T(8,128)S(1)}) custom-call(s32[3]{0:T(128)S(1)} %pad_add_fusion.idx, f32[91,8,128]{2,1,0:T(8,128)S(1)} %collective-permute-done.4.y_lo, f32[91,8,128]{2,1,0:T(8,128)S(1)} %pad_maximum_fusion.y_mid, ...), custom_call_target="tpu_custom_call" | custom-call | tf_op jit(solution)/shard_map/pallas_call | solution.py:486
  55.7 14.6 %all_to_all.20.values.assigned = f32[16,8,128]{2,1,0:T(8,128)S(1)} all-to-all(f32[16,8,128]{2,1,0:T(8,128)S(1)} %get-tuple-element.18), channel_id=1, replica_groups=mesh['gx'=8,'gy'=16,'col'=4] {'gy'}, dimensions={0} | all-to-all | bytes 131072 | tf_op jit(solution)/shard_map/all_to_all | solution.py:501
  70.3 0.9 shard_map.71
  71.2 26.0 %all_to_all.21.parts = f32[32,16,128]{2,1,0:T(8,128)S(1)} all-to-all(f32[32,16,128]{2,1,0:T(8,128)S(1)} %shard_map.71), channel_id=1, replica_groups=mesh['gx'=8,'gy'=16,'col'=4] {'gx','col'}, dimensions={0} | all-to-all | bytes 524288 | tf_op jit(solution)/shard_map/all_to_all | solution.py:505
  97.3 16.4 %shard_map.72 = f32[16,8,128]{2,1,0:T(8,128)S(1)} custom-call(s32[3]{0:T(128)S(1)} %pad_add_fusion.idx, f32[32,16,128]{2,1,0:T(8,128)S(1)} %all_to_all.21.parts, f32[6,24,24,256]{3,2,1,0:T(8,128)S(1)} %get-tuple-element.19.weights, s32[24,24,256]{2,1,0:T(8,128)S(1)} %get-tuple-element.20.labels, f32[91,8,128]{2,1,0:T(8,128)S(1)} %collective-permute-done.4.y_lo, ...), custom_call_target="tpu_custom_call" | custom-call | tf_op jit(solution)/shard_map/pallas_call | solution.py:506
  113.7 12.6 %all_to_all.22.values = f32[16,8,128]{2,1,0:T(8,128)S(1)} all-to-all(f32[16,8,128]{2,1,0:T(8,128)S(1)} %shard_map.72), channel_id=1, replica_groups=mesh['gx'=8,'gy'=16,'col'=4] {'gy'}, dimensions={0} | all-to-all | bytes 131072 | tf_op jit(solution)/shard_map/all_to_all | solution.py:518
  126.3 0.9 shard_map.73
  127.2 12.7 %all_to_all.23.images = f32[32,8,128]{2,1,0:T(8,128)S(1)} all-to-all(f32[32,8,128]{2,1,0:T(8,128)S(1)} %shard_map.73), channel_id=1, replica_groups=mesh['gx'=8,'gy'=16,'col'=4] {'gx','col'}, dimensions={0} | all-to-all | bytes 262144 | tf_op jit(solution)/shard_map/all_to_all | solution.py:522
  139.9 6.6 %shard_map.74 = (f32[8,8,128]{2,1,0:T(8,128)}, f32[1,16]{1,0:T(1,128)}) custom-call(s32[3]{0:T(128)S(1)} %pad_add_fusion.idx, f32[32,16,128]{2,1,0:T(8,128)S(1)} %all_to_all.21.parts, f32[32,8,128]{2,1,0:T(8,128)S(1)} %all_to_all.23.images, f32[6,24,24,256]{3,2,1,0:T(8,128)S(1)} %get-tuple-element.19.weights, s32[24,24,256]{2,1,0:T(8,128)S(1)} %get-tuple-element.20.labels, ...), custom_call_target="tpu_custom_call" | custom-call | tf_op jit(solution)/shard_map/pallas_call | solution.py:524
  (5 shorter events, 0.1 us)
Async XLA Ops:
  0.6 0.8 copy-start
  1.4 0.8 copy-start.1
  2.1 0.8 copy-start.2
  2.9 0.7 copy-start.3
  3.7 7.0 %collective-permute-start = (f32[9,8,128]{2,1,0:T(8,128)S(1)}, f32[9,8,128]{2,1,0:T(8,128)S(1)}, u32[]{:S(2)}, u32[]{:S(2)}) collective-permute-start(f32[9,8,128]{2,1,0:T(8,128)S(1)} %get-tuple-element.12), channel_id=1, source_target_pairs={{1,0},{2,1},{3,2},{5,4},{6,5},{7,6},{9,8},{10,9},{11,10},{13,12},{... | collective-permute-start | bytes 110600 | tf_op jit(solution)/shard_map/ppermute | solution.py:470
  5.0 6.7 %collective-permute-start.1 = (f32[9,8,128]{2,1,0:T(8,128)S(1)}, f32[9,8,128]{2,1,0:T(8,128)S(1)}, u32[]{:S(2)}, u32[]{:S(2)}) collective-permute-start(f32[9,8,128]{2,1,0:T(8,128)S(1)} %get-tuple-element.13), channel_id=1, source_target_pairs={{0,1},{1,2},{2,3},{4,5},{5,6},{6,7},{8,9},{9,10},{10,11},{12,13},{... | collective-permute-start | bytes 110600 | tf_op jit(solution)/shard_map/ppermute | solution.py:470
  11.7 5.1 %collective-permute-start.2 = (f32[33,8,128]{2,1,0:T(8,128)S(1)}, f32[33,8,128]{2,1,0:T(8,128)S(1)}, u32[]{:S(2)}, u32[]{:S(2)}) collective-permute-start(f32[33,8,128]{2,1,0:T(8,128)S(1)} %shard_map.69), channel_id=1, source_target_pairs={{0,64},{64,128},{128,192},{192,256},{256,320},{320,384},{384,448},... | collective-permute-start | bytes 405512 | tf_op jit(solution)/shard_map/ppermute | solution.py:470
  14.9 5.8 %collective-permute-start.3 = (f32[33,8,128]{2,1,0:T(8,128)S(1)}, f32[33,8,128]{2,1,0:T(8,128)S(1)}, u32[]{:S(2)}, u32[]{:S(2)}) collective-permute-start(f32[33,8,128]{2,1,0:T(8,128)S(1)} %shard_map.69), channel_id=1, source_target_pairs={{64,0},{128,64},{192,128},{256,192},{320,256},{384,320},{448,384},... | collective-permute-start | bytes 405512 | tf_op jit(solution)/shard_map/ppermute | solution.py:470
  20.7 23.1 %collective-permute-start.5 = (f32[91,8,128]{2,1,0:T(8,128)S(1)}, f32[91,8,128]{2,1,0:T(8,128)S(1)}, u32[]{:S(2)}, u32[]{:S(2)}) collective-permute-start(f32[91,8,128]{2,1,0:T(8,128)S(1)} %pad_maximum_fusion.y_mid), channel_id=1, source_target_pairs={{0,60},{4,0},{8,4},{12,8},{16,12},{20,16},{24,20},{28,24},{32,28},... | collective-permute-start | bytes 1118216 | tf_op jit(solution)/shard_map/ppermute | solution.py:470
  27.2 16.6 %collective-permute-start.4 = (f32[91,8,128]{2,1,0:T(8,128)S(1)}, f32[91,8,128]{2,1,0:T(8,128)S(1)}, u32[]{:S(2)}, u32[]{:S(2)}) collective-permute-start(f32[91,8,128]{2,1,0:T(8,128)S(1)} %pad_maximum_fusion.y_mid), channel_id=1, source_target_pairs={{0,4},{4,8},{8,12},{12,16},{16,20},{20,24},{24,28},{28,32},{32,36}... | collective-permute-start | bytes 1118216 | tf_op jit(solution)/shard_map/ppermute | solution.py:470
  27.2 9.2 %collective-permute-start.6 = (f32[3,8,128]{2,1,0:T(8,128)S(1)}, f32[3,8,128]{2,1,0:T(8,128)S(1)}, u32[]{:S(2)}, u32[]{:S(2)}) collective-permute-start(f32[3,8,128]{2,1,0:T(8,128)S(1)} %get-tuple-element.14), channel_id=1, source_target_pairs={{0,128},{64,192},{128,256},{192,320},{256,384},{320,448},{1,129},{... | collective-permute-start | bytes 36872 | tf_op jit(solution)/shard_map/ppermute | solution.py:470
  30.3 12.8 %collective-permute-start.7 = (f32[3,8,128]{2,1,0:T(8,128)S(1)}, f32[3,8,128]{2,1,0:T(8,128)S(1)}, u32[]{:S(2)}, u32[]{:S(2)}) collective-permute-start(f32[3,8,128]{2,1,0:T(8,128)S(1)} %get-tuple-element.15), channel_id=1, source_target_pairs={{128,0},{192,64},{256,128},{320,192},{384,256},{448,320},{129,1},{... | collective-permute-start | bytes 36872 | tf_op jit(solution)/shard_map/ppermute | solution.py:470
  31.6 11.5 %collective-permute-start.8 = (f32[3,8,128]{2,1,0:T(8,128)S(1)}, f32[3,8,128]{2,1,0:T(8,128)S(1)}, u32[]{:S(2)}, u32[]{:S(2)}) collective-permute-start(f32[3,8,128]{2,1,0:T(8,128)S(1)} %get-tuple-element.16), channel_id=1, source_target_pairs={{0,8},{4,12},{8,16},{12,20},{16,24},{20,28},{24,32},{28,36},{32,40... | collective-permute-start | bytes 36872 | tf_op jit(solution)/shard_map/ppermute | solution.py:470
  36.4 7.4 %collective-permute-start.9 = (f32[3,8,128]{2,1,0:T(8,128)S(1)}, f32[3,8,128]{2,1,0:T(8,128)S(1)}, u32[]{:S(2)}, u32[]{:S(2)}) collective-permute-start(f32[3,8,128]{2,1,0:T(8,128)S(1)} %get-tuple-element.17), channel_id=1, source_target_pairs={{0,56},{4,60},{8,0},{12,4},{16,8},{20,12},{24,16},{28,20},{32,24},... | collective-permute-start | bytes 36872 | tf_op jit(solution)/shard_map/ppermute | solution.py:470

commit v2 on v0

v2 whole, which is shorter than its diff:
```python
import functools

import jax
import jax.numpy as jnp
from jax import lax
from jax.experimental import pallas as pl
from jax.experimental.pallas import tpu as pltpu
from jax.sharding import PartitionSpec as P

f32 = jnp.float32
i32 = jnp.int32
bf16 = jnp.bfloat16
NSUB = 64
B = 8
LZ = 128
NP = 3 * B
W = 9
FULL = (NP, 2 * LZ)
CHUNK = 8
fine_relax = 0.6666667
coarse_relax = 0.7
VMEM_LIMIT = 48 * 1024 * 1024

PERM, OWN, HZ, ASG, SRC = 0, 8, 16, 24, 25
STACK = 33
HEAD = 25
LINE = 3 * HEAD + 2 * B


def lanes(shape):
    return lax.broadcasted_iota(i32, shape, len(shape) - 1)


def rows(shape):
    return lax.broadcasted_iota(i32, shape, len(shape) - 2)


def sds(*shape, dtype=f32):
    return jax.ShapeDtypeStruct(shape, dtype)


def call(kernel, outs, n_in, scratch=(), space=pltpu.VMEM):
    single = not isinstance(outs, (list, tuple))
    vm = pl.BlockSpec(memory_space=pltpu.VMEM)
    return pl.pallas_call(
        kernel,
        out_shape=outs,
        in_specs=[pl.BlockSpec(memory_space=space)] * n_in,
        out_specs=vm if single else [vm] * len(outs),
        scratch_shapes=list(scratch),
        compiler_params=pltpu.CompilerParams(vmem_limit_bytes=VMEM_LIMIT),
    )


def spread(row):
    return jnp.broadcast_to(row, (B, LZ))


def z_messages(perm_in, src_in, own_in, asg_in, flags_in, mr, ml, base, flags_out,
               perm, src, own, asg, flags, sem):
    copies = [
        pltpu.make_async_copy(a, b, sem.at[i])
        for i, (a, b) in enumerate(
            ((perm_in, perm), (src_in, src), (own_in, own), (asg_in, asg), (flags_in, flags))
        )
    ]
    for copy in copies:
        copy.start()
    for copy in copies:
        copy.wait()
    lane = lanes((B, LZ))
    tile = jnp.concatenate([asg[...].astype(f32), jnp.zeros((1, LZ - NSUB), f32)], axis=1)
    tile = jnp.where(rows((B, LZ)) == 0, spread(tile), 0.0)
    for p in range(B):
        k, s, o = perm[p], src[p], own[p].astype(f32)
        base[p], base[B + p], base[2 * B + p] = k, o, s
        mr[p] = jnp.where(
            lane < 16, k, jnp.where(lane < 32, pltpu.roll(o, 16, 1), pltpu.roll(s, 32, 1))
        )
        ml[p] = jnp.where(
            lane >= 112, k, jnp.where(lane >= 96, pltpu.roll(o, 112, 1), pltpu.roll(s, 96, 1))
        )
    base[3 * B] = tile
    mr[B] = tile
    ml[B] = tile
    col, n_col = lax.axis_index("col"), flags_in.shape[0]
    for i, at in enumerate((col - 1, col, col + 1)):
        at = jnp.clip(at, 0, n_col - 1)
        flags_out[pl.ds(i, 1), :] = flags[pl.ds(at, 1), :].astype(f32)


def stack_up(base, mr, ml, stack):
    lane = lanes((B, LZ))
    row = rows((B, LZ))
    for p in range(B):
        stack[PERM + p] = base[p]
        stack[OWN + p] = base[B + p]
        stack[SRC + p] = base[2 * B + p]
        stack[HZ + p] = jnp.where(lane < 64, mr[p], ml[p])
    stack[ASG] = jnp.where(
        row == 1, spread(mr[B, 0:1, :]), jnp.where(row == 2, spread(ml[B, 0:1, :]), base[3 * B])
    )


def around(u_ref, w_ref, p):
    u = u_ref[p + 1]
    return u, (
        (w_ref[0, p] * u_ref[p + 2] + w_ref[1, p] * u_ref[p])
        + (w_ref[2, p] * pltpu.roll(u, NP - 1, 0) + w_ref[3, p] * pltpu.roll(u, 1, 0))
        + (w_ref[4, p] * pltpu.roll(u, 2 * LZ - 1, 1) + w_ref[5, p] * pltpu.roll(u, 1, 1))
    )


def sweeps(both, w_ref, first, last, after=None, operator_at=-1):
    def one_sweep(k, carry):
        now = lax.rem(k, 2)
        src, dst = both.at[now], both.at[1 - now]
        count = NP - 2 * k
        keep = jnp.where(k == operator_at, 1.0, 1.0 - fine_relax)
        give = jnp.where(k == operator_at, -1.0 / fine_relax, 1.0)

        def chunk(i, carry):
            start = jnp.minimum(k + CHUNK * i, k + count - CHUNK)
            moved = []
            for j in range(CHUNK):
                u, near = around(src, w_ref, start + j)
                moved.append(keep * u + give * near)
            for j in range(CHUNK):
                dst[start + j + 1] = moved[j]
            return carry

        lax.fori_loop(0, (count + CHUNK - 1) // CHUNK, chunk, 0)
        if after is not None:
            after(k)
        return carry

    lax.fori_loop(first, last + 1, one_sweep, 0)


def label_sums(groups, sums):
    def one(s, carry):
        for first, labels, fields in groups:
            hits = [tile == s for tile in labels]
            for i, tiles in enumerate(fields):
                parts = [jnp.where(hit, tile, 0.0) for hit, tile in zip(hits, tiles)]
                while len(parts) > 1:
                    parts = [a + b for a, b in zip(parts[::2], parts[1::2])]
                sums[pl.ds(first + i * NSUB + s, 1), :] = jnp.sum(parts[0], axis=0, keepdims=True)
        return carry

    lax.fori_loop(0, NSUB, one, 0, unroll=4)


def lane_sums(sums):
    return lax.dot_general(
        jnp.ones((B, LZ), f32), sums, (((1,), (1,)), ((), ())),
        precision=lax.Precision.HIGHEST, preferred_element_type=f32,
    )


def harmonic(a, b):
    return 2.0 * a * b / (a + b)


def row_product(tile):
    for by in (4, 2, 1):
        tile = tile * pltpu.roll(tile, by, 0)
    return tile


def first_sums(n_gx, n_gy, n_col, y_lo, y_mid, y_hi, flags,
               weights, labels, chunk, dvals, paths, kext, fx, both, masks, sums):
    gx, gy, col = (lax.axis_index(a) for a in ("gx", "gy", "col"))
    lines = (y_lo, y_mid, y_hi)
    lane = lanes((B, LZ))
    row = rows((B, LZ))
    halo = (lane < W) | (lane >= LZ - W)
    near_side = lane < 64

    def positive(t):
        return jnp.where(t > 0.0, t, 1.0)

    def fill(p, carry):
        at = HEAD * (p // B) + lax.rem(p, B)
        for ty in range(3):
            line = lines[ty]
            r = slice(ty * B, (ty + 1) * B)
            packed = line[at + HZ]
            kext[p + 1, r, 0:LZ] = positive(line[at + PERM])
            kext[p + 1, r, LZ:] = positive(jnp.where(halo, packed, 1.0))
            labels[p, r, 0:LZ] = line[at + OWN].astype(i32)
            own_z = jnp.where(near_side, pltpu.roll(packed, LZ - 16, 1), pltpu.roll(packed, 16, 1))
            labels[p, r, LZ:] = jnp.where(halo, own_z, 0.0).astype(i32)
        return carry

    lax.fori_loop(0, NP, fill, 0, unroll=4)
    kext[0] = jnp.ones(FULL, f32)
    kext[NP + 1] = jnp.ones(FULL, f32)

    flag_row = jnp.concatenate(
        [flags[1:2, :], jnp.where(lane[0:1] < 64, flags[2:3, :], flags[0:1, :])], axis=1
    )
    row_all, lane_all = rows(FULL), lanes(FULL)
    wrap_row = jnp.where(gy == 0, B - 1, jnp.where(gy == n_gy - 1, 2 * B - 1, -1))
    masks[0] = jnp.where(row_all == wrap_row, jnp.broadcast_to(flag_row, FULL), 1.0)
    closed = ((lane_all == LZ - 1) & (col == n_col - 1)) | ((lane_all == 2 * LZ - 1) & (col == 0))
    masks[1] = jnp.where(closed, 0.0, 1.0)

    def x_face(p, carry):
        fx[p] = harmonic(kext[p], kext[p + 1])
        return carry

    lax.fori_loop(0, NP + 1, x_face, 0, unroll=5)

    @pl.when(gx == 0)
    def _():
        fx[B] = kext[B + 1]

    @pl.when(gx == n_gx - 1)
    def _():
        fx[2 * B] = kext[2 * B]

    def terms(p, carry):
        b = p // B
        out = ((b == 0) & (gx == 0)) | ((b == 2) & (gx == n_gx - 1))
        k = kext[p + 1]
        fy_up = harmonic(k, pltpu.roll(k, NP - 1, 0)) * masks[0]
        fy_down = pltpu.roll(fy_up, 1, 0)
        fz_right = harmonic(k, pltpu.roll(k, 2 * LZ - 1, 1)) * masks[1]
        fz_left = pltpu.roll(fz_right, 1, 1)
        fx_up, fx_down = fx[p + 1], fx[p]
        diag = fx_up + fx_down + fy_up + fy_down + fz_right + fz_left
        inverse = 1.0 / diag
        scale = jnp.where(out, 0.0, fine_relax) * inverse
        for i, face in enumerate((fx_up, fx_down, fy_up, fy_down, fz_right, fz_left)):
            weights[i, p] = face * scale
        at = 3 * HEAD + jnp.clip(p - 4, 0, 2 * B - 1)
        hz = HEAD * b + HZ + lax.rem(p, B)
        for ty in range(3):
            line = lines[ty]
            r = slice(ty * B, (ty + 1) * B)
            packed = line[hz]
            src_z = jnp.where(near_side, pltpu.roll(packed, LZ - 32, 1), pltpu.roll(packed, 32, 1))
            both[1, p + 1, r, 0:LZ] = line[at] * inverse[r, 0:LZ]
            both[1, p + 1, r, LZ:] = jnp.where(halo, src_z, 0.0) * inverse[r, LZ:]

        @pl.when(b == 1)
        def _():
            q = p - B
            r = slice(B, 2 * B)
            dvals[q] = diag[r, 0:LZ]
            up, down = (face[r, 0:LZ] for face in (fy_up, fy_down))
            s = scale[r, 0:LZ]
            rise = row_product(jnp.where(row == 0, 1.0, down * s))
            fall = row_product(jnp.where(row == B - 1, 1.0, up * s))
            paths[2, pl.ds(q, 1), :] = rise[0:1] * up[B - 1 : B]
            paths[3, pl.ds(q, 1), :] = fall[0:1] * down[0:1]

        return carry

    lax.fori_loop(0, NP, terms, 0, unroll=2)
    rise, fall = fx[2 * B, B : 2 * B, 0:LZ], fx[B, B : 2 * B, 0:LZ]
    for p in range(B + 1, 2 * B):
        rise = rise * weights[1, p, B : 2 * B, 0:LZ]
        fall = fall * weights[0, p - 1, B : 2 * B, 0:LZ]
    paths[0] = rise
    paths[1] = fall

    sweeps(both, weights, 5, 8)
    tiles = [both[1, B + 1 + q, B : 2 * B, 0:LZ] * dvals[q] for q in range(B)]
    diag_tiles = [dvals[q] for q in range(B)]
    label_tiles = [labels[B + q, B : 2 * B, 0:LZ] for q in range(B)]
    label_sums([(0, label_tiles, (tiles, diag_tiles))], sums)
    totals = lane_sums(sums[...])

    def twice(low, high):
        return jnp.where(lane < NSUB, low, pltpu.roll(high, NSUB, 1))

    own, left, right = (spread(y_mid[HEAD * b + ASG, 0:1, :]) for b in (1, 0, 2))
    tile = jnp.where(
        row == 0, totals, jnp.where(row == 1, twice(own, own), twice(right, left))
    )
    for d in range(n_gy):
        chunk[d] = tile


def one_hot_product(lefts, lows, out, n_out):
    left = jnp.concatenate(lefts, axis=1)
    l1 = left.astype(bf16)
    rest = left - l1.astype(f32)
    l2 = rest.astype(bf16)
    l3 = (rest - l2.astype(f32)).astype(bf16)
    wide = rows((LZ, LZ))
    right = jnp.concatenate(
        [
            jnp.where(jnp.broadcast_to(low, (LZ, LZ)) == wide, 1.0, 0.0).astype(bf16)
            for low in lows
        ],
        axis=1,
    )
    total = sum(
        lax.dot_general(part, right, (((1,), (1,)), ((), ())), preferred_element_type=f32)
        for part in (l3, l2, l1)
    )
    for d in range(n_out):
        out[d] = total


def halves(value, high):
    lane = lanes((B, LZ))
    scaled = jnp.where(high == rows((B, LZ)), value, 0.0)
    return jnp.where(lane < NSUB, scaled, 0.0), jnp.where(lane < NSUB, 0.0, scaled)


def first_partial(n_gy, n_out, values, out):
    lefts, lows = [], []
    for g in range(n_gy):
        a = values[g, 1:2, :].astype(i32)
        lefts.append(jnp.concatenate(halves(spread(values[g, 0:1, :]), spread(a >> 7)), axis=0))
        lows.append(a & 127)
    one_hot_product(lefts, lows, out, n_out)


def second_partial(n_gy, n_out, values, first, out):
    lane = lanes((B, LZ))
    lefts, lows = [], []
    for g in range(n_gy):
        before, after = (g - 1) % n_gy, (g + 1) % n_gy
        own = spread(values[g, 0:1, :] + values[before, 2:3, :])
        own = own + pltpu.roll(spread(values[after, 2:3, :]), NSUB, 1)
        a = first[g, 1:2, :].astype(i32)
        mine, _ = halves(own, spread(a >> 7))
        lows.append(a & 127)
        a = first[g, 2:3, :].astype(i32)
        above, below = halves(spread(values[g, 1:2, :]), spread(a >> 7))
        lows.append(a & 127)
        zero = jnp.zeros((B, LZ), f32)
        lefts.append(jnp.concatenate([mine, zero, zero], axis=0))
        lefts.append(jnp.concatenate([zero, above, below], axis=0))
    one_hot_product(lefts, lows, out, n_out)


def lookup(table, index):
    low, high = index & 127, index >> 7
    result = jnp.zeros((B, LZ), f32)
    for h in range(B):
        got = jnp.take_along_axis(spread(table[h : h + 1]), low, axis=1)
        result = jnp.where(high == h, got, result)
    return result


def pick(row, index):
    return jnp.take_along_axis(spread(row), index, axis=1)


def slab_total(parts, g, n_gx, n_col, part, size):
    at = jnp.clip(g, 0, n_gx - 1) * n_col
    total = parts[at, part : part + size]
    for c in range(1, n_col):
        total = total + parts[at + c, part : part + size]
    return jnp.where((g >= 0) & (g < n_gx), total, 0.0)


def guess(parts, g, n_gx, n_col):
    total = slab_total(parts, g, n_gx, n_col, 0, 2 * B)
    exists = (g >= 0) & (g < n_gx)
    rhs, diag = total[0:B], jnp.where(exists, total[B : 2 * B], 1.0)
    return rhs, diag, coarse_relax * rhs / diag


def expand(coarse, lines, labels, u, tables, first, last):
    near_side = lanes((B, LZ)) < 64

    def table(b, carry):
        for ty in range(3):
            tables[b, ty] = lookup(coarse[b], lines[ty][HEAD * b + ASG].astype(i32))
        return carry

    lax.fori_loop(0, 3, table, 0)

    def one(p, carry):
        b = p // B
        for ty in range(3):
            r = slice(ty * B, (ty + 1) * B)
            t = tables[b, ty]
            u[p + 1, r, 0:LZ] = pick(t[0:1], labels[p, r, 0:LZ])
            lab = labels[p, r, LZ:]
            u[p + 1, r, LZ:] = jnp.where(near_side, pick(t[1:2], lab), pick(t[2:3], lab))
        return carry

    lax.fori_loop(first, last + 1, one, 0, unroll=4)


def second_sums(n_gx, n_gy, n_col, parts, weights, labels, y_lo, y_mid, y_hi, dvals, paths,
                chunk, both, coarse, tables, ends, sums):
    gx = lax.axis_index("gx")
    row = rows((B, LZ))
    r = slice(B, 2 * B)
    for i in range(3):
        coarse[i] = guess(parts, gx + i - 1, n_gx, n_col)[2]
    expand(coarse, (y_lo, y_mid, y_hi), labels, both.at[0], tables, 0, NP - 1)

    def after(k):
        @pl.when(k == 0)
        def _():
            first = both.at[1]
            zero = jnp.zeros(FULL, f32)
            first[1] = zero
            first[NP] = zero
            first[:, 0:1, :] = jnp.zeros((NP + 2, 1, 2 * LZ), f32)
            first[:, NP - 1 :, :] = jnp.zeros((NP + 2, 1, 2 * LZ), f32)
            ends[0] = first[B + 1, r, 0:LZ] * -paths[0]
            ends[1] = first[2 * B, r, 0:LZ] * -paths[1]
            for q in range(B):
                plane = first[B + 1 + q, r, 0:LZ]
                ends[2, q : q + 1, :] = plane[0:1] * -paths[2, q : q + 1, :]
                ends[3, q : q + 1, :] = plane[B - 1 : B] * -paths[3, q : q + 1, :]

    sweeps(both, weights, 0, 8, after=after, operator_at=4)
    tiles = [both[1, B + 1 + q, r, 0:LZ] * dvals[q] for q in range(B)]
    label_tiles = [labels[B + q, r, 0:LZ] for q in range(B)]
    beyond = [labels[2 * B, r, 0:LZ], labels[B - 1, r, 0:LZ]]
    for at in (2 * B, B - 1):
        edge = labels[B, at : at + 1, 0:LZ]
        edge = spread(edge)
        for q in range(1, B):
            edge = jnp.where(row == q, spread(labels[B + q, at : at + 1, 0:LZ]), edge)
        beyond.append(edge)
    groups = [(0, label_tiles, (tiles,))]
    groups += [((2 + i) * NSUB, [beyond[i]], ([ends[i]],)) for i in range(4)]
    sums[NSUB : 2 * NSUB, :] = jnp.zeros((NSUB, LZ), f32)
    label_sums(groups, sums)
    totals = lane_sums(sums[...])
    tile = jnp.where(
        row == 0,
        totals[:, 0:LZ],
        jnp.where(row == 1, totals[:, LZ : 2 * LZ], totals[:, 2 * LZ :]),
    )
    for d in range(n_gy):
        chunk[d] = tile


def last_sweeps(n_gx, n_gy, n_col, parts, images, weights, labels, y_lo, y_mid, y_hi,
                pressure, coarse_out, both, coarse, tables):
    gx, gy, col = (lax.axis_index(a) for a in ("gx", "gy", "col"))
    for i in range(3):
        g = gx + i - 1
        rhs, diag, start = guess(parts, g, n_gx, n_col)
        image = (
            slab_total(images, g, n_gx, n_col, 0, B)
            + slab_total(images, g - 1, n_gx, n_col, B, B)
            + slab_total(images, g + 1, n_gx, n_col, 2 * B, B)
        )
        second = start + coarse_relax * (rhs - image) / diag
        coarse[i] = jnp.where((g >= 0) & (g < n_gx), second, 0.0)
    share = B * LZ // (n_gy * n_col)
    per_row = LZ // share
    mine = gy * n_col + col
    row = coarse[1, pl.ds(mine // per_row, 1), :]
    turned = pltpu.roll(spread(row), lax.rem(LZ - lax.rem(mine, per_row) * share, LZ), 1)
    coarse_out[...] = turned[0:1, 0:share]
    expand(coarse, (y_lo, y_mid, y_hi), labels, both.at[1], tables, 4, 19)
    sweeps(both, weights, 5, 8)
    for q in range(B):
        pressure[q] = both[1, B + 1 + q, B : 2 * B, 0:LZ]


def steps(count, by, wrap):
    return [
        (i, (i + by) % count) for i in range(count) if wrap or 0 <= i + by < count
    ]


def on_device(n_gx, n_gy, n_col, permeability, source, ownership, assignment, layer_flags):
    n_out = n_gx * n_col
    sizes = (n_gx, n_gy, n_col)
    vm = pltpu.VMEM
    fields = vm((2, NP + 2, *FULL), f32)
    plane = (B, B, LZ)

    def send(x, axis, by, wrap=False):
        return lax.ppermute(x, axis, steps(lax.axis_size(axis), by, wrap))

    mr, ml, base, flags = call(
        z_messages,
        [sds(B + 1, B, LZ)] * 2 + [sds(3 * B + 1, B, LZ), sds(3, LZ)],
        5,
        scratch=[
            vm(plane, f32), vm(plane, f32), vm(plane, i32), vm((1, NSUB), i32),
            vm((n_col, LZ), i32), pltpu.SemaphoreType.DMA((5,)),
        ],
        space=pl.ANY,
    )(permeability, source, ownership, assignment.reshape(1, NSUB), layer_flags.reshape(n_col, LZ))
    mr, ml = send(mr, "col", -1), send(ml, "col", 1)
    stack = call(stack_up, sds(STACK, B, LZ), 3)(base, mr, ml)
    low, high = send(stack, "gx", 1), send(stack, "gx", -1)
    line = jnp.concatenate(
        [low[:HEAD], stack[:HEAD], high[:HEAD], low[SRC + 4 :], stack[SRC:], high[SRC : SRC + 4]],
        axis=0,
    )
    y_lo, y_hi = send(line, "gy", 1, True), send(line, "gy", -1, True)

    weights, labels, chunk, dvals, paths = call(
        functools.partial(first_sums, *sizes),
        [
            sds(6, NP, *FULL), sds(NP, *FULL, dtype=i32), sds(n_gy, B, LZ), sds(*plane),
            sds(4, B, LZ),
        ],
        4,
        scratch=[
            vm((NP + 2, *FULL), f32), vm((NP + 1, *FULL), f32), fields, vm((2, *FULL), f32),
            vm((2 * NSUB, LZ), f32),
        ],
    )(y_lo, line, y_hi, flags)
    bricks = lax.all_to_all(chunk, "gy", 0, 0, tiled=True)
    parts = call(
        functools.partial(first_partial, n_gy, n_out), sds(n_out, 2 * B, LZ), 1
    )(bricks)
    parts = lax.all_to_all(parts, ("gx", "col"), 0, 0, tiled=True)
    tables = [vm((3, B, LZ), f32), vm((3, 3, B, LZ), f32)]
    chunk = call(
        functools.partial(second_sums, *sizes),
        sds(n_gy, B, LZ),
        8,
        scratch=[fields, *tables, vm((4, B, LZ), f32), vm((6 * NSUB, LZ), f32)],
    )(parts, weights, labels, y_lo, line, y_hi, dvals, paths)
    images = lax.all_to_all(chunk, "gy", 0, 0, tiled=True)
    images = call(
        functools.partial(second_partial, n_gy, n_out), sds(n_out, 3 * B, LZ), 2
    )(images, bricks)
    images = lax.all_to_all(images, ("gx", "col"), 0, 0, tiled=True)
    return call(
        functools.partial(last_sweeps, *sizes),
        [sds(*plane), sds(1, B * LZ // (n_gy * n_col))],
        7,
        scratch=[fields, *tables],
    )(parts, images, weights, labels, y_lo, line, y_hi)


def solution(mesh):
    placed = (
        P("gx", "gy", "col"),
        P("gx", "gy", "col"),
        P("gx", "gy", "col"),
        P("gx", "gy", "col", None),
        P(),
    )
    sizes = mesh.shape
    return jax.shard_map(
        functools.partial(on_device, sizes["gx"], sizes["gy"], sizes["col"]),
        mesh=mesh,
        in_specs=placed,
        out_specs=(P("gx", "gy", "col"), P("gx", ("gy", "col"))),
        check_vma=False,
    )
```

time: 876 us -> 125 us (0.14)
  starting transfers between devices: 377 us -> 17.9 us
  blocking collectives: 288 us -> 73 us
  local copies, waits for them, and re-layouts: 103 us -> 3.64 us
  waiting for transfers between devices: 80.5 us -> 9.97 us
  Pallas kernels: 0 us -> 19 us
  other arithmetic: 10.7 us -> 0 us
    ppermute x108 -> x6, starting transfers between devices: 377 us -> 17.9 us  [send(): return lax.ppermute(x, axis, steps(lax.axis_size(axis), by, wrap))]
    psum x2 -> x0, blocking collectives: 288 us -> none  [slab_sums(): return lax.psum(pair, ('gy', 'col'))]
    gather x2 -> x0, local copies, waits for them, and re-layouts: 97.8 us -> none  [expand(): return jnp.take(per_subdomain, ownership)]
    all_to_all x0 -> x4, blocking collectives: none -> 73 us  [the longest x1 24.6 us: on_device(): parts = lax.all_to_all(parts, ('gx', 'col'), 0, 0, tiled=True)]
    ppermute x108 -> x6, waiting for transfers between devices: 80.5 us -> 9.97 us  [send(): return lax.ppermute(x, axis, steps(lax.axis_size(axis), by, wrap))]
    pallas_call x0 -> x7, Pallas kernels: none -> 19 us  [the longest x1 7.16 us: on_device(): call(functools.partial(first_sums, *sizes), [sds(6, NP, *FULL), sds(NP, *...]
  transfers between devices with their start and end apart: 108 -> 6, of which waited for: 73 -> 5; matrix products, arithmetic and copies ran while one was open for 0% -> 0% of each run, Pallas kernels for 0% -> 0%
where the time goes in v2:
time: 125 us; the launch traced here: 124 us
  blocking collectives  73 us (58%)
  Pallas kernels  19 us (15%)
  starting transfers between devices  17.9 us (14%)
  waiting for transfers between devices  9.97 us (8%)
  local copies, waits for them, and re-layouts  3.64 us (3%)
    all_to_all x1, blocking collectives, on_device(): parts = lax.all_to_all(parts, ('gx', 'col'), 0, 0, tiled=True)  24.6 us
    all_to_all x1, blocking collectives, on_device(): bricks = lax.all_to_all(chunk, 'gy', 0, 0, tiled=True)  18.4 us
    ppermute x6, starting transfers between devices, send(): return lax.ppermute(x, axis, steps(lax.axis_size(axis), by, wrap))  17.9 us
    all_to_all x1, blocking collectives, on_device(): images = lax.all_to_all(images, ('gx', 'col'), 0, 0, tiled=True)  17.4 us
    all_to_all x1, blocking collectives, on_device(): images = lax.all_to_all(chunk, 'gy', 0, 0, tiled=True)  12.6 us
    ppermute x6, waiting for transfers between devices, send(): return lax.ppermute(x, axis, steps(lax.axis_size(axis), by, wrap))  9.97 us
    pallas_call x1, Pallas kernels, on_device(): call(functools.partial(first_sums, *sizes), [sds(6, NP, *FULL), sds(NP, *...  7.16 us
    pallas_call x1, Pallas kernels, on_device(): call(functools.partial(second_sums, *sizes), sds(n_gy, B, LZ), 8, scratch...  6.69 us
  transfers between devices with their start and end apart: 6, of which 5 were waited for; matrix products, arithmetic and copies ran while one was open for 0% of the time, Pallas kernels for 0%

profile of v2, /device:TPU:1, one launch (start us, length us, event | category | flops | bytes accessed | tf_op | source)
XLA Modules:
  0.0 124.4 jit_solution(12831474792015815089)
XLA Ops:
  0.6 0.0 copy-start
  0.6 0.7 copy-done
  1.4 0.0 copy-start.1
  1.4 0.8 copy-done.1
  2.1 0.0 copy-start.2
  2.2 0.8 copy-done.2
  2.9 0.0 copy-start.3
  2.9 0.7 copy-done.3
  3.6 0.0 copy-start.4
  3.6 0.7 copy-done.4
  4.2 0.2 shard_map.68
  4.5 1.3 %collective-permute-start = (f32[9,8,128]{2,1,0:T(8,128)S(1)}, f32[9,8,128]{2,1,0:T(8,128)S(1)}, u32[]{:S(2)}, u32[]{:S(2)}) collective-permute-start(f32[9,8,128]{2,1,0:T(8,128)S(1)} %get-tuple-element.12), channel_id=1, source_target_pairs={{1,0},{2,1},{3,2},{5,4},{6,5},{7,6},{9,8},{10,9},{11,10},{13,12},{... | collective-permute-start | bytes 110600 | tf_op jit(solution)/shard_map/ppermute | solution.py:482
  5.8 5.7 %collective-permute-start.1 = (f32[9,8,128]{2,1,0:T(8,128)S(1)}, f32[9,8,128]{2,1,0:T(8,128)S(1)}, u32[]{:S(2)}, u32[]{:S(2)}) collective-permute-start(f32[9,8,128]{2,1,0:T(8,128)S(1)} %get-tuple-element.13), channel_id=1, source_target_pairs={{0,1},{1,2},{2,3},{4,5},{5,6},{6,7},{8,9},{9,10},{10,11},{12,13},{... | collective-permute-start | bytes 110600 | tf_op jit(solution)/shard_map/ppermute | solution.py:482
  11.5 0.0 collective-permute-done.mr
  11.5 1.0 collective-permute-done.1.ml
  12.5 3.2 %collective-permute-start.2 = (f32[33,8,128]{2,1,0:T(8,128)S(1)}, f32[33,8,128]{2,1,0:T(8,128)S(1)}, u32[]{:S(2)}, u32[]{:S(2)}) collective-permute-start(f32[33,8,128]{2,1,0:T(8,128)S(1)} %shard_map.69), channel_id=1, source_target_pairs={{0,64},{64,128},{128,192},{192,256},{256,320},{320,384},{384,448},... | collective-permute-start | bytes 405512 | tf_op jit(solution)/shard_map/ppermute | solution.py:482
  15.7 1.3 %collective-permute-start.3 = (f32[33,8,128]{2,1,0:T(8,128)S(1)}, f32[33,8,128]{2,1,0:T(8,128)S(1)}, u32[]{:S(2)}, u32[]{:S(2)}) collective-permute-start(f32[33,8,128]{2,1,0:T(8,128)S(1)} %shard_map.69), channel_id=1, source_target_pairs={{64,0},{128,64},{192,128},{256,192},{320,256},{384,320},{448,384},... | collective-permute-start | bytes 405512 | tf_op jit(solution)/shard_map/ppermute | solution.py:482
  17.0 0.7 collective-permute-done.2
  17.7 3.8 %collective-permute-done.3 = f32[33,8,128]{2,1,0:T(8,128)S(1)} collective-permute-done((f32[33,8,128]{2,1,0:T(8,128)S(1)}, f32[33,8,128]{2,1,0:T(8,128)S(1)}, u32[]{:S(2)}, u32[]{:S(2)}) %collective-permute-start.3) | collective-permute-done | bytes 135200 | tf_op jit(solution)/shard_map/ppermute | solution.py:482
  21.5 6.5 %collective-permute-start.5 = (f32[91,8,128]{2,1,0:T(8,128)S(1)}, f32[91,8,128]{2,1,0:T(8,128)S(1)}, u32[]{:S(2)}, u32[]{:S(2)}) collective-permute-start(f32[91,8,128]{2,1,0:T(8,128)S(1)} %slice_dynamic-update-slice_fusion.4.y_mid), channel_id=1, source_target_pairs={{0,60},{4,0},{8,4},{12,8},{16,12},{20,16},{24,20},{28,24},{32,28},... | collective-permute-start | bytes 1118216 | tf_op jit(solution)/shard_map/ppermute | solution.py:482
  28.0 0.0 collective-permute-start.4
  28.0 3.9 %collective-permute-done.5.y_hi = f32[91,8,128]{2,1,0:T(8,128)S(1)} collective-permute-done((f32[91,8,128]{2,1,0:T(8,128)S(1)}, f32[91,8,128]{2,1,0:T(8,128)S(1)}, u32[]{:S(2)}, u32[]{:S(2)}) %collective-permute-start.5) | collective-permute-done | bytes 372768 | tf_op jit(solution)/shard_map/ppermute | solution.py:482
  32.0 0.6 collective-permute-done.4.y_lo
  32.5 7.2 %shard_map.70 = (f32[6,24,24,256]{3,2,1,0:T(8,128)S(1)}, s32[24,24,256]{2,1,0:T(8,128)S(1)}, f32[16,8,128]{2,1,0:T(8,128)S(1)}, f32[8,8,128]{2,1,0:T(8,128)S(1)}, f32[4,8,128]{2,1,0:T(8,128)S(1)}) custom-call(f32[91,8,128]{2,1,0:T(8,128)S(1)} %collective-permute-done.4.y_lo, f32[91,8,128]{2,1,0:T(8,128)S(1)} %slice_dynamic-update-slice_fusion.4.y_mid, ...), custom_call_target="tpu_custom_call" | custom-call | tf_op jit(solution)/shard_map/pallas_call | solution.py:503
  39.7 18.4 %all_to_all.20.values.first = f32[16,8,128]{2,1,0:T(8,128)S(1)} all-to-all(f32[16,8,128]{2,1,0:T(8,128)S(1)} %get-tuple-element.15), channel_id=1, replica_groups=mesh['gx'=8,'gy'=16,'col'=4] {'gy'}, dimensions={0} | all-to-all | bytes 131072 | tf_op jit(solution)/shard_map/all_to_all | solution.py:515
  58.1 0.5 shard_map.71
  58.6 24.6 %all_to_all.21.parts = f32[32,16,128]{2,1,0:T(8,128)S(1)} all-to-all(f32[32,16,128]{2,1,0:T(8,128)S(1)} %shard_map.71), channel_id=1, replica_groups=mesh['gx'=8,'gy'=16,'col'=4] {'gx','col'}, dimensions={0} | all-to-all | bytes 524288 | tf_op jit(solution)/shard_map/all_to_all | solution.py:519
  83.2 6.7 %shard_map.72 = f32[16,8,128]{2,1,0:T(8,128)S(1)} custom-call(f32[32,16,128]{2,1,0:T(8,128)S(1)} %all_to_all.21.parts, f32[6,24,24,256]{3,2,1,0:T(8,128)S(1)} %get-tuple-element.16.weights, s32[24,24,256]{2,1,0:T(8,128)S(1)} %get-tuple-element.17.labels, f32[91,8,128]{2,1,0:T(8,128)S(1)} %collective-permute-done.4.y_lo, ...), custom_call_target="tpu_custom_call" | custom-call | tf_op jit(solution)/shard_map/pallas_call | solution.py:521
  89.9 12.6 %all_to_all.22.values = f32[16,8,128]{2,1,0:T(8,128)S(1)} all-to-all(f32[16,8,128]{2,1,0:T(8,128)S(1)} %shard_map.72), channel_id=1, replica_groups=mesh['gx'=8,'gy'=16,'col'=4] {'gy'}, dimensions={0} | all-to-all | bytes 131072 | tf_op jit(solution)/shard_map/all_to_all | solution.py:527
  102.6 1.2 shard_map.73
  103.8 17.4 %all_to_all.23.images = f32[32,24,128]{2,1,0:T(8,128)S(1)} all-to-all(f32[32,24,128]{2,1,0:T(8,128)S(1)} %shard_map.73), channel_id=1, replica_groups=mesh['gx'=8,'gy'=16,'col'=4] {'gx','col'}, dimensions={0} | all-to-all | bytes 786432 | tf_op jit(solution)/shard_map/all_to_all | solution.py:531
  121.2 3.2 %shard_map.74 = (f32[8,8,128]{2,1,0:T(8,128)}, f32[1,16]{1,0:T(1,128)}) custom-call(f32[32,16,128]{2,1,0:T(8,128)S(1)} %all_to_all.21.parts, f32[32,24,128]{2,1,0:T(8,128)S(1)} %all_to_all.23.images, f32[6,24,24,256]{3,2,1,0:T(8,128)S(1)} %get-tuple-element.16.weights, s32[24,24,256]{2,1,0:T(8,128)S(1)} %get-tuple-element.17.labels, ...), custom_call_target="tpu_custom_call" | custom-call | tf_op jit(solution)/shard_map/pallas_call | solution.py:532
  (7 shorter events, 0.1 us)
Async XLA Ops:
  0.6 0.8 copy-start
  1.4 0.8 copy-start.1
  2.1 0.8 copy-start.2
  2.9 0.7 copy-start.3
  3.6 0.7 copy-start.4
  4.5 7.0 %collective-permute-start = (f32[9,8,128]{2,1,0:T(8,128)S(1)}, f32[9,8,128]{2,1,0:T(8,128)S(1)}, u32[]{:S(2)}, u32[]{:S(2)}) collective-permute-start(f32[9,8,128]{2,1,0:T(8,128)S(1)} %get-tuple-element.12), channel_id=1, source_target_pairs={{1,0},{2,1},{3,2},{5,4},{6,5},{7,6},{9,8},{10,9},{11,10},{13,12},{... | collective-permute-start | bytes 110600 | tf_op jit(solution)/shard_map/ppermute | solution.py:482
  5.8 6.7 %collective-permute-start.1 = (f32[9,8,128]{2,1,0:T(8,128)S(1)}, f32[9,8,128]{2,1,0:T(8,128)S(1)}, u32[]{:S(2)}, u32[]{:S(2)}) collective-permute-start(f32[9,8,128]{2,1,0:T(8,128)S(1)} %get-tuple-element.13), channel_id=1, source_target_pairs={{0,1},{1,2},{2,3},{4,5},{5,6},{6,7},{8,9},{9,10},{10,11},{12,13},{... | collective-permute-start | bytes 110600 | tf_op jit(solution)/shard_map/ppermute | solution.py:482
  12.5 5.1 %collective-permute-start.2 = (f32[33,8,128]{2,1,0:T(8,128)S(1)}, f32[33,8,128]{2,1,0:T(8,128)S(1)}, u32[]{:S(2)}, u32[]{:S(2)}) collective-permute-start(f32[33,8,128]{2,1,0:T(8,128)S(1)} %shard_map.69), channel_id=1, source_target_pairs={{0,64},{64,128},{128,192},{192,256},{256,320},{320,384},{384,448},... | collective-permute-start | bytes 405512 | tf_op jit(solution)/shard_map/ppermute | solution.py:482
  15.7 5.8 %collective-permute-start.3 = (f32[33,8,128]{2,1,0:T(8,128)S(1)}, f32[33,8,128]{2,1,0:T(8,128)S(1)}, u32[]{:S(2)}, u32[]{:S(2)}) collective-permute-start(f32[33,8,128]{2,1,0:T(8,128)S(1)} %shard_map.69), channel_id=1, source_target_pairs={{64,0},{128,64},{192,128},{256,192},{320,256},{384,320},{448,384},... | collective-permute-start | bytes 405512 | tf_op jit(solution)/shard_map/ppermute | solution.py:482
  21.5 10.5 %collective-permute-start.5 = (f32[91,8,128]{2,1,0:T(8,128)S(1)}, f32[91,8,128]{2,1,0:T(8,128)S(1)}, u32[]{:S(2)}, u32[]{:S(2)}) collective-permute-start(f32[91,8,128]{2,1,0:T(8,128)S(1)} %slice_dynamic-update-slice_fusion.4.y_mid), channel_id=1, source_target_pairs={{0,60},{4,0},{8,4},{12,8},{16,12},{20,16},{24,20},{28,24},{32,28},... | collective-permute-start | bytes 1118216 | tf_op jit(solution)/shard_map/ppermute | solution.py:482
  28.0 4.5 %collective-permute-start.4 = (f32[91,8,128]{2,1,0:T(8,128)S(1)}, f32[91,8,128]{2,1,0:T(8,128)S(1)}, u32[]{:S(2)}, u32[]{:S(2)}) collective-permute-start(f32[91,8,128]{2,1,0:T(8,128)S(1)} %slice_dynamic-update-slice_fusion.4.y_mid), channel_id=1, source_target_pairs={{0,4},{4,8},{8,12},{12,16},{16,20},{20,24},{24,28},{28,32},{32,36}... | collective-permute-start | bytes 1118216 | tf_op jit(solution)/shard_map/ppermute | solution.py:482

commit v3 on v2

--- a/solution.py
+++ b/solution.py
@@ -20,6 +20,7 @@
 fine_relax = 0.6666667
 coarse_relax = 0.7
 VMEM_LIMIT = 48 * 1024 * 1024
+WHOLE_VMEM = 63 * 1024 * 1024
 
 PERM, OWN, HZ, ASG, SRC = 0, 8, 16, 24, 25
 STACK = 33
@@ -39,7 +40,7 @@
     return jax.ShapeDtypeStruct(shape, dtype)
 
 
-def call(kernel, outs, n_in, scratch=(), space=pltpu.VMEM):
+def call(kernel, outs, n_in, scratch=(), space=pltpu.VMEM, limit=VMEM_LIMIT):
     single = not isinstance(outs, (list, tuple))
     vm = pl.BlockSpec(memory_space=pltpu.VMEM)
     return pl.pallas_call(
@@ -48,7 +49,7 @@
         in_specs=[pl.BlockSpec(memory_space=space)] * n_in,
         out_specs=vm if single else [vm] * len(outs),
         scratch_shapes=list(scratch),
-        compiler_params=pltpu.CompilerParams(vmem_limit_bytes=VMEM_LIMIT),
+        compiler_params=pltpu.CompilerParams(vmem_limit_bytes=limit),
     )
 
 
@@ -273,18 +274,14 @@
     label_sums([(0, label_tiles, (tiles, diag_tiles))], sums)
     totals = lane_sums(sums[...])
 
-    def twice(low, high):
-        return jnp.where(lane < NSUB, low, pltpu.roll(high, NSUB, 1))
-
-    own, left, right = (spread(y_mid[HEAD * b + ASG, 0:1, :]) for b in (1, 0, 2))
-    tile = jnp.where(
-        row == 0, totals, jnp.where(row == 1, twice(own, own), twice(right, left))
-    )
-    for d in range(n_gy):
+    own = spread(y_mid[HEAD + ASG, 0:1, :])
+    own = jnp.where(lane < NSUB, own, pltpu.roll(own, NSUB, 1))
+    tile = jnp.where(row == 0, totals, own)[0:2]
+    for d in range(n_gy * n_col):
         chunk[d] = tile
 
 
-def one_hot_product(lefts, lows, out, n_out):
+def one_hot_product(lefts, lows):
     left = jnp.concatenate(lefts, axis=1)
     l1 = left.astype(bf16)
     rest = left - l1.astype(f32)
@@ -298,46 +295,72 @@
         ],
         axis=1,
     )
-    total = sum(
+    return sum(
         lax.dot_general(part, right, (((1,), (1,)), ((), ())), preferred_element_type=f32)
         for part in (l3, l2, l1)
     )
-    for d in range(n_out):
-        out[d] = total
 
 
 def halves(value, high):
     lane = lanes((B, LZ))
     scaled = jnp.where(high == rows((B, LZ)), value, 0.0)
-    return jnp.where(lane < NSUB, scaled, 0.0), jnp.where(lane < NSUB, 0.0, scaled)
-
-
-def first_partial(n_gy, n_out, values, out):
-    lefts, lows = [], []
-    for g in range(n_gy):
-        a = values[g, 1:2, :].astype(i32)
-        lefts.append(jnp.concatenate(halves(spread(values[g, 0:1, :]), spread(a >> 7)), axis=0))
-        lows.append(a & 127)
-    one_hot_product(lefts, lows, out, n_out)
-
-
-def second_partial(n_gy, n_out, values, first, out):
+    return jnp.concatenate(
+        [jnp.where(lane < NSUB, scaled, 0.0), jnp.where(lane < NSUB, 0.0, scaled)], axis=0
+    )
+
+
+GROUP = 8
+
+
+def first_coarse(n_bricks, n_out, values, out):
+    def one(i, total):
+        lefts, lows = [], []
+        for j in range(GROUP):
+            value = values[i * GROUP + j]
+            a = value[1:2].astype(i32)
+            lefts.append(halves(spread(value[0:1]), spread(a >> 7)))
+            lows.append(a & 127)
+        return total + one_hot_product(lefts, lows)
+
+    total = lax.fori_loop(0, n_bricks // GROUP, one, jnp.zeros((2 * B, LZ), f32))
+    for d in range(n_out):
+        out[d] = total
+
+
+def second_coarse(n_gy, n_col, n_out, values, first, out):
+    n_bricks = n_gy * n_col
     lane = lanes((B, LZ))
-    lefts, lows = [], []
-    for g in range(n_gy):
-        before, after = (g - 1) % n_gy, (g + 1) % n_gy
-        own = spread(values[g, 0:1, :] + values[before, 2:3, :])
-        own = own + pltpu.roll(spread(values[after, 2:3, :]), NSUB, 1)
-        a = first[g, 1:2, :].astype(i32)
-        mine, _ = halves(own, spread(a >> 7))
-        lows.append(a & 127)
-        a = first[g, 2:3, :].astype(i32)
-        above, below = halves(spread(values[g, 1:2, :]), spread(a >> 7))
-        lows.append(a & 127)
-        zero = jnp.zeros((B, LZ), f32)
-        lefts.append(jnp.concatenate([mine, zero, zero], axis=0))
-        lefts.append(jnp.concatenate([zero, above, below], axis=0))
-    one_hot_product(lefts, lows, out, n_out)
+    near = lanes((1, LZ)) < NSUB
+
+    def own(j):
+        before = lax.rem(j + n_bricks - n_col, n_bricks)
+        after = lax.rem(j + n_col, n_bricks)
+        mine = spread(values[j, 0:1] + values[before, 2:3])
+        return mine + pltpu.roll(spread(values[after, 2:3]), NSUB, 1)
+
+    def one(i, totals):
+        lefts, lows, edge_lefts, edge_lows = [], [], [], []
+        for j in range(GROUP // 2):
+            at = i * GROUP + 2 * j
+            pair = jnp.where(lane < NSUB, own(at), pltpu.roll(own(at + 1), NSUB, 1))
+            a = jnp.where(near, first[at, 1:2], first[at + 1, 1:2]).astype(i32)
+            lefts.append(jnp.where(spread(a >> 7) == rows((B, LZ)), pair, 0.0))
+            lows.append(a & 127)
+        for j in range(GROUP):
+            a = values[i * GROUP + j, 3:4].astype(i32)
+            edge_lefts.append(halves(spread(values[i * GROUP + j, 1:2]), spread(a >> 7)))
+            edge_lows.append(a & 127)
+        return (
+            totals[0] + one_hot_product(lefts, lows),
+            totals[1] + one_hot_product(edge_lefts, edge_lows),
+        )
+
+    mine, edges = lax.fori_loop(
+        0, n_bricks // GROUP, one, (jnp.zeros((B, LZ), f32), jnp.zeros((2 * B, LZ), f32))
+    )
+    total = jnp.concatenate([mine, edges], axis=0)
+    for d in range(n_out):
+        out[d] = total
 
 
 def lookup(table, index):
@@ -353,16 +376,13 @@
     return jnp.take_along_axis(spread(row), index, axis=1)
 
 
-def slab_total(parts, g, n_gx, n_col, part, size):
-    at = jnp.clip(g, 0, n_gx - 1) * n_col
-    total = parts[at, part : part + size]
-    for c in range(1, n_col):
-        total = total + parts[at + c, part : part + size]
+def slab_total(parts, g, n_gx, part, size):
+    total = parts[jnp.clip(g, 0, n_gx - 1), part : part + size]
     return jnp.where((g >= 0) & (g < n_gx), total, 0.0)
 
 
-def guess(parts, g, n_gx, n_col):
-    total = slab_total(parts, g, n_gx, n_col, 0, 2 * B)
+def guess(parts, g, n_gx):
+    total = slab_total(parts, g, n_gx, 0, 2 * B)
     exists = (g >= 0) & (g < n_gx)
     rhs, diag = total[0:B], jnp.where(exists, total[B : 2 * B], 1.0)
     return rhs, diag, coarse_relax * rhs / diag
@@ -397,7 +417,7 @@
     row = rows((B, LZ))
     r = slice(B, 2 * B)
     for i in range(3):
-        coarse[i] = guess(parts, gx + i - 1, n_gx, n_col)[2]
+        coarse[i] = guess(parts, gx + i - 1, n_gx)[2]
     expand(coarse, (y_lo, y_mid, y_hi), labels, both.at[0], tables, 0, NP - 1)
 
     def after(k):
@@ -431,12 +451,14 @@
     sums[NSUB : 2 * NSUB, :] = jnp.zeros((NSUB, LZ), f32)
     label_sums(groups, sums)
     totals = lane_sums(sums[...])
+    right, left = (spread(y_mid[HEAD * b + ASG, 0:1, :]) for b in (2, 0))
+    asg = jnp.where(lanes((B, LZ)) < NSUB, right, pltpu.roll(left, NSUB, 1))
     tile = jnp.where(
-        row == 0,
-        totals[:, 0:LZ],
-        jnp.where(row == 1, totals[:, LZ : 2 * LZ], totals[:, 2 * LZ :]),
-    )
-    for d in range(n_gy):
+        row < 2,
+        jnp.where(row == 0, totals[:, 0:LZ], totals[:, LZ : 2 * LZ]),
+        jnp.where(row == 2, totals[:, 2 * LZ :], asg),
+    )[0:4]
+    for d in range(n_gy * n_col):
         chunk[d] = tile
 
 
@@ -445,11 +467,11 @@
     gx, gy, col = (lax.axis_index(a) for a in ("gx", "gy", "col"))
     for i in range(3):
         g = gx + i - 1
-        rhs, diag, start = guess(parts, g, n_gx, n_col)
+        rhs, diag, start = guess(parts, g, n_gx)
         image = (
-            slab_total(images, g, n_gx, n_col, 0, B)
-            + slab_total(images, g - 1, n_gx, n_col, B, B)
-            + slab_total(images, g + 1, n_gx, n_col, 2 * B, B)
+            slab_total(images, g, n_gx, 0, B)
+            + slab_total(images, g - 1, n_gx, B, B)
+            + slab_total(images, g + 1, n_gx, 2 * B, B)
         )
         second = start + coarse_relax * (rhs - image) / diag
         coarse[i] = jnp.where((g >= 0) & (g < n_gx), second, 0.0)
@@ -472,7 +494,7 @@
 
 
 def on_device(n_gx, n_gy, n_col, permeability, source, ownership, assignment, layer_flags):
-    n_out = n_gx * n_col
+    n_bricks = n_gy * n_col
     sizes = (n_gx, n_gy, n_col)
     vm = pltpu.VMEM
     fields = vm((2, NP + 2, *FULL), f32)
@@ -490,6 +512,7 @@
             vm((n_col, LZ), i32), pltpu.SemaphoreType.DMA((5,)),
         ],
         space=pl.ANY,
+        limit=WHOLE_VMEM,
     )(permeability, source, ownership, assignment.reshape(1, NSUB), layer_flags.reshape(n_col, LZ))
     mr, ml = send(mr, "col", -1), send(ml, "col", 1)
     stack = call(stack_up, sds(STACK, B, LZ), 3)(base, mr, ml)
@@ -503,7 +526,7 @@
     weights, labels, chunk, dvals, paths = call(
         functools.partial(first_sums, *sizes),
         [
-            sds(6, NP, *FULL), sds(NP, *FULL, dtype=i32), sds(n_gy, B, LZ), sds(*plane),
+            sds(6, NP, *FULL), sds(NP, *FULL, dtype=i32), sds(n_bricks, 2, LZ), sds(*plane),
             sds(4, B, LZ),
         ],
         4,
@@ -512,23 +535,23 @@
             vm((2 * NSUB, LZ), f32),
         ],
     )(y_lo, line, y_hi, flags)
-    bricks = lax.all_to_all(chunk, "gy", 0, 0, tiled=True)
+    bricks = lax.all_to_all(chunk, ("gy", "col"), 0, 0, tiled=True)
     parts = call(
-        functools.partial(first_partial, n_gy, n_out), sds(n_out, 2 * B, LZ), 1
+        functools.partial(first_coarse, n_bricks, n_gx), sds(n_gx, 2 * B, LZ), 1
     )(bricks)
-    parts = lax.all_to_all(parts, ("gx", "col"), 0, 0, tiled=True)
+    parts = lax.all_to_all(parts, "gx", 0, 0, tiled=True)
     tables = [vm((3, B, LZ), f32), vm((3, 3, B, LZ), f32)]
     chunk = call(
         functools.partial(second_sums, *sizes),
-        sds(n_gy, B, LZ),
+        sds(n_bricks, 4, LZ),
         8,
         scratch=[fields, *tables, vm((4, B, LZ), f32), vm((6 * NSUB, LZ), f32)],
     )(parts, weights, labels, y_lo, line, y_hi, dvals, paths)
-    images = lax.all_to_all(chunk, "gy", 0, 0, tiled=True)
+    images = lax.all_to_all(chunk, ("gy", "col"), 0, 0, tiled=True)
     images = call(
-        functools.partial(second_partial, n_gy, n_out), sds(n_out, 3 * B, LZ), 2
+        functools.partial(second_coarse, n_gy, n_col, n_gx), sds(n_gx, 3 * B, LZ), 2
     )(images, bricks)
-    images = lax.all_to_all(images, ("gx", "col"), 0, 0, tiled=True)
+    images = lax.all_to_all(images, "gx", 0, 0, tiled=True)
     return call(
         functools.partial(last_sweeps, *sizes),
         [sds(*plane), sds(1, B * LZ // (n_gy * n_col))],

time: 125 us -> 124 us (level)
  Pallas kernels: 19 us -> 25.9 us
  blocking collectives: 73 us -> 66.7 us
  local copies, waits for them, and re-layouts: 3.64 us -> 1.61 us
    all_to_all x4, blocking collectives: 73 us -> 66.7 us  [the longest x1 29.7 us: on_device(): bricks = lax.all_to_all(chunk, ('gy', 'col'), 0, 0, tiled=True)]
    pallas_call x3, Pallas kernels: 8.43 us -> 14 us  [the longest x1 6.7 us: on_device(): call(functools.partial(second_sums, *sizes), sds(n_bricks, 4, LZ), 8, scr...]
    unnamed x15 -> x9, local copies, waits for them, and re-layouts: 3.63 us -> 1.61 us
    pallas_call x1, Pallas kernels: 0.25 us -> 1.58 us  [on_device(): call(z_messages, [sds(B + 1, B, LZ)] * 2 + [sds(3 * B + 1, B, LZ), sds(3,...]
where the time goes in v3:
time: 124 us; the launch traced here: 123 us
  blocking collectives  66.7 us (54%)
  Pallas kernels  25.9 us (21%)
  starting transfers between devices  17.9 us (14%)
  waiting for transfers between devices  10.3 us (8%)
  local copies, waits for them, and re-layouts  1.61 us (1%)
    all_to_all x1, blocking collectives, on_device(): bricks = lax.all_to_all(chunk, ('gy', 'col'), 0, 0, tiled=True)  29.7 us
    all_to_all x1, blocking collectives, on_device(): images = lax.all_to_all(chunk, ('gy', 'col'), 0, 0, tiled=True)  18.2 us
    ppermute x6, starting transfers between devices, send(): return lax.ppermute(x, axis, steps(lax.axis_size(axis), by, wrap))  17.9 us
    all_to_all x1, blocking collectives, on_device(): parts = lax.all_to_all(parts, 'gx', 0, 0, tiled=True)  11.2 us
    ppermute x6, waiting for transfers between devices, send(): return lax.ppermute(x, axis, steps(lax.axis_size(axis), by, wrap))  10.3 us
    all_to_all x1, blocking collectives, on_device(): images = lax.all_to_all(images, 'gx', 0, 0, tiled=True)  7.68 us
    pallas_call x1, Pallas kernels, on_device(): call(functools.partial(first_sums, *sizes), [sds(6, NP, *FULL), sds(NP, *...  7.2 us
    pallas_call x1, Pallas kernels, on_device(): call(functools.partial(second_sums, *sizes), sds(n_bricks, 4, LZ), 8, scr...  6.7 us
  transfers between devices with their start and end apart: 6, of which 5 were waited for; matrix products, arithmetic and copies ran while one was open for 0% of the time, Pallas kernels for 0%

profile of v3, /device:TPU:1, one launch (start us, length us, event | category | flops | bytes accessed | tf_op | source)
XLA Modules:
  0.0 123.3 jit_solution(5614577792597867676)
XLA Ops:
  0.6 1.6 %shard_map.68 = (f32[9,8,128]{2,1,0:T(8,128)}, f32[9,8,128]{2,1,0:T(8,128)}, f32[25,8,128]{2,1,0:T(8,128)}, f32[3,128]{1,0:T(4,128)}) custom-call(f32[8,8,128]{2,1,0:T(8,128)} %perm_in.1, f32[8,8,128]{2,1,0:T(8,128)} %src_in.1, s32[8,8,128]{2,1,0:T(8,128)} %own_in.1, s32[1,64]{1,0:T(1,128)} %bitcast.3, s32[4,128]{1,0:T(4,128)} %bitcast.2), custom_call_target="tpu_custom_call" | custom-call | tf_op jit(solution)/shard_map/pallas_call | solution.py:506
  2.2 1.3 %collective-permute-start = (f32[9,8,128]{2,1,0:T(8,128)}, f32[9,8,128]{2,1,0:T(8,128)S(1)}, u32[]{:S(2)}, u32[]{:S(2)}) collective-permute-start(f32[9,8,128]{2,1,0:T(8,128)} %get-tuple-element.12), channel_id=1, source_target_pairs={{1,0},{2,1},{3,2},{5,4},{6,5},{7,6},{9,8},{10,9},{11,10},{13,12},{... | collective-permute-start | bytes 110600 | tf_op jit(solution)/shard_map/ppermute | solution.py:504
  3.5 5.7 %collective-permute-start.1 = (f32[9,8,128]{2,1,0:T(8,128)}, f32[9,8,128]{2,1,0:T(8,128)S(1)}, u32[]{:S(2)}, u32[]{:S(2)}) collective-permute-start(f32[9,8,128]{2,1,0:T(8,128)} %get-tuple-element.13), channel_id=1, source_target_pairs={{0,1},{1,2},{2,3},{4,5},{5,6},{6,7},{8,9},{9,10},{10,11},{12,13},{... | collective-permute-start | bytes 110600 | tf_op jit(solution)/shard_map/ppermute | solution.py:504
  9.2 0.0 collective-permute-done.mr
  9.2 1.3 %collective-permute-done.1.ml = f32[9,8,128]{2,1,0:T(8,128)S(1)} collective-permute-done((f32[9,8,128]{2,1,0:T(8,128)}, f32[9,8,128]{2,1,0:T(8,128)S(1)}, u32[]{:S(2)}, u32[]{:S(2)}) %collective-permute-start.1) | collective-permute-done | bytes 36896 | tf_op jit(solution)/shard_map/ppermute | solution.py:504
  10.6 0.0 copy-start
  10.6 0.9 copy-done
  11.5 3.2 %collective-permute-start.2 = (f32[33,8,128]{2,1,0:T(8,128)S(1)}, f32[33,8,128]{2,1,0:T(8,128)S(1)}, u32[]{:S(2)}, u32[]{:S(2)}) collective-permute-start(f32[33,8,128]{2,1,0:T(8,128)S(1)} %shard_map.69), channel_id=1, source_target_pairs={{0,64},{64,128},{128,192},{192,256},{256,320},{320,384},{384,448},... | collective-permute-start | bytes 405512 | tf_op jit(solution)/shard_map/ppermute | solution.py:504
  14.6 1.3 %collective-permute-start.3 = (f32[33,8,128]{2,1,0:T(8,128)S(1)}, f32[33,8,128]{2,1,0:T(8,128)S(1)}, u32[]{:S(2)}, u32[]{:S(2)}) collective-permute-start(f32[33,8,128]{2,1,0:T(8,128)S(1)} %shard_map.69), channel_id=1, source_target_pairs={{64,0},{128,64},{192,128},{256,192},{320,256},{384,320},{448,384},... | collective-permute-start | bytes 405512 | tf_op jit(solution)/shard_map/ppermute | solution.py:504
  15.9 0.7 collective-permute-done.2
  16.6 3.8 %collective-permute-done.3 = f32[33,8,128]{2,1,0:T(8,128)S(1)} collective-permute-done((f32[33,8,128]{2,1,0:T(8,128)S(1)}, f32[33,8,128]{2,1,0:T(8,128)S(1)}, u32[]{:S(2)}, u32[]{:S(2)}) %collective-permute-start.3) | collective-permute-done | bytes 135200 | tf_op jit(solution)/shard_map/ppermute | solution.py:504
  20.4 6.5 %collective-permute-start.5 = (f32[91,8,128]{2,1,0:T(8,128)S(1)}, f32[91,8,128]{2,1,0:T(8,128)S(1)}, u32[]{:S(2)}, u32[]{:S(2)}) collective-permute-start(f32[91,8,128]{2,1,0:T(8,128)S(1)} %slice_dynamic-update-slice_fusion.4.y_mid), channel_id=1, source_target_pairs={{0,60},{4,0},{8,4},{12,8},{16,12},{20,16},{24,20},{28,24},{32,28},... | collective-permute-start | bytes 1118216 | tf_op jit(solution)/shard_map/ppermute | solution.py:504
  27.0 0.0 collective-permute-start.4
  27.0 3.9 %collective-permute-done.5.y_hi = f32[91,8,128]{2,1,0:T(8,128)S(1)} collective-permute-done((f32[91,8,128]{2,1,0:T(8,128)S(1)}, f32[91,8,128]{2,1,0:T(8,128)S(1)}, u32[]{:S(2)}, u32[]{:S(2)}) %collective-permute-start.5) | collective-permute-done | bytes 372768 | tf_op jit(solution)/shard_map/ppermute | solution.py:504
  30.9 0.6 collective-permute-done.4.y_lo
  31.5 0.0 copy-start.1
  31.5 0.7 copy-done.1
  32.2 7.2 %shard_map.70 = (f32[6,24,24,256]{3,2,1,0:T(8,128)S(1)}, s32[24,24,256]{2,1,0:T(8,128)S(1)}, f32[64,2,128]{2,1,0:T(2,128)S(1)}, f32[8,8,128]{2,1,0:T(8,128)S(1)}, f32[4,8,128]{2,1,0:T(8,128)S(1)}) custom-call(f32[91,8,128]{2,1,0:T(8,128)S(1)} %collective-permute-done.4.y_lo, f32[91,8,128]{2,1,0:T(8,128)S(1)} %slice_dynamic-update-slice_fusion.4.y_mid, ...), custom_call_target="tpu_custom_call" | custom-call | tf_op jit(solution)/shard_map/pallas_call | solution.py:526
  39.4 29.7 %all_to_all.20.values.first = f32[64,2,128]{2,1,0:T(2,128)S(1)} all-to-all(f32[64,2,128]{2,1,0:T(2,128)S(1)} %get-tuple-element.15), channel_id=1, replica_groups=mesh['gx'=8,'gy'=16,'col'=4] {'gy','col'}, dimensions={0} | all-to-all | bytes 131072 | tf_op jit(solution)/shard_map/all_to_all | solution.py:538
  69.1 2.9 %shard_map.71 = f32[8,16,128]{2,1,0:T(8,128)S(1)} custom-call(f32[64,2,128]{2,1,0:T(2,128)S(1)} %all_to_all.20.values.first), custom_call_target="tpu_custom_call" | custom-call | tf_op jit(solution)/shard_map/pallas_call | solution.py:539
  72.0 11.2 %all_to_all.21.parts = f32[8,16,128]{2,1,0:T(8,128)S(1)} all-to-all(f32[8,16,128]{2,1,0:T(8,128)S(1)} %shard_map.71), channel_id=1, replica_groups=mesh['gx'=8,'gy'=16,'col'=4] {'gx'}, dimensions={0} | all-to-all | bytes 131072 | tf_op jit(solution)/shard_map/all_to_all | solution.py:542
  83.1 6.7 %shard_map.72 = f32[64,4,128]{2,1,0:T(4,128)S(1)} custom-call(f32[8,16,128]{2,1,0:T(8,128)S(1)} %all_to_all.21.parts, f32[6,24,24,256]{3,2,1,0:T(8,128)S(1)} %get-tuple-element.16.weights, s32[24,24,256]{2,1,0:T(8,128)S(1)} %get-tuple-element.17.labels, f32[91,8,128]{2,1,0:T(8,128)S(1)} %collective-permute-done.4.y_lo, ...), custom_call_target="tpu_custom_call" | custom-call | tf_op jit(solution)/shard_map/pallas_call | solution.py:544
  89.8 18.2 %all_to_all.22.values = f32[64,4,128]{2,1,0:T(4,128)S(1)} all-to-all(f32[64,4,128]{2,1,0:T(4,128)S(1)} %shard_map.72), channel_id=1, replica_groups=mesh['gx'=8,'gy'=16,'col'=4] {'gy','col'}, dimensions={0} | all-to-all | bytes 262144 | tf_op jit(solution)/shard_map/all_to_all | solution.py:550
  108.0 4.4 %shard_map.73 = f32[8,24,128]{2,1,0:T(8,128)S(1)} custom-call(f32[64,4,128]{2,1,0:T(4,128)S(1)} %all_to_all.22.values, f32[64,2,128]{2,1,0:T(2,128)S(1)} %all_to_all.20.values.first), custom_call_target="tpu_custom_call" | custom-call | tf_op jit(solution)/shard_map/pallas_call | solution.py:551
  112.4 7.7 %all_to_all.23.images = f32[8,24,128]{2,1,0:T(8,128)S(1)} all-to-all(f32[8,24,128]{2,1,0:T(8,128)S(1)} %shard_map.73), channel_id=1, replica_groups=mesh['gx'=8,'gy'=16,'col'=4] {'gx'}, dimensions={0} | all-to-all | bytes 196608 | tf_op jit(solution)/shard_map/all_to_all | solution.py:554
  120.1 3.2 %shard_map.74 = (f32[8,8,128]{2,1,0:T(8,128)}, f32[1,16]{1,0:T(1,128)}) custom-call(f32[8,16,128]{2,1,0:T(8,128)S(1)} %all_to_all.21.parts, f32[8,24,128]{2,1,0:T(8,128)S(1)} %all_to_all.23.images, f32[6,24,24,256]{3,2,1,0:T(8,128)S(1)} %get-tuple-element.16.weights, s32[24,24,256]{2,1,0:T(8,128)S(1)} %get-tuple-element.17.labels, ...), custom_call_target="tpu_custom_call" | custom-call | tf_op jit(solution)/shard_map/pallas_call | solution.py:555
  (7 shorter events, 0.1 us)
Async XLA Ops:
  2.2 7.0 %collective-permute-start = (f32[9,8,128]{2,1,0:T(8,128)}, f32[9,8,128]{2,1,0:T(8,128)S(1)}, u32[]{:S(2)}, u32[]{:S(2)}) collective-permute-start(f32[9,8,128]{2,1,0:T(8,128)} %get-tuple-element.12), channel_id=1, source_target_pairs={{1,0},{2,1},{3,2},{5,4},{6,5},{7,6},{9,8},{10,9},{11,10},{13,12},{... | collective-permute-start | bytes 110600 | tf_op jit(solution)/shard_map/ppermute | solution.py:504
  3.5 7.0 %collective-permute-start.1 = (f32[9,8,128]{2,1,0:T(8,128)}, f32[9,8,128]{2,1,0:T(8,128)S(1)}, u32[]{:S(2)}, u32[]{:S(2)}) collective-permute-start(f32[9,8,128]{2,1,0:T(8,128)} %get-tuple-element.13), channel_id=1, source_target_pairs={{0,1},{1,2},{2,3},{4,5},{5,6},{6,7},{8,9},{9,10},{10,11},{12,13},{... | collective-permute-start | bytes 110600 | tf_op jit(solution)/shard_map/ppermute | solution.py:504
  10.6 0.9 copy-start
  11.5 5.1 %collective-permute-start.2 = (f32[33,8,128]{2,1,0:T(8,128)S(1)}, f32[33,8,128]{2,1,0:T(8,128)S(1)}, u32[]{:S(2)}, u32[]{:S(2)}) collective-permute-start(f32[33,8,128]{2,1,0:T(8,128)S(1)} %shard_map.69), channel_id=1, source_target_pairs={{0,64},{64,128},{128,192},{192,256},{256,320},{320,384},{384,448},... | collective-permute-start | bytes 405512 | tf_op jit(solution)/shard_map/ppermute | solution.py:504
  14.6 5.8 %collective-permute-start.3 = (f32[33,8,128]{2,1,0:T(8,128)S(1)}, f32[33,8,128]{2,1,0:T(8,128)S(1)}, u32[]{:S(2)}, u32[]{:S(2)}) collective-permute-start(f32[33,8,128]{2,1,0:T(8,128)S(1)} %shard_map.69), channel_id=1, source_target_pairs={{64,0},{128,64},{192,128},{256,192},{320,256},{384,320},{448,384},... | collective-permute-start | bytes 405512 | tf_op jit(solution)/shard_map/ppermute | solution.py:504
  20.4 10.5 %collective-permute-start.5 = (f32[91,8,128]{2,1,0:T(8,128)S(1)}, f32[91,8,128]{2,1,0:T(8,128)S(1)}, u32[]{:S(2)}, u32[]{:S(2)}) collective-permute-start(f32[91,8,128]{2,1,0:T(8,128)S(1)} %slice_dynamic-update-slice_fusion.4.y_mid), channel_id=1, source_target_pairs={{0,60},{4,0},{8,4},{12,8},{16,12},{20,16},{24,20},{28,24},{32,28},... | collective-permute-start | bytes 1118216 | tf_op jit(solution)/shard_map/ppermute | solution.py:504
  27.0 4.5 %collective-permute-start.4 = (f32[91,8,128]{2,1,0:T(8,128)S(1)}, f32[91,8,128]{2,1,0:T(8,128)S(1)}, u32[]{:S(2)}, u32[]{:S(2)}) collective-permute-start(f32[91,8,128]{2,1,0:T(8,128)S(1)} %slice_dynamic-update-slice_fusion.4.y_mid), channel_id=1, source_target_pairs={{0,4},{4,8},{8,12},{12,16},{16,20},{20,24},{24,28},{28,32},{32,36}... | collective-permute-start | bytes 1118216 | tf_op jit(solution)/shard_map/ppermute | solution.py:504
  31.5 0.7 copy-start.1

commit v4 on v3

--- a/solution.py
+++ b/solution.py
@@ -16,7 +16,7 @@
 NP = 3 * B
 W = 9
 FULL = (NP, 2 * LZ)
-CHUNK = 8
+CHUNK = 12
 fine_relax = 0.6666667
 coarse_relax = 0.7
 VMEM_LIMIT = 48 * 1024 * 1024
@@ -194,7 +194,7 @@
             labels[p, r, LZ:] = jnp.where(halo, own_z, 0.0).astype(i32)
         return carry
 
-    lax.fori_loop(0, NP, fill, 0, unroll=4)
+    lax.fori_loop(0, NP, fill, 0, unroll=8)
     kext[0] = jnp.ones(FULL, f32)
     kext[NP + 1] = jnp.ones(FULL, f32)
 
@@ -231,35 +231,38 @@
         fz_left = pltpu.roll(fz_right, 1, 1)
         fx_up, fx_down = fx[p + 1], fx[p]
         diag = fx_up + fx_down + fy_up + fy_down + fz_right + fz_left
-        inverse = 1.0 / diag
-        scale = jnp.where(out, 0.0, fine_relax) * inverse
+        scale = jnp.where(out, 0.0, fine_relax) / diag
         for i, face in enumerate((fx_up, fx_down, fy_up, fy_down, fz_right, fz_left)):
             weights[i, p] = face * scale
-        at = 3 * HEAD + jnp.clip(p - 4, 0, 2 * B - 1)
-        hz = HEAD * b + HZ + lax.rem(p, B)
+        both[0, p + 1] = scale
+        dvals[p] = diag[B : 2 * B, 0:LZ]
+        return carry
+
+    lax.fori_loop(0, NP, terms, 0, unroll=8)
+
+    def start(i, carry):
+        p = i + B // 2
+        packed_at = HEAD * (p // B) + HZ + lax.rem(p, B)
         for ty in range(3):
             line = lines[ty]
             r = slice(ty * B, (ty + 1) * B)
-            packed = line[hz]
+            packed = line[packed_at]
             src_z = jnp.where(near_side, pltpu.roll(packed, LZ - 32, 1), pltpu.roll(packed, 32, 1))
-            both[1, p + 1, r, 0:LZ] = line[at] * inverse[r, 0:LZ]
-            both[1, p + 1, r, LZ:] = jnp.where(halo, src_z, 0.0) * inverse[r, LZ:]
-
-        @pl.when(b == 1)
-        def _():
-            q = p - B
-            r = slice(B, 2 * B)
-            dvals[q] = diag[r, 0:LZ]
-            up, down = (face[r, 0:LZ] for face in (fy_up, fy_down))
-            s = scale[r, 0:LZ]
-            rise = row_product(jnp.where(row == 0, 1.0, down * s))
-            fall = row_product(jnp.where(row == B - 1, 1.0, up * s))
-            paths[2, pl.ds(q, 1), :] = rise[0:1] * up[B - 1 : B]
-            paths[3, pl.ds(q, 1), :] = fall[0:1] * down[0:1]
-
-        return carry
-
-    lax.fori_loop(0, NP, terms, 0, unroll=2)
+            over = both[0, p + 1, r, :] * (1.0 / fine_relax)
+            both[1, p + 1, r, 0:LZ] = line[3 * HEAD + i] * over[:, 0:LZ]
+            both[1, p + 1, r, LZ:] = jnp.where(halo, src_z, 0.0) * over[:, LZ:]
+        return carry
+
+    lax.fori_loop(0, 2 * B, start, 0, unroll=8)
+    r = slice(B, 2 * B)
+    for q in range(B):
+        p = B + q
+        up, down = weights[2, p, r, 0:LZ], weights[3, p, r, 0:LZ]
+        rise = row_product(jnp.where(row == 0, 1.0, down)) * up
+        fall = row_product(jnp.where(row == B - 1, 1.0, up)) * down
+        per = dvals[p] * (1.0 / fine_relax)
+        paths[2, q : q + 1, :] = (rise * per)[B - 1 : B]
+        paths[3, q : q + 1, :] = (fall * per)[0:1]
     rise, fall = fx[2 * B, B : 2 * B, 0:LZ], fx[B, B : 2 * B, 0:LZ]
     for p in range(B + 1, 2 * B):
         rise = rise * weights[1, p, B : 2 * B, 0:LZ]
@@ -268,8 +271,8 @@
     paths[1] = fall
 
     sweeps(both, weights, 5, 8)
-    tiles = [both[1, B + 1 + q, B : 2 * B, 0:LZ] * dvals[q] for q in range(B)]
-    diag_tiles = [dvals[q] for q in range(B)]
+    tiles = [both[1, B + 1 + q, B : 2 * B, 0:LZ] * dvals[B + q] for q in range(B)]
+    diag_tiles = [dvals[B + q] for q in range(B)]
     label_tiles = [labels[B + q, B : 2 * B, 0:LZ] for q in range(B)]
     label_sums([(0, label_tiles, (tiles, diag_tiles))], sums)
     totals = lane_sums(sums[...])
@@ -295,10 +298,15 @@
         ],
         axis=1,
     )
-    return sum(
-        lax.dot_general(part, right, (((1,), (1,)), ((), ())), preferred_element_type=f32)
-        for part in (l3, l2, l1)
-    )
+    return lax.dot_general(
+        jnp.concatenate([l1, l2, l3], axis=0), right, (((1,), (1,)), ((), ())),
+        preferred_element_type=f32,
+    )
+
+
+def joined(total):
+    n = total.shape[0] // 3
+    return (total[2 * n :] + total[n : 2 * n]) + total[:n]
 
 
 def halves(value, high):
@@ -309,20 +317,21 @@
     )
 
 
-GROUP = 8
+GROUP = 64
 
 
 def first_coarse(n_bricks, n_out, values, out):
     def one(i, total):
         lefts, lows = [], []
-        for j in range(GROUP):
-            value = values[i * GROUP + j]
+        for j in range(min(GROUP, n_bricks)):
+            value = values[i * min(GROUP, n_bricks) + j]
             a = value[1:2].astype(i32)
             lefts.append(halves(spread(value[0:1]), spread(a >> 7)))
             lows.append(a & 127)
         return total + one_hot_product(lefts, lows)
 
-    total = lax.fori_loop(0, n_bricks // GROUP, one, jnp.zeros((2 * B, LZ), f32))
+    total = lax.fori_loop(0, n_bricks // min(GROUP, n_bricks), one, jnp.zeros((6 * B, LZ), f32))
+    total = joined(total)
     for d in range(n_out):
         out[d] = total
 
@@ -340,15 +349,15 @@
 
     def one(i, totals):
         lefts, lows, edge_lefts, edge_lows = [], [], [], []
-        for j in range(GROUP // 2):
-            at = i * GROUP + 2 * j
+        for j in range(min(GROUP, n_bricks) // 2):
+            at = i * min(GROUP, n_bricks) + 2 * j
             pair = jnp.where(lane < NSUB, own(at), pltpu.roll(own(at + 1), NSUB, 1))
             a = jnp.where(near, first[at, 1:2], first[at + 1, 1:2]).astype(i32)
             lefts.append(jnp.where(spread(a >> 7) == rows((B, LZ)), pair, 0.0))
             lows.append(a & 127)
-        for j in range(GROUP):
-            a = values[i * GROUP + j, 3:4].astype(i32)
-            edge_lefts.append(halves(spread(values[i * GROUP + j, 1:2]), spread(a >> 7)))
+        for j in range(min(GROUP, n_bricks)):
+            a = values[i * min(GROUP, n_bricks) + j, 3:4].astype(i32)
+            edge_lefts.append(halves(spread(values[i * min(GROUP, n_bricks) + j, 1:2]), spread(a >> 7)))
             edge_lows.append(a & 127)
         return (
             totals[0] + one_hot_product(lefts, lows),
@@ -356,9 +365,9 @@
         )
 
     mine, edges = lax.fori_loop(
-        0, n_bricks // GROUP, one, (jnp.zeros((B, LZ), f32), jnp.zeros((2 * B, LZ), f32))
-    )
-    total = jnp.concatenate([mine, edges], axis=0)
+        0, n_bricks // min(GROUP, n_bricks), one, (jnp.zeros((3 * B, LZ), f32), jnp.zeros((6 * B, LZ), f32))
+    )
+    total = jnp.concatenate([joined(mine), joined(edges)], axis=0)
     for d in range(n_out):
         out[d] = total
 
@@ -408,7 +417,7 @@
             u[p + 1, r, LZ:] = jnp.where(near_side, pick(t[1:2], lab), pick(t[2:3], lab))
         return carry
 
-    lax.fori_loop(first, last + 1, one, 0, unroll=4)
+    lax.fori_loop(first, last + 1, one, 0, unroll=8)
 
 
 def second_sums(n_gx, n_gy, n_col, parts, weights, labels, y_lo, y_mid, y_hi, dvals, paths,
@@ -437,7 +446,7 @@
                 ends[3, q : q + 1, :] = plane[B - 1 : B] * -paths[3, q : q + 1, :]
 
     sweeps(both, weights, 0, 8, after=after, operator_at=4)
-    tiles = [both[1, B + 1 + q, r, 0:LZ] * dvals[q] for q in range(B)]
+    tiles = [both[1, B + 1 + q, r, 0:LZ] * dvals[B + q] for q in range(B)]
     label_tiles = [labels[B + q, r, 0:LZ] for q in range(B)]
     beyond = [labels[2 * B, r, 0:LZ], labels[B - 1, r, 0:LZ]]
     for at in (2 * B, B - 1):
@@ -526,7 +535,7 @@
     weights, labels, chunk, dvals, paths = call(
         functools.partial(first_sums, *sizes),
         [
-            sds(6, NP, *FULL), sds(NP, *FULL, dtype=i32), sds(n_bricks, 2, LZ), sds(*plane),
+            sds(6, NP, *FULL), sds(NP, *FULL, dtype=i32), sds(n_bricks, 2, LZ), sds(NP, B, LZ),
             sds(4, B, LZ),
         ],
         4,

time: 124 us -> 115 us (0.927)
  Pallas kernels: 25.9 us -> 16.6 us
    pallas_call x1, Pallas kernels: 7.2 us -> 3.86 us  [on_device(): call(functools.partial(first_sums, *sizes), [sds(6, NP, *FULL), sds(NP, *...]
    pallas_call x1, Pallas kernels: 4.36 us -> 1.09 us  [on_device(): call(functools.partial(second_coarse, n_gy, n_col, n_gx), sds(n_gx, 3 * B...]
    pallas_call x1, Pallas kernels: 2.89 us -> 0.74 us  [on_device(): call(functools.partial(first_coarse, n_bricks, n_gx), sds(n_gx, 2 * B, LZ...]
where the time goes in v4:
time: 115 us; the launch traced here: 114 us
  blocking collectives  66.7 us (58%)
  starting transfers between devices  17.9 us (16%)
  Pallas kernels  16.6 us (14%)
  waiting for transfers between devices  10.3 us (9%)
  local copies, waits for them, and re-layouts  1.61 us (1%)
    all_to_all x1, blocking collectives, on_device(): bricks = lax.all_to_all(chunk, ('gy', 'col'), 0, 0, tiled=True)  29.7 us
    all_to_all x1, blocking collectives, on_device(): images = lax.all_to_all(chunk, ('gy', 'col'), 0, 0, tiled=True)  18.2 us
    ppermute x6, starting transfers between devices, send(): return lax.ppermute(x, axis, steps(lax.axis_size(axis), by, wrap))  17.9 us
    all_to_all x1, blocking collectives, on_device(): parts = lax.all_to_all(parts, 'gx', 0, 0, tiled=True)  11.1 us
    ppermute x6, waiting for transfers between devices, send(): return lax.ppermute(x, axis, steps(lax.axis_size(axis), by, wrap))  10.3 us
    all_to_all x1, blocking collectives, on_device(): images = lax.all_to_all(images, 'gx', 0, 0, tiled=True)  7.68 us
    pallas_call x1, Pallas kernels, on_device(): call(functools.partial(second_sums, *sizes), sds(n_bricks, 4, LZ), 8, scr...  6.35 us
    pallas_call x1, Pallas kernels, on_device(): call(functools.partial(first_sums, *sizes), [sds(6, NP, *FULL), sds(NP, *...  3.86 us
  transfers between devices with their start and end apart: 6, of which 5 were waited for; matrix products, arithmetic and copies ran while one was open for 0% of the time, Pallas kernels for 0%

profile of v4, /device:TPU:1, one launch (start us, length us, event | category | flops | bytes accessed | tf_op | source)
XLA Modules:
  0.0 113.9 jit_solution(9718327724722028670)
XLA Ops:
  0.6 1.6 %shard_map.68 = (f32[9,8,128]{2,1,0:T(8,128)}, f32[9,8,128]{2,1,0:T(8,128)}, f32[25,8,128]{2,1,0:T(8,128)}, f32[3,128]{1,0:T(4,128)}) custom-call(f32[8,8,128]{2,1,0:T(8,128)} %perm_in.1, f32[8,8,128]{2,1,0:T(8,128)} %src_in.1, s32[8,8,128]{2,1,0:T(8,128)} %own_in.1, s32[1,64]{1,0:T(1,128)} %bitcast.3, s32[4,128]{1,0:T(4,128)} %bitcast.2), custom_call_target="tpu_custom_call" | custom-call | tf_op jit(solution)/shard_map/pallas_call | solution.py:515
  2.2 1.3 %collective-permute-start = (f32[9,8,128]{2,1,0:T(8,128)}, f32[9,8,128]{2,1,0:T(8,128)S(1)}, u32[]{:S(2)}, u32[]{:S(2)}) collective-permute-start(f32[9,8,128]{2,1,0:T(8,128)} %get-tuple-element.12), channel_id=1, source_target_pairs={{1,0},{2,1},{3,2},{5,4},{6,5},{7,6},{9,8},{10,9},{11,10},{13,12},{... | collective-permute-start | bytes 110600 | tf_op jit(solution)/shard_map/ppermute | solution.py:513
  3.5 5.7 %collective-permute-start.1 = (f32[9,8,128]{2,1,0:T(8,128)}, f32[9,8,128]{2,1,0:T(8,128)S(1)}, u32[]{:S(2)}, u32[]{:S(2)}) collective-permute-start(f32[9,8,128]{2,1,0:T(8,128)} %get-tuple-element.13), channel_id=1, source_target_pairs={{0,1},{1,2},{2,3},{4,5},{5,6},{6,7},{8,9},{9,10},{10,11},{12,13},{... | collective-permute-start | bytes 110600 | tf_op jit(solution)/shard_map/ppermute | solution.py:513
  9.2 0.0 collective-permute-done.mr
  9.2 1.3 %collective-permute-done.1.ml = f32[9,8,128]{2,1,0:T(8,128)S(1)} collective-permute-done((f32[9,8,128]{2,1,0:T(8,128)}, f32[9,8,128]{2,1,0:T(8,128)S(1)}, u32[]{:S(2)}, u32[]{:S(2)}) %collective-permute-start.1) | collective-permute-done | bytes 36896 | tf_op jit(solution)/shard_map/ppermute | solution.py:513
  10.6 0.0 copy-start
  10.6 0.9 copy-done
  11.5 3.2 %collective-permute-start.2 = (f32[33,8,128]{2,1,0:T(8,128)S(1)}, f32[33,8,128]{2,1,0:T(8,128)S(1)}, u32[]{:S(2)}, u32[]{:S(2)}) collective-permute-start(f32[33,8,128]{2,1,0:T(8,128)S(1)} %shard_map.69), channel_id=1, source_target_pairs={{0,64},{64,128},{128,192},{192,256},{256,320},{320,384},{384,448},... | collective-permute-start | bytes 405512 | tf_op jit(solution)/shard_map/ppermute | solution.py:513
  14.6 1.3 %collective-permute-start.3 = (f32[33,8,128]{2,1,0:T(8,128)S(1)}, f32[33,8,128]{2,1,0:T(8,128)S(1)}, u32[]{:S(2)}, u32[]{:S(2)}) collective-permute-start(f32[33,8,128]{2,1,0:T(8,128)S(1)} %shard_map.69), channel_id=1, source_target_pairs={{64,0},{128,64},{192,128},{256,192},{320,256},{384,320},{448,384},... | collective-permute-start | bytes 405512 | tf_op jit(solution)/shard_map/ppermute | solution.py:513
  15.9 0.7 collective-permute-done.2
  16.6 3.8 %collective-permute-done.3 = f32[33,8,128]{2,1,0:T(8,128)S(1)} collective-permute-done((f32[33,8,128]{2,1,0:T(8,128)S(1)}, f32[33,8,128]{2,1,0:T(8,128)S(1)}, u32[]{:S(2)}, u32[]{:S(2)}) %collective-permute-start.3) | collective-permute-done | bytes 135200 | tf_op jit(solution)/shard_map/ppermute | solution.py:513
  20.4 6.5 %collective-permute-start.5 = (f32[91,8,128]{2,1,0:T(8,128)S(1)}, f32[91,8,128]{2,1,0:T(8,128)S(1)}, u32[]{:S(2)}, u32[]{:S(2)}) collective-permute-start(f32[91,8,128]{2,1,0:T(8,128)S(1)} %slice_dynamic-update-slice_fusion.4.y_mid), channel_id=1, source_target_pairs={{0,60},{4,0},{8,4},{12,8},{16,12},{20,16},{24,20},{28,24},{32,28},... | collective-permute-start | bytes 1118216 | tf_op jit(solution)/shard_map/ppermute | solution.py:513
  27.0 0.0 collective-permute-start.4
  27.0 3.9 %collective-permute-done.5.y_hi = f32[91,8,128]{2,1,0:T(8,128)S(1)} collective-permute-done((f32[91,8,128]{2,1,0:T(8,128)S(1)}, f32[91,8,128]{2,1,0:T(8,128)S(1)}, u32[]{:S(2)}, u32[]{:S(2)}) %collective-permute-start.5) | collective-permute-done | bytes 372768 | tf_op jit(solution)/shard_map/ppermute | solution.py:513
  30.9 0.6 collective-permute-done.4.y_lo
  31.5 0.0 copy-start.1
  31.5 0.7 copy-done.1
  32.2 3.9 %shard_map.70 = (f32[6,24,24,256]{3,2,1,0:T(8,128)S(1)}, s32[24,24,256]{2,1,0:T(8,128)S(1)}, f32[64,2,128]{2,1,0:T(2,128)S(1)}, f32[24,8,128]{2,1,0:T(8,128)S(1)}, f32[4,8,128]{2,1,0:T(8,128)S(1)}) custom-call(f32[91,8,128]{2,1,0:T(8,128)S(1)} %collective-permute-done.4.y_lo, f32[91,8,128]{2,1,0:T(8,128)S(1)} %slice_dynamic-update-slice_fusion.4.y_mid, ...), custom_call_target="tpu_custom_call" | custom-call | tf_op jit(solution)/shard_map/pallas_call | solution.py:535
  36.0 29.7 %all_to_all.20.values.first = f32[64,2,128]{2,1,0:T(2,128)S(1)} all-to-all(f32[64,2,128]{2,1,0:T(2,128)S(1)} %get-tuple-element.15), channel_id=1, replica_groups=mesh['gx'=8,'gy'=16,'col'=4] {'gy','col'}, dimensions={0} | all-to-all | bytes 131072 | tf_op jit(solution)/shard_map/all_to_all | solution.py:547
  65.7 0.7 shard_map.71
  66.5 11.1 %all_to_all.21.parts = f32[8,16,128]{2,1,0:T(8,128)S(1)} all-to-all(f32[8,16,128]{2,1,0:T(8,128)S(1)} %shard_map.71), channel_id=1, replica_groups=mesh['gx'=8,'gy'=16,'col'=4] {'gx'}, dimensions={0} | all-to-all | bytes 131072 | tf_op jit(solution)/shard_map/all_to_all | solution.py:551
  77.6 6.3 %shard_map.72 = f32[64,4,128]{2,1,0:T(4,128)S(1)} custom-call(f32[8,16,128]{2,1,0:T(8,128)S(1)} %all_to_all.21.parts, f32[6,24,24,256]{3,2,1,0:T(8,128)S(1)} %get-tuple-element.16.weights, s32[24,24,256]{2,1,0:T(8,128)S(1)} %get-tuple-element.17.labels, f32[91,8,128]{2,1,0:T(8,128)S(1)} %collective-permute-done.4.y_lo, ...), custom_call_target="tpu_custom_call" | custom-call | tf_op jit(solution)/shard_map/pallas_call | solution.py:553
  84.0 18.2 %all_to_all.22.values = f32[64,4,128]{2,1,0:T(4,128)S(1)} all-to-all(f32[64,4,128]{2,1,0:T(4,128)S(1)} %shard_map.72), channel_id=1, replica_groups=mesh['gx'=8,'gy'=16,'col'=4] {'gy','col'}, dimensions={0} | all-to-all | bytes 262144 | tf_op jit(solution)/shard_map/all_to_all | solution.py:559
  102.2 1.1 shard_map.73
  103.3 7.7 %all_to_all.23.images = f32[8,24,128]{2,1,0:T(8,128)S(1)} all-to-all(f32[8,24,128]{2,1,0:T(8,128)S(1)} %shard_map.73), channel_id=1, replica_groups=mesh['gx'=8,'gy'=16,'col'=4] {'gx'}, dimensions={0} | all-to-all | bytes 196608 | tf_op jit(solution)/shard_map/all_to_all | solution.py:563
  111.0 3.0 %shard_map.74 = (f32[8,8,128]{2,1,0:T(8,128)}, f32[1,16]{1,0:T(1,128)}) custom-call(f32[8,16,128]{2,1,0:T(8,128)S(1)} %all_to_all.21.parts, f32[8,24,128]{2,1,0:T(8,128)S(1)} %all_to_all.23.images, f32[6,24,24,256]{3,2,1,0:T(8,128)S(1)} %get-tuple-element.16.weights, s32[24,24,256]{2,1,0:T(8,128)S(1)} %get-tuple-element.17.labels, ...), custom_call_target="tpu_custom_call" | custom-call | tf_op jit(solution)/shard_map/pallas_call | solution.py:564
  (7 shorter events, 0.1 us)
Async XLA Ops:
  2.2 7.0 %collective-permute-start = (f32[9,8,128]{2,1,0:T(8,128)}, f32[9,8,128]{2,1,0:T(8,128)S(1)}, u32[]{:S(2)}, u32[]{:S(2)}) collective-permute-start(f32[9,8,128]{2,1,0:T(8,128)} %get-tuple-element.12), channel_id=1, source_target_pairs={{1,0},{2,1},{3,2},{5,4},{6,5},{7,6},{9,8},{10,9},{11,10},{13,12},{... | collective-permute-start | bytes 110600 | tf_op jit(solution)/shard_map/ppermute | solution.py:513
  3.5 7.0 %collective-permute-start.1 = (f32[9,8,128]{2,1,0:T(8,128)}, f32[9,8,128]{2,1,0:T(8,128)S(1)}, u32[]{:S(2)}, u32[]{:S(2)}) collective-permute-start(f32[9,8,128]{2,1,0:T(8,128)} %get-tuple-element.13), channel_id=1, source_target_pairs={{0,1},{1,2},{2,3},{4,5},{5,6},{6,7},{8,9},{9,10},{10,11},{12,13},{... | collective-permute-start | bytes 110600 | tf_op jit(solution)/shard_map/ppermute | solution.py:513
  10.6 0.9 copy-start
  11.5 5.1 %collective-permute-start.2 = (f32[33,8,128]{2,1,0:T(8,128)S(1)}, f32[33,8,128]{2,1,0:T(8,128)S(1)}, u32[]{:S(2)}, u32[]{:S(2)}) collective-permute-start(f32[33,8,128]{2,1,0:T(8,128)S(1)} %shard_map.69), channel_id=1, source_target_pairs={{0,64},{64,128},{128,192},{192,256},{256,320},{320,384},{384,448},... | collective-permute-start | bytes 405512 | tf_op jit(solution)/shard_map/ppermute | solution.py:513
  14.6 5.8 %collective-permute-start.3 = (f32[33,8,128]{2,1,0:T(8,128)S(1)}, f32[33,8,128]{2,1,0:T(8,128)S(1)}, u32[]{:S(2)}, u32[]{:S(2)}) collective-permute-start(f32[33,8,128]{2,1,0:T(8,128)S(1)} %shard_map.69), channel_id=1, source_target_pairs={{64,0},{128,64},{192,128},{256,192},{320,256},{384,320},{448,384},... | collective-permute-start | bytes 405512 | tf_op jit(solution)/shard_map/ppermute | solution.py:513
  20.4 10.5 %collective-permute-start.5 = (f32[91,8,128]{2,1,0:T(8,128)S(1)}, f32[91,8,128]{2,1,0:T(8,128)S(1)}, u32[]{:S(2)}, u32[]{:S(2)}) collective-permute-start(f32[91,8,128]{2,1,0:T(8,128)S(1)} %slice_dynamic-update-slice_fusion.4.y_mid), channel_id=1, source_target_pairs={{0,60},{4,0},{8,4},{12,8},{16,12},{20,16},{24,20},{28,24},{32,28},... | collective-permute-start | bytes 1118216 | tf_op jit(solution)/shard_map/ppermute | solution.py:513
  27.0 4.5 %collective-permute-start.4 = (f32[91,8,128]{2,1,0:T(8,128)S(1)}, f32[91,8,128]{2,1,0:T(8,128)S(1)}, u32[]{:S(2)}, u32[]{:S(2)}) collective-permute-start(f32[91,8,128]{2,1,0:T(8,128)S(1)} %slice_dynamic-update-slice_fusion.4.y_mid), channel_id=1, source_target_pairs={{0,4},{4,8},{8,12},{12,16},{16,20},{20,24},{24,28},{28,32},{32,36}... | collective-permute-start | bytes 1118216 | tf_op jit(solution)/shard_map/ppermute | solution.py:513
  31.5 0.7 copy-start.1

commit v5 on v4

--- a/solution.py
+++ b/solution.py
@@ -16,16 +16,33 @@
 NP = 3 * B
 W = 9
 FULL = (NP, 2 * LZ)
+FILL_UNROLL = 8
 CHUNK = 12
 fine_relax = 0.6666667
 coarse_relax = 0.7
 VMEM_LIMIT = 48 * 1024 * 1024
 WHOLE_VMEM = 63 * 1024 * 1024
 
-PERM, OWN, HZ, ASG, SRC = 0, 8, 16, 24, 25
-STACK = 33
-HEAD = 25
-LINE = 3 * HEAD + 2 * B
+PERM, OWN, HZ, ASG, SRC = 0, 8, 16, 20, 21
+STACK = 29
+
+FOLDS = [(p, None, 0) for p in range(7, 17)]
+FOLDS += [(6, 0, 1), (5, 1, 2), (4, 2, 3), (17, 23, 1), (18, 22, 2), (19, 21, 3), (3, 20, 4)]
+FOLD_OF = {}
+for _at, (_main, _other, _rows) in enumerate(FOLDS):
+    FOLD_OF[_main] = (_at, 0)
+    if _other is not None:
+        FOLD_OF[_other] = (_at, _rows)
+N_FOLD = len(FOLDS)
+M_PERM, M_OWN, M_HZ, M_ASG, M_SRC = 0, N_FOLD, 2 * N_FOLD, 2 * N_FOLD + 12, 2 * N_FOLD + 13
+SRC_FOLDS = [(8 + q, ((12 + q, 4, 4),)) for q in range(4)]
+SRC_FOLDS += [(7, ((6, 2, 2), (5, 1, 3))), (16, ((17, 2, 2), (18, 1, 3)))]
+SRC_OF = {}
+for _at, (_main, _others) in enumerate(SRC_FOLDS):
+    SRC_OF[_main] = (_at, 0)
+    for _other, _rows, _top in _others:
+        SRC_OF[_other] = (_at, _top)
+MESSAGE = M_SRC + len(SRC_FOLDS)
 
 
 def lanes(shape):
@@ -40,7 +57,7 @@
     return jax.ShapeDtypeStruct(shape, dtype)
 
 
-def call(kernel, outs, n_in, scratch=(), space=pltpu.VMEM, limit=VMEM_LIMIT):
+def call(kernel, outs, n_in, scratch=(), space=pltpu.VMEM, limit=VMEM_LIMIT, cost=None):
     single = not isinstance(outs, (list, tuple))
     vm = pl.BlockSpec(memory_space=pltpu.VMEM)
     return pl.pallas_call(
@@ -50,6 +67,7 @@
         out_specs=vm if single else [vm] * len(outs),
         scratch_shapes=list(scratch),
         compiler_params=pltpu.CompilerParams(vmem_limit_bytes=limit),
+        cost_estimate=cost,
     )
 
 
@@ -57,12 +75,16 @@
     return jnp.broadcast_to(row, (B, LZ))
 
 
-def z_messages(perm_in, src_in, own_in, asg_in, flags_in, mr, ml, base, flags_out,
-               perm, src, own, asg, flags, sem):
+def asg_tile(asg):
+    tile = jnp.concatenate([asg[...].astype(f32), jnp.zeros((1, LZ - NSUB), f32)], axis=1)
+    return jnp.where(rows((B, LZ)) == 0, spread(tile), 0.0)
+
+
+def z_messages(perm_in, src_in, own_in, asg_in, mr, ml, perm, src, own, asg, sem):
     copies = [
         pltpu.make_async_copy(a, b, sem.at[i])
         for i, (a, b) in enumerate(
-            ((perm_in, perm), (src_in, src), (own_in, own), (asg_in, asg), (flags_in, flags))
+            ((perm_in, perm), (src_in, src), (own_in, own), (asg_in, asg))
         )
     ]
     for copy in copies:
@@ -70,21 +92,32 @@
     for copy in copies:
         copy.wait()
     lane = lanes((B, LZ))
-    tile = jnp.concatenate([asg[...].astype(f32), jnp.zeros((1, LZ - NSUB), f32)], axis=1)
-    tile = jnp.where(rows((B, LZ)) == 0, spread(tile), 0.0)
-    for p in range(B):
-        k, s, o = perm[p], src[p], own[p].astype(f32)
-        base[p], base[B + p], base[2 * B + p] = k, o, s
-        mr[p] = jnp.where(
-            lane < 16, k, jnp.where(lane < 32, pltpu.roll(o, 16, 1), pltpu.roll(s, 32, 1))
+
+    def first_cells(q):
+        k, s, o = perm[q], src[q], own[q].astype(f32)
+        return jnp.where(
+            lane < 9, k, jnp.where(lane < 18, pltpu.roll(o, 9, 1), pltpu.roll(s, 18, 1))
         )
-        ml[p] = jnp.where(
-            lane >= 112, k, jnp.where(lane >= 96, pltpu.roll(o, 112, 1), pltpu.roll(s, 96, 1))
+
+    def last_cells(q):
+        k, s, o = perm[q], src[q], own[q].astype(f32)
+        return jnp.where(
+            lane >= 55,
+            pltpu.roll(k, 64, 1),
+            jnp.where(lane >= 46, pltpu.roll(o, 55, 1), pltpu.roll(s, 46, 1)),
         )
-    base[3 * B] = tile
-    mr[B] = tile
-    ml[B] = tile
-    col, n_col = lax.axis_index("col"), flags_in.shape[0]
+
+    for out, cells in ((mr, first_cells), (ml, last_cells)):
+        for q in range(B // 2):
+            out[q] = jnp.where(lane < 64, cells(q), pltpu.roll(cells(q + B // 2), 64, 1))
+        out[B // 2] = asg_tile(asg)
+
+
+def own_stack(perm, src, own, asg, flags, base, flags_out):
+    for q in range(B):
+        base[q], base[B + q], base[2 * B + q] = perm[q], own[q].astype(f32), src[q]
+    base[3 * B] = asg_tile(asg)
+    col, n_col = lax.axis_index("col"), flags.shape[0]
     for i, at in enumerate((col - 1, col, col + 1)):
         at = jnp.clip(at, 0, n_col - 1)
         flags_out[pl.ds(i, 1), :] = flags[pl.ds(at, 1), :].astype(f32)
@@ -93,14 +126,54 @@
 def stack_up(base, mr, ml, stack):
     lane = lanes((B, LZ))
     row = rows((B, LZ))
-    for p in range(B):
-        stack[PERM + p] = base[p]
-        stack[OWN + p] = base[B + p]
-        stack[SRC + p] = base[2 * B + p]
-        stack[HZ + p] = jnp.where(lane < 64, mr[p], ml[p])
+    for q in range(B):
+        stack[PERM + q] = base[q]
+        stack[OWN + q] = base[B + q]
+        stack[SRC + q] = base[2 * B + q]
+    for q in range(B // 2):
+        stack[HZ + q] = jnp.where((lane & 63) < 32, mr[q], ml[q])
+    at = B // 2
     stack[ASG] = jnp.where(
-        row == 1, spread(mr[B, 0:1, :]), jnp.where(row == 2, spread(ml[B, 0:1, :]), base[3 * B])
-    )
+        row == 1, spread(mr[at, 0:1, :]), jnp.where(row == 2, spread(ml[at, 0:1, :]), base[3 * B])
+    )
+
+
+def y_messages(low, mid, high, up, down):
+    stacks = (low, mid, high)
+    row = rows((B, LZ))
+    lane = lanes((B, LZ))
+
+    def fold(main, other, n, top, upward):
+        if upward:
+            return jnp.where((row >= top - n) & (row < top), pltpu.roll(other, top, 0), main)
+        return jnp.where(
+            (row >= B - top) & (row < B - top + n), pltpu.roll(other, B - top, 0), main
+        )
+
+    for out, upward in ((up, True), (down, False)):
+        for field, first in ((PERM, M_PERM), (OWN, M_OWN)):
+            for at, (main, other, n) in enumerate(FOLDS):
+                tile = stacks[main // B][field + main % B]
+                if other is not None:
+                    tile = fold(tile, stacks[other // B][field + other % B], n, n, upward)
+                out[first + at] = tile
+        for b in range(3):
+            for q in range(B // 2):
+                out[M_HZ + 4 * b + q] = stacks[b][HZ + q]
+        for at, (main, others) in enumerate(SRC_FOLDS):
+            tile = stacks[main // B][SRC + main % B]
+            for other, n, top in others:
+                tile = fold(tile, stacks[other // B][SRC + other % B], n, top, upward)
+            out[M_SRC + at] = tile
+        sides = jnp.where(lane < NSUB, low[ASG], pltpu.roll(high[ASG], NSUB, 1))
+        out[M_ASG] = jnp.where(row < 3, sides, pltpu.roll(mid[ASG], 3, 0))
+
+
+def line_asg(stacks, below, above, ty, b):
+    if ty == 1:
+        return stacks[b][ASG]
+    tile = (below if ty == 0 else above)[M_ASG]
+    return (tile, pltpu.roll(tile, 5, 0), pltpu.roll(tile, NSUB, 1))[b]
 
 
 def around(u_ref, w_ref, p):
@@ -169,32 +242,72 @@
     return tile
 
 
-def first_sums(n_gx, n_gy, n_col, y_lo, y_mid, y_hi, flags,
-               weights, labels, chunk, dvals, paths, kext, fx, both, masks, sums):
+def positive(t):
+    return jnp.where(t > 0.0, t, 1.0)
+
+
+def near_and_far(tile, q):
+    turned = pltpu.roll(tile, 64, 1)
+    return jnp.where(q < 4, tile, turned), jnp.where(q < 4, turned, tile)
+
+
+def halo_values(near, far):
+    lane = lanes((B, LZ))
+    near_side = lane < 64
+    halo = (lane < W) | (lane >= LZ - W)
+    source_halo = (lane < 4) | (lane >= LZ - 4)
+    k = positive(jnp.where(halo, jnp.where(near_side, near, far), 1.0))
+    own = jnp.where(near_side, pltpu.roll(near, LZ - 9, 1), pltpu.roll(near, 73, 1))
+    src = jnp.where(near_side, pltpu.roll(near, LZ - 18, 1), pltpu.roll(near, 82, 1))
+    return k, jnp.where(halo, own, 0.0).astype(i32), jnp.where(source_halo, src, 0.0)
+
+
+def own_rows(low, mid, high, kmid, lmid, smid):
+    for p in range(NP):
+        stack, q = (low, mid, high)[p // B], p % B
+        k, label, src = halo_values(*near_and_far(stack[HZ + q % 4], q))
+        kmid[p, :, 0:LZ] = positive(stack[PERM + q])
+        kmid[p, :, LZ:] = k
+        lmid[p, :, 0:LZ] = stack[OWN + q].astype(i32)
+        lmid[p, :, LZ:] = label
+        if 4 <= p < 20:
+            smid[p - 4, :, 0:LZ] = stack[SRC + q]
+            smid[p - 4, :, LZ:] = src
+
+
+def first_sums(n_gx, n_gy, n_col, low, mid, high, below, above, flags, kmid, lmid, smid,
+               weights, labels, chunk, dvals, paths, asg, kext, fx, both, masks, sums):
     gx, gy, col = (lax.axis_index(a) for a in ("gx", "gy", "col"))
-    lines = (y_lo, y_mid, y_hi)
+    mids = (low, mid, high)
     lane = lanes((B, LZ))
     row = rows((B, LZ))
-    halo = (lane < W) | (lane >= LZ - W)
-    near_side = lane < 64
-
-    def positive(t):
-        return jnp.where(t > 0.0, t, 1.0)
+    def unfolded(ty, first, place):
+        at, n = place
+        tile = (below if ty == 0 else above)[first + at]
+        return pltpu.roll(tile, (B - n if ty == 0 else n) % B, 0) if n else tile
+
+    def beyond(ty, p):
+        b, q = p // B, lax.rem(p, B)
+        tile = (below if ty == 0 else above)[M_HZ + 4 * b + lax.rem(q, 4)]
+        return halo_values(*near_and_far(tile, q))
 
     def fill(p, carry):
-        at = HEAD * (p // B) + lax.rem(p, B)
+        kext[p + 1, B : 2 * B, :] = kmid[p]
+        labels[p, B : 2 * B, :] = lmid[p]
+        for ty in (0, 2):
+            r = slice(ty * B, (ty + 1) * B)
+            kext[p + 1, r, LZ:], labels[p, r, LZ:], _ = beyond(ty, p)
+        return carry
+
+    lax.fori_loop(0, NP, fill, 0, unroll=FILL_UNROLL)
+    for p in range(NP):
+        for ty in (0, 2):
+            r = slice(ty * B, (ty + 1) * B)
+            kext[p + 1, r, 0:LZ] = positive(unfolded(ty, M_PERM, FOLD_OF[p]))
+            labels[p, r, 0:LZ] = unfolded(ty, M_OWN, FOLD_OF[p]).astype(i32)
+    for b in range(3):
         for ty in range(3):
-            line = lines[ty]
-            r = slice(ty * B, (ty + 1) * B)
-            packed = line[at + HZ]
-            kext[p + 1, r, 0:LZ] = positive(line[at + PERM])
-            kext[p + 1, r, LZ:] = positive(jnp.where(halo, packed, 1.0))
-            labels[p, r, 0:LZ] = line[at + OWN].astype(i32)
-            own_z = jnp.where(near_side, pltpu.roll(packed, LZ - 16, 1), pltpu.roll(packed, 16, 1))
-            labels[p, r, LZ:] = jnp.where(halo, own_z, 0.0).astype(i32)
-        return carry
-
-    lax.fori_loop(0, NP, fill, 0, unroll=8)
+            asg[b, ty] = line_asg(mids, below, above, ty, b).astype(i32)
     kext[0] = jnp.ones(FULL, f32)
     kext[NP + 1] = jnp.ones(FULL, f32)
 
@@ -240,20 +353,26 @@
 
     lax.fori_loop(0, NP, terms, 0, unroll=8)
 
+
     def start(i, carry):
         p = i + B // 2
-        packed_at = HEAD * (p // B) + HZ + lax.rem(p, B)
-        for ty in range(3):
-            line = lines[ty]
+        over = both[0, p + 1] * (1.0 / fine_relax)
+        both[1, p + 1, B : 2 * B, :] = smid[i] * over[B : 2 * B]
+        for ty in (0, 2):
             r = slice(ty * B, (ty + 1) * B)
-            packed = line[packed_at]
-            src_z = jnp.where(near_side, pltpu.roll(packed, LZ - 32, 1), pltpu.roll(packed, 32, 1))
-            over = both[0, p + 1, r, :] * (1.0 / fine_relax)
-            both[1, p + 1, r, 0:LZ] = line[3 * HEAD + i] * over[:, 0:LZ]
-            both[1, p + 1, r, LZ:] = jnp.where(halo, src_z, 0.0) * over[:, LZ:]
+            both[1, p + 1, r, LZ:] = beyond(ty, p)[2] * over[r, LZ:]
         return carry
 
     lax.fori_loop(0, 2 * B, start, 0, unroll=8)
+    for p in range(B // 2, NP - B // 2):
+        for ty in (0, 2):
+            r = slice(ty * B, (ty + 1) * B)
+            if p in SRC_OF:
+                over = both[0, p + 1, r, 0:LZ] * (1.0 / fine_relax)
+                both[1, p + 1, r, 0:LZ] = unfolded(ty, M_SRC, SRC_OF[p]) * over
+            else:
+                both[1, p + 1, r, 0:LZ] = jnp.zeros((B, LZ), f32)
+
     r = slice(B, 2 * B)
     for q in range(B):
         p = B + q
@@ -277,7 +396,7 @@
     label_sums([(0, label_tiles, (tiles, diag_tiles))], sums)
     totals = lane_sums(sums[...])
 
-    own = spread(y_mid[HEAD + ASG, 0:1, :])
+    own = spread(mid[ASG, 0:1, :])
     own = jnp.where(lane < NSUB, own, pltpu.roll(own, NSUB, 1))
     tile = jnp.where(row == 0, totals, own)[0:2]
     for d in range(n_gy * n_col):
@@ -397,15 +516,15 @@
     return rhs, diag, coarse_relax * rhs / diag
 
 
-def expand(coarse, lines, labels, u, tables, first, last):
+def expand(coarse, asg, labels, u, tables, first, last):
     near_side = lanes((B, LZ)) < 64
 
-    def table(b, carry):
-        for ty in range(3):
-            tables[b, ty] = lookup(coarse[b], lines[ty][HEAD * b + ASG].astype(i32))
+    def table(i, carry):
+        b, ty = i // 3, lax.rem(i, 3)
+        tables[b, ty] = lookup(coarse[b], asg[b, ty])
         return carry
 
-    lax.fori_loop(0, 3, table, 0)
+    lax.fori_loop(0, 9, table, 0, unroll=3)
 
     def one(p, carry):
         b = p // B
@@ -420,14 +539,14 @@
     lax.fori_loop(first, last + 1, one, 0, unroll=8)
 
 
-def second_sums(n_gx, n_gy, n_col, parts, weights, labels, y_lo, y_mid, y_hi, dvals, paths,
+def second_sums(n_gx, n_gy, n_col, parts, weights, labels, asg, dvals, paths,
                 chunk, both, coarse, tables, ends, sums):
     gx = lax.axis_index("gx")
     row = rows((B, LZ))
     r = slice(B, 2 * B)
     for i in range(3):
         coarse[i] = guess(parts, gx + i - 1, n_gx)[2]
-    expand(coarse, (y_lo, y_mid, y_hi), labels, both.at[0], tables, 0, NP - 1)
+    expand(coarse, asg, labels, both.at[0], tables, 0, NP - 1)
 
     def after(k):
         @pl.when(k == 0)
@@ -460,18 +579,18 @@
     sums[NSUB : 2 * NSUB, :] = jnp.zeros((NSUB, LZ), f32)
     label_sums(groups, sums)
     totals = lane_sums(sums[...])
-    right, left = (spread(y_mid[HEAD * b + ASG, 0:1, :]) for b in (2, 0))
-    asg = jnp.where(lanes((B, LZ)) < NSUB, right, pltpu.roll(left, NSUB, 1))
+    right, left = (spread(asg[b, 1, 0:1, :].astype(f32)) for b in (2, 0))
+    sides = jnp.where(lanes((B, LZ)) < NSUB, right, pltpu.roll(left, NSUB, 1))
     tile = jnp.where(
         row < 2,
         jnp.where(row == 0, totals[:, 0:LZ], totals[:, LZ : 2 * LZ]),
-        jnp.where(row == 2, totals[:, 2 * LZ :], asg),
+        jnp.where(row == 2, totals[:, 2 * LZ :], sides),
     )[0:4]
     for d in range(n_gy * n_col):
         chunk[d] = tile
 
 
-def last_sweeps(n_gx, n_gy, n_col, parts, images, weights, labels, y_lo, y_mid, y_hi,
+def last_sweeps(n_gx, n_gy, n_col, parts, images, weights, labels, asg,
                 pressure, coarse_out, both, coarse, tables):
     gx, gy, col = (lax.axis_index(a) for a in ("gx", "gy", "col"))
     for i in range(3):
@@ -490,7 +609,7 @@
     row = coarse[1, pl.ds(mine // per_row, 1), :]
     turned = pltpu.roll(spread(row), lax.rem(LZ - lax.rem(mine, per_row) * share, LZ), 1)
     coarse_out[...] = turned[0:1, 0:share]
-    expand(coarse, (y_lo, y_mid, y_hi), labels, both.at[1], tables, 4, 19)
+    expand(coarse, asg, labels, both.at[1], tables, 4, 19)
     sweeps(both, weights, 5, 8)
     for q in range(B):
         pressure[q] = both[1, B + 1 + q, B : 2 * B, 0:LZ]
@@ -512,38 +631,48 @@
     def send(x, axis, by, wrap=False):
         return lax.ppermute(x, axis, steps(lax.axis_size(axis), by, wrap))
 
-    mr, ml, base, flags = call(
+    assigned, flags = assignment.reshape(1, NSUB), layer_flags.reshape(n_col, LZ)
+    mr, ml = call(
         z_messages,
-        [sds(B + 1, B, LZ)] * 2 + [sds(3 * B + 1, B, LZ), sds(3, LZ)],
-        5,
+        [sds(B // 2 + 1, B, LZ)] * 2,
+        4,
         scratch=[
             vm(plane, f32), vm(plane, f32), vm(plane, i32), vm((1, NSUB), i32),
-            vm((n_col, LZ), i32), pltpu.SemaphoreType.DMA((5,)),
+            pltpu.SemaphoreType.DMA((4,)),
         ],
         space=pl.ANY,
         limit=WHOLE_VMEM,
-    )(permeability, source, ownership, assignment.reshape(1, NSUB), layer_flags.reshape(n_col, LZ))
+    )(permeability, source, ownership, assigned)
     mr, ml = send(mr, "col", -1), send(ml, "col", 1)
-    stack = call(stack_up, sds(STACK, B, LZ), 3)(base, mr, ml)
-    low, high = send(stack, "gx", 1), send(stack, "gx", -1)
-    line = jnp.concatenate(
-        [low[:HEAD], stack[:HEAD], high[:HEAD], low[SRC + 4 :], stack[SRC:], high[SRC : SRC + 4]],
-        axis=0,
-    )
-    y_lo, y_hi = send(line, "gy", 1, True), send(line, "gy", -1, True)
-
-    weights, labels, chunk, dvals, paths = call(
+    base, flags = call(
+        own_stack,
+        [sds(3 * B + 1, B, LZ), sds(3, LZ)],
+        5,
+        cost=pl.CostEstimate(flops=100000, bytes_accessed=300000, transcendentals=0),
+    )(permeability, source, ownership, assigned, flags)
+    mid = call(stack_up, sds(STACK, B, LZ), 3)(base, mr, ml)
+    low, high = send(mid, "gx", 1), send(mid, "gx", -1)
+    up, down = call(y_messages, [sds(MESSAGE, B, LZ)] * 2, 3)(low, mid, high)
+    below, above = send(up, "gy", 1, True), send(down, "gy", -1, True)
+    middle = call(
+        own_rows,
+        [sds(NP, B, 2 * LZ), sds(NP, B, 2 * LZ, dtype=i32), sds(2 * B, B, 2 * LZ)],
+        3,
+        cost=pl.CostEstimate(flops=1000000, bytes_accessed=1000000, transcendentals=0),
+    )(low, mid, high)
+
+    weights, labels, chunk, dvals, paths, asg = call(
         functools.partial(first_sums, *sizes),
         [
             sds(6, NP, *FULL), sds(NP, *FULL, dtype=i32), sds(n_bricks, 2, LZ), sds(NP, B, LZ),
-            sds(4, B, LZ),
+            sds(4, B, LZ), sds(3, 3, B, LZ, dtype=i32),
         ],
-        4,
+        9,
         scratch=[
             vm((NP + 2, *FULL), f32), vm((NP + 1, *FULL), f32), fields, vm((2, *FULL), f32),
             vm((2 * NSUB, LZ), f32),
         ],
-    )(y_lo, line, y_hi, flags)
+    )(low, mid, high, below, above, flags, *middle)
     bricks = lax.all_to_all(chunk, ("gy", "col"), 0, 0, tiled=True)
     parts = call(
         functools.partial(first_coarse, n_bricks, n_gx), sds(n_gx, 2 * B, LZ), 1
@@ -553,9 +682,9 @@
     chunk = call(
         functools.partial(second_sums, *sizes),
         sds(n_bricks, 4, LZ),
-        8,
+        6,
         scratch=[fields, *tables, vm((4, B, LZ), f32), vm((6 * NSUB, LZ), f32)],
-    )(parts, weights, labels, y_lo, line, y_hi, dvals, paths)
+    )(parts, weights, labels, asg, dvals, paths)
     images = lax.all_to_all(chunk, ("gy", "col"), 0, 0, tiled=True)
     images = call(
         functools.partial(second_coarse, n_gy, n_col, n_gx), sds(n_gx, 3 * B, LZ), 2
@@ -564,9 +693,9 @@
     return call(
         functools.partial(last_sweeps, *sizes),
         [sds(*plane), sds(1, B * LZ // (n_gy * n_col))],
-        7,
+        5,
         scratch=[fields, *tables],
-    )(parts, images, weights, labels, y_lo, line, y_hi)
+    )(parts, images, weights, labels, asg)
 
 
 def solution(mesh):

time: 115 us -> 112 us (0.974)
  waiting for transfers between devices: 10.3 us -> 3.51 us
  starting transfers between devices: 17.9 us -> 20 us
  local copies, waits for them, and re-layouts: 1.61 us -> 3.6 us
    ppermute x6, waiting for transfers between devices: 10.3 us -> 3.51 us  [send(): return lax.ppermute(x, axis, steps(lax.axis_size(axis), by, wrap))]
    all_to_all x1, blocking collectives: 29.7 us -> 27 us  [on_device(): bricks = lax.all_to_all(chunk, ('gy', 'col'), 0, 0, tiled=True)]
    ppermute x6, starting transfers between devices: 17.9 us -> 20 us  [send(): return lax.ppermute(x, axis, steps(lax.axis_size(axis), by, wrap))]
    unnamed x9 -> x10, local copies, waits for them, and re-layouts: 1.61 us -> 3.6 us
    all_to_all x1, blocking collectives: 11.1 us -> 12.7 us  [on_device(): parts = lax.all_to_all(parts, 'gx', 0, 0, tiled=True)]
    pallas_call x3 -> x6, Pallas kernels: 7.94 us -> 8.24 us  [the longest x1 6.34 us: on_device(): call(functools.partial(second_sums, *sizes), sds(n_bricks, 4, LZ), 6, scr...]
  transfers between devices with their start and end apart: 6 -> 6, of which waited for: 5 -> 4; matrix products, arithmetic and copies ran while one was open for 0% -> 0% of each run, Pallas kernels for 0% -> 0%
where the time goes in v5:
time: 112 us; the launch traced here: 111 us
  blocking collectives  65.6 us (59%)
  starting transfers between devices  20 us (18%)
  Pallas kernels  17.3 us (15%)
  local copies, waits for them, and re-layouts  3.6 us (3%)
  waiting for transfers between devices  3.51 us (3%)
    all_to_all x1, blocking collectives, on_device(): bricks = lax.all_to_all(chunk, ('gy', 'col'), 0, 0, tiled=True)  27 us
    ppermute x6, starting transfers between devices, send(): return lax.ppermute(x, axis, steps(lax.axis_size(axis), by, wrap))  20 us
    all_to_all x1, blocking collectives, on_device(): images = lax.all_to_all(chunk, ('gy', 'col'), 0, 0, tiled=True)  18.2 us
    all_to_all x1, blocking collectives, on_device(): parts = lax.all_to_all(parts, 'gx', 0, 0, tiled=True)  12.7 us
    all_to_all x1, blocking collectives, on_device(): images = lax.all_to_all(images, 'gx', 0, 0, tiled=True)  7.68 us
    pallas_call x1, Pallas kernels, on_device(): call(functools.partial(second_sums, *sizes), sds(n_bricks, 4, LZ), 6, scr...  6.34 us
    pallas_call x1, Pallas kernels, on_device(): call(functools.partial(first_sums, *sizes), [sds(6, NP, *FULL), sds(NP, *...  4.23 us
    unnamed x10, local copies, waits for them, and re-layouts  3.6 us
  transfers between devices with their start and end apart: 6, of which 4 were waited for; matrix products, arithmetic and copies ran while one was open for 0% of the time, Pallas kernels for 0%

profile of v5, /device:TPU:1, one launch (start us, length us, event | category | flops | bytes accessed | tf_op | source)
XLA Modules:
  0.0 110.8 jit_solution(6520037256686848741)
XLA Ops:
  0.6 1.6 %shard_map.69 = (f32[5,8,128]{2,1,0:T(8,128)}, f32[5,8,128]{2,1,0:T(8,128)}) custom-call(f32[8,8,128]{2,1,0:T(8,128)} %perm_in.1, f32[8,8,128]{2,1,0:T(8,128)} %src_in.1, s32[8,8,128]{2,1,0:T(8,128)} %own_in.1, s32[1,64]{1,0:T(1,128)} %bitcast.2), custom_call_target="tpu_custom_call" | custom-call | tf_op jit(solution)/shard_map/pallas_call | solution.py:635
  2.2 1.3 %collective-permute-start = (f32[5,8,128]{2,1,0:T(8,128)}, f32[5,8,128]{2,1,0:T(8,128)S(1)}, u32[]{:S(2)}, u32[]{:S(2)}) collective-permute-start(f32[5,8,128]{2,1,0:T(8,128)} %get-tuple-element.18), channel_id=1, source_target_pairs={{1,0},{2,1},{3,2},{5,4},{6,5},{7,6},{9,8},{10,9},{11,10},{13,12},{... | collective-permute-start | bytes 61448 | tf_op jit(solution)/shard_map/ppermute | solution.py:632
  3.5 5.7 %collective-permute-start.1 = (f32[5,8,128]{2,1,0:T(8,128)}, f32[5,8,128]{2,1,0:T(8,128)S(1)}, u32[]{:S(2)}, u32[]{:S(2)}) collective-permute-start(f32[5,8,128]{2,1,0:T(8,128)} %get-tuple-element.19), channel_id=1, source_target_pairs={{0,1},{1,2},{2,3},{4,5},{5,6},{6,7},{8,9},{9,10},{10,11},{12,13},{... | collective-permute-start | bytes 61448 | tf_op jit(solution)/shard_map/ppermute | solution.py:632
  9.2 0.0 copy-start
  9.2 0.7 copy-done
  10.0 0.0 copy-start.1
  10.0 0.8 copy-done.1
  10.7 0.0 copy-start.2
  10.7 0.8 copy-done.2
  11.5 0.0 copy-start.3
  11.5 0.7 copy-done.3
  12.1 0.0 copy-start.4
  12.1 0.7 copy-done.4
  12.8 0.0 collective-permute-done.mr
  12.8 0.0 collective-permute-done.1.ml
  12.9 1.3 %collective-permute-start.3 = (f32[29,8,128]{2,1,0:T(8,128)S(1)}, f32[29,8,128]{2,1,0:T(8,128)S(1)}, u32[]{:S(2)}, u32[]{:S(2)}) collective-permute-start(f32[29,8,128]{2,1,0:T(8,128)S(1)} %shard_map.70.mid), channel_id=1, source_target_pairs={{64,0},{128,64},{192,128},{256,192},{320,256},{384,320},{448,384},... | collective-permute-start | bytes 356360 | tf_op jit(solution)/shard_map/ppermute | solution.py:632
  14.2 4.0 %collective-permute-start.2 = (f32[29,8,128]{2,1,0:T(8,128)S(1)}, f32[29,8,128]{2,1,0:T(8,128)S(1)}, u32[]{:S(2)}, u32[]{:S(2)}) collective-permute-start(f32[29,8,128]{2,1,0:T(8,128)S(1)} %shard_map.70.mid), channel_id=1, source_target_pairs={{0,64},{64,128},{128,192},{192,256},{256,320},{320,384},{384,448},... | collective-permute-start | bytes 356360 | tf_op jit(solution)/shard_map/ppermute | solution.py:632
  18.2 0.3 collective-permute-done.3.high
  18.5 1.5 %collective-permute-done.2.low = f32[29,8,128]{2,1,0:T(8,128)S(1)} collective-permute-done((f32[29,8,128]{2,1,0:T(8,128)S(1)}, f32[29,8,128]{2,1,0:T(8,128)S(1)}, u32[]{:S(2)}, u32[]{:S(2)}) %collective-permute-start.2) | collective-permute-done | bytes 118816 | tf_op jit(solution)/shard_map/ppermute | solution.py:632
  20.0 0.1 shard_map.71
  20.1 4.4 %collective-permute-start.4 = (f32[53,8,128]{2,1,0:T(8,128)S(1)}, f32[53,8,128]{2,1,0:T(8,128)S(1)}, u32[]{:S(2)}, u32[]{:S(2)}) collective-permute-start(f32[53,8,128]{2,1,0:T(8,128)S(1)} %get-tuple-element.20), channel_id=1, source_target_pairs={{0,4},{4,8},{8,12},{12,16},{16,20},{20,24},{24,28},{28,32},{32,36}... | collective-permute-start | bytes 651272 | tf_op jit(solution)/shard_map/ppermute | solution.py:632
  24.4 3.4 %collective-permute-start.5 = (f32[53,8,128]{2,1,0:T(8,128)S(1)}, f32[53,8,128]{2,1,0:T(8,128)S(1)}, u32[]{:S(2)}, u32[]{:S(2)}) collective-permute-start(f32[53,8,128]{2,1,0:T(8,128)S(1)} %get-tuple-element.21), channel_id=1, source_target_pairs={{0,60},{4,0},{8,4},{12,8},{16,12},{20,16},{24,20},{28,24},{32,28},... | collective-permute-start | bytes 651272 | tf_op jit(solution)/shard_map/ppermute | solution.py:632
  27.8 0.2 shard_map.72
  28.1 0.7 collective-permute-done.4.below
  28.8 1.0 collective-permute-done.5.above
  29.8 4.2 %shard_map.73 = (f32[6,24,24,256]{3,2,1,0:T(8,128)S(1)}, s32[24,24,256]{2,1,0:T(8,128)S(1)}, f32[64,2,128]{2,1,0:T(2,128)S(1)}, f32[24,8,128]{2,1,0:T(8,128)S(1)...) custom-call(f32[29,8,128]{2,1,0:T(8,128)S(1)} %collective-permute-done.2.low, f32[29,8,128]{2,1,0:T(8,128)S(1)} %shard_map.70.mid, ...), custom_call_target="tpu_custom_call" | custom-call | tf_op jit(solution)/shard_map/pallas_call | solution.py:664
  34.0 27.0 %all_to_all.20.values.first = f32[64,2,128]{2,1,0:T(2,128)S(1)} all-to-all(f32[64,2,128]{2,1,0:T(2,128)S(1)} %get-tuple-element.26), channel_id=1, replica_groups=mesh['gx'=8,'gy'=16,'col'=4] {'gy','col'}, dimensions={0} | all-to-all | bytes 131072 | tf_op jit(solution)/shard_map/all_to_all | solution.py:676
  61.0 0.7 shard_map.74
  61.8 12.7 %all_to_all.21.parts = f32[8,16,128]{2,1,0:T(8,128)S(1)} all-to-all(f32[8,16,128]{2,1,0:T(8,128)S(1)} %shard_map.74), channel_id=1, replica_groups=mesh['gx'=8,'gy'=16,'col'=4] {'gx'}, dimensions={0} | all-to-all | bytes 131072 | tf_op jit(solution)/shard_map/all_to_all | solution.py:680
  74.5 6.3 %shard_map.75 = f32[64,4,128]{2,1,0:T(4,128)S(1)} custom-call(f32[8,16,128]{2,1,0:T(8,128)S(1)} %all_to_all.21.parts, f32[6,24,24,256]{3,2,1,0:T(8,128)S(1)} %get-tuple-element.27.weights, s32[24,24,256]{2,1,0:T(8,128)S(1)} %get-tuple-element.28.labels, s32[3,3,8,128]{3,2,1,0:T(8,128)S(1)} %get-tuple-element.29.asg, ...), custom_call_target="tpu_custom_call" | custom-call | tf_op jit(solution)/shard_map/pallas_call | solution.py:682
  80.9 18.2 %all_to_all.22.values = f32[64,4,128]{2,1,0:T(4,128)S(1)} all-to-all(f32[64,4,128]{2,1,0:T(4,128)S(1)} %shard_map.75), channel_id=1, replica_groups=mesh['gx'=8,'gy'=16,'col'=4] {'gy','col'}, dimensions={0} | all-to-all | bytes 262144 | tf_op jit(solution)/shard_map/all_to_all | solution.py:688
  99.1 1.1 shard_map.76
  100.1 7.7 %all_to_all.23.images = f32[8,24,128]{2,1,0:T(8,128)S(1)} all-to-all(f32[8,24,128]{2,1,0:T(8,128)S(1)} %shard_map.76), channel_id=1, replica_groups=mesh['gx'=8,'gy'=16,'col'=4] {'gx'}, dimensions={0} | all-to-all | bytes 196608 | tf_op jit(solution)/shard_map/all_to_all | solution.py:692
  107.8 3.0 %shard_map.77 = (f32[8,8,128]{2,1,0:T(8,128)}, f32[1,16]{1,0:T(1,128)}) custom-call(f32[8,16,128]{2,1,0:T(8,128)S(1)} %all_to_all.21.parts, f32[8,24,128]{2,1,0:T(8,128)S(1)} %all_to_all.23.images, f32[6,24,24,256]{3,2,1,0:T(8,128)S(1)} %get-tuple-element.27.weights, s32[24,24,256]{2,1,0:T(8,128)S(1)} %get-tuple-element.28.labels, ...), custom_call_target="tpu_custom_call" | custom-call | tf_op jit(solution)/shard_map/pallas_call | solution.py:693
  (2 shorter events, 0.0 us)
Async XLA Ops:
  2.2 10.6 %collective-permute-start = (f32[5,8,128]{2,1,0:T(8,128)}, f32[5,8,128]{2,1,0:T(8,128)S(1)}, u32[]{:S(2)}, u32[]{:S(2)}) collective-permute-start(f32[5,8,128]{2,1,0:T(8,128)} %get-tuple-element.18), channel_id=1, source_target_pairs={{1,0},{2,1},{3,2},{5,4},{6,5},{7,6},{9,8},{10,9},{11,10},{13,12},{... | collective-permute-start | bytes 61448 | tf_op jit(solution)/shard_map/ppermute | solution.py:632
  3.5 9.3 %collective-permute-start.1 = (f32[5,8,128]{2,1,0:T(8,128)}, f32[5,8,128]{2,1,0:T(8,128)S(1)}, u32[]{:S(2)}, u32[]{:S(2)}) collective-permute-start(f32[5,8,128]{2,1,0:T(8,128)} %get-tuple-element.19), channel_id=1, source_target_pairs={{0,1},{1,2},{2,3},{4,5},{5,6},{6,7},{8,9},{9,10},{10,11},{12,13},{... | collective-permute-start | bytes 61448 | tf_op jit(solution)/shard_map/ppermute | solution.py:632
  9.2 0.8 copy-start
  10.0 0.8 copy-start.1
  10.7 0.8 copy-start.2
  11.5 0.7 copy-start.3
  12.1 0.7 copy-start.4
  12.9 5.6 %collective-permute-start.3 = (f32[29,8,128]{2,1,0:T(8,128)S(1)}, f32[29,8,128]{2,1,0:T(8,128)S(1)}, u32[]{:S(2)}, u32[]{:S(2)}) collective-permute-start(f32[29,8,128]{2,1,0:T(8,128)S(1)} %shard_map.70.mid), channel_id=1, source_target_pairs={{64,0},{128,64},{192,128},{256,192},{320,256},{384,320},{448,384},... | collective-permute-start | bytes 356360 | tf_op jit(solution)/shard_map/ppermute | solution.py:632
  14.2 5.8 %collective-permute-start.2 = (f32[29,8,128]{2,1,0:T(8,128)S(1)}, f32[29,8,128]{2,1,0:T(8,128)S(1)}, u32[]{:S(2)}, u32[]{:S(2)}) collective-permute-start(f32[29,8,128]{2,1,0:T(8,128)S(1)} %shard_map.70.mid), channel_id=1, source_target_pairs={{0,64},{64,128},{128,192},{192,256},{256,320},{320,384},{384,448},... | collective-permute-start | bytes 356360 | tf_op jit(solution)/shard_map/ppermute | solution.py:632
  20.1 8.8 %collective-permute-start.4 = (f32[53,8,128]{2,1,0:T(8,128)S(1)}, f32[53,8,128]{2,1,0:T(8,128)S(1)}, u32[]{:S(2)}, u32[]{:S(2)}) collective-permute-start(f32[53,8,128]{2,1,0:T(8,128)S(1)} %get-tuple-element.20), channel_id=1, source_target_pairs={{0,4},{4,8},{8,12},{12,16},{16,20},{20,24},{24,28},{28,32},{32,36}... | collective-permute-start | bytes 651272 | tf_op jit(solution)/shard_map/ppermute | solution.py:632
  24.4 5.3 %collective-permute-start.5 = (f32[53,8,128]{2,1,0:T(8,128)S(1)}, f32[53,8,128]{2,1,0:T(8,128)S(1)}, u32[]{:S(2)}, u32[]{:S(2)}) collective-permute-start(f32[53,8,128]{2,1,0:T(8,128)S(1)} %get-tuple-element.21), channel_id=1, source_target_pairs={{0,60},{4,0},{8,4},{12,8},{16,12},{20,16},{24,20},{28,24},{32,28},... | collective-permute-start | bytes 651272 | tf_op jit(solution)/shard_map/ppermute | solution.py:632

commit v6 on v5

--- a/solution.py
+++ b/solution.py
@@ -25,6 +25,7 @@
 
 PERM, OWN, HZ, ASG, SRC = 0, 8, 16, 20, 21
 STACK = 29
+X_MESSAGE = 25
 
 FOLDS = [(p, None, 0) for p in range(7, 17)]
 FOLDS += [(6, 0, 1), (5, 1, 2), (4, 2, 3), (17, 23, 1), (18, 22, 2), (19, 21, 3), (3, 20, 4)]
@@ -57,6 +58,10 @@
     return jax.ShapeDtypeStruct(shape, dtype)
 
 
+def pinned(*shape):
+    return pltpu.VMEM(shape, f32)
+
+
 def call(kernel, outs, n_in, scratch=(), space=pltpu.VMEM, limit=VMEM_LIMIT, cost=None):
     single = not isinstance(outs, (list, tuple))
     vm = pl.BlockSpec(memory_space=pltpu.VMEM)
@@ -80,11 +85,12 @@
     return jnp.where(rows((B, LZ)) == 0, spread(tile), 0.0)
 
 
-def z_messages(perm_in, src_in, own_in, asg_in, mr, ml, perm, src, own, asg, sem):
+def z_messages(perm_in, src_in, own_in, asg_in, flags_in, mr, ml, base, flags_out,
+               perm, src, own, asg, flags, sem):
     copies = [
         pltpu.make_async_copy(a, b, sem.at[i])
         for i, (a, b) in enumerate(
-            ((perm_in, perm), (src_in, src), (own_in, own), (asg_in, asg))
+            ((perm_in, perm), (src_in, src), (own_in, own), (asg_in, asg), (flags_in, flags))
         )
     ]
     for copy in copies:
@@ -111,9 +117,6 @@
         for q in range(B // 2):
             out[q] = jnp.where(lane < 64, cells(q), pltpu.roll(cells(q + B // 2), 64, 1))
         out[B // 2] = asg_tile(asg)
-
-
-def own_stack(perm, src, own, asg, flags, base, flags_out):
     for q in range(B):
         base[q], base[B + q], base[2 * B + q] = perm[q], own[q].astype(f32), src[q]
     base[3 * B] = asg_tile(asg)
@@ -123,7 +126,11 @@
         flags_out[pl.ds(i, 1), :] = flags[pl.ds(at, 1), :].astype(f32)
 
 
-def stack_up(base, mr, ml, stack):
+def source_at(b, q):
+    return SRC + (q - 4 if b == 0 else q)
+
+
+def stack_up(base, mr, ml, stack, to_low, to_high):
     lane = lanes((B, LZ))
     row = rows((B, LZ))
     for q in range(B):
@@ -136,6 +143,10 @@
     stack[ASG] = jnp.where(
         row == 1, spread(mr[at, 0:1, :]), jnp.where(row == 2, spread(ml[at, 0:1, :]), base[3 * B])
     )
+    for out, first in ((to_low, 0), (to_high, 4)):
+        out[0:SRC] = stack[0:SRC]
+        for q in range(4):
+            out[SRC + q] = base[2 * B + first + q]
 
 
 def y_messages(low, mid, high, up, down):
@@ -161,9 +172,9 @@
             for q in range(B // 2):
                 out[M_HZ + 4 * b + q] = stacks[b][HZ + q]
         for at, (main, others) in enumerate(SRC_FOLDS):
-            tile = stacks[main // B][SRC + main % B]
+            tile = stacks[main // B][source_at(main // B, main % B)]
             for other, n, top in others:
-                tile = fold(tile, stacks[other // B][SRC + other % B], n, top, upward)
+                tile = fold(tile, stacks[other // B][source_at(other // B, other % B)], n, top, upward)
             out[M_SRC + at] = tile
         sides = jnp.where(lane < NSUB, low[ASG], pltpu.roll(high[ASG], NSUB, 1))
         out[M_ASG] = jnp.where(row < 3, sides, pltpu.roll(mid[ASG], 3, 0))
@@ -222,13 +233,20 @@
                 sums[pl.ds(first + i * NSUB + s, 1), :] = jnp.sum(parts[0], axis=0, keepdims=True)
         return carry
 
-    lax.fori_loop(0, NSUB, one, 0, unroll=4)
+    lax.fori_loop(0, NSUB, one, 0, unroll=8)
+
+
+def three_parts(x):
+    l1 = x.astype(bf16)
+    rest = x - l1.astype(f32)
+    l2 = rest.astype(bf16)
+    return l1, l2, (rest - l2.astype(f32)).astype(bf16)
 
 
 def lane_sums(sums):
     return lax.dot_general(
-        jnp.ones((B, LZ), f32), sums, (((1,), (1,)), ((), ())),
-        precision=lax.Precision.HIGHEST, preferred_element_type=f32,
+        jnp.ones((B, 3 * LZ), bf16), jnp.concatenate(three_parts(sums), axis=1),
+        (((1,), (1,)), ((), ())), preferred_element_type=f32,
     )
 
 
@@ -271,7 +289,7 @@
         lmid[p, :, 0:LZ] = stack[OWN + q].astype(i32)
         lmid[p, :, LZ:] = label
         if 4 <= p < 20:
-            smid[p - 4, :, 0:LZ] = stack[SRC + q]
+            smid[p - 4, :, 0:LZ] = stack[source_at(p // B, q)]
             smid[p - 4, :, LZ:] = src
 
 
@@ -405,10 +423,6 @@
 
 def one_hot_product(lefts, lows):
     left = jnp.concatenate(lefts, axis=1)
-    l1 = left.astype(bf16)
-    rest = left - l1.astype(f32)
-    l2 = rest.astype(bf16)
-    l3 = (rest - l2.astype(f32)).astype(bf16)
     wide = rows((LZ, LZ))
     right = jnp.concatenate(
         [
@@ -418,7 +432,7 @@
         axis=1,
     )
     return lax.dot_general(
-        jnp.concatenate([l1, l2, l3], axis=0), right, (((1,), (1,)), ((), ())),
+        jnp.concatenate(three_parts(left), axis=0), right, (((1,), (1,)), ((), ())),
         preferred_element_type=f32,
     )
 
@@ -631,27 +645,22 @@
     def send(x, axis, by, wrap=False):
         return lax.ppermute(x, axis, steps(lax.axis_size(axis), by, wrap))
 
-    assigned, flags = assignment.reshape(1, NSUB), layer_flags.reshape(n_col, LZ)
-    mr, ml = call(
+    mr, ml, base, flags = call(
         z_messages,
-        [sds(B // 2 + 1, B, LZ)] * 2,
-        4,
+        [pinned(B // 2 + 1, B, LZ)] * 2 + [pinned(3 * B + 1, B, LZ), pinned(3, LZ)],
+        5,
         scratch=[
             vm(plane, f32), vm(plane, f32), vm(plane, i32), vm((1, NSUB), i32),
-            pltpu.SemaphoreType.DMA((4,)),
+            vm((n_col, LZ), i32), pltpu.SemaphoreType.DMA((5,)),
         ],
         space=pl.ANY,
         limit=WHOLE_VMEM,
-    )(permeability, source, ownership, assigned)
+    )(permeability, source, ownership, assignment.reshape(1, NSUB), layer_flags.reshape(n_col, LZ))
     mr, ml = send(mr, "col", -1), send(ml, "col", 1)
-    base, flags = call(
-        own_stack,
-        [sds(3 * B + 1, B, LZ), sds(3, LZ)],
-        5,
-        cost=pl.CostEstimate(flops=100000, bytes_accessed=300000, transcendentals=0),
-    )(permeability, source, ownership, assigned, flags)
-    mid = call(stack_up, sds(STACK, B, LZ), 3)(base, mr, ml)
-    low, high = send(mid, "gx", 1), send(mid, "gx", -1)
+    mid, to_low, to_high = call(
+        stack_up, [sds(STACK, B, LZ)] + [sds(X_MESSAGE, B, LZ)] * 2, 3
+    )(base, mr, ml)
+    low, high = send(to_high, "gx", 1), send(to_low, "gx", -1)
     up, down = call(y_messages, [sds(MESSAGE, B, LZ)] * 2, 3)(low, mid, high)
     below, above = send(up, "gy", 1, True), send(down, "gy", -1, True)
     middle = call(

time: 112 us -> 110 us (0.982)
  waiting for transfers between devices: 3.51 us -> 9.08 us
  local copies, waits for them, and re-layouts: 3.6 us -> 0 us
  starting transfers between devices: 20 us -> 17.9 us
    ppermute x6, waiting for transfers between devices: 3.51 us -> 9.08 us  [send(): return lax.ppermute(x, axis, steps(lax.axis_size(axis), by, wrap))]
    unnamed x10 -> x0, local copies, waits for them, and re-layouts: 3.6 us -> none
    ppermute x6, starting transfers between devices: 20 us -> 17.9 us  [send(): return lax.ppermute(x, axis, steps(lax.axis_size(axis), by, wrap))]
    all_to_all x1, blocking collectives: 12.7 us -> 10.9 us  [on_device(): parts = lax.all_to_all(parts, 'gx', 0, 0, tiled=True)]
    all_to_all x1, blocking collectives: 27 us -> 28.6 us  [on_device(): bricks = lax.all_to_all(chunk, ('gy', 'col'), 0, 0, tiled=True)]
  transfers between devices with their start and end apart: 6 -> 6, of which waited for: 4 -> 5; matrix products, arithmetic and copies ran while one was open for 0% -> 0% of each run, Pallas kernels for 0% -> 0%
where the time goes in v6:
time: 110 us
  blocking collectives  65.4 us (59%)
  starting transfers between devices  17.9 us (16%)
  Pallas kernels  16.4 us (15%)
  waiting for transfers between devices  9.08 us (8%)
    all_to_all x1, blocking collectives, on_device(): bricks = lax.all_to_all(chunk, ('gy', 'col'), 0, 0, tiled=True)  28.6 us
    all_to_all x1, blocking collectives, on_device(): images = lax.all_to_all(chunk, ('gy', 'col'), 0, 0, tiled=True)  18.2 us
    ppermute x6, starting transfers between devices, send(): return lax.ppermute(x, axis, steps(lax.axis_size(axis), by, wrap))  17.9 us
    all_to_all x1, blocking collectives, on_device(): parts = lax.all_to_all(parts, 'gx', 0, 0, tiled=True)  10.9 us
    ppermute x6, waiting for transfers between devices, send(): return lax.ppermute(x, axis, steps(lax.axis_size(axis), by, wrap))  9.08 us
    all_to_all x1, blocking collectives, on_device(): images = lax.all_to_all(images, 'gx', 0, 0, tiled=True)  7.68 us
    pallas_call x1, Pallas kernels, on_device(): call(functools.partial(second_sums, *sizes), sds(n_bricks, 4, LZ), 6, scr...  6.2 us
    pallas_call x1, Pallas kernels, on_device(): call(functools.partial(first_sums, *sizes), [sds(6, NP, *FULL), sds(NP, *...  4.1 us
  transfers between devices with their start and end apart: 6, of which 5 were waited for; matrix products, arithmetic and copies ran while one was open for 0% of the time, Pallas kernels for 0%

profile of v6, /device:TPU:1, one launch (start us, length us, event | category | flops | bytes accessed | tf_op | source)
XLA Modules:
  0.0 109.6 jit_solution(7747107546509196703)
XLA Ops:
  0.6 1.0 shard_map.68
  1.6 1.3 %collective-permute-start = (f32[5,8,128]{2,1,0:T(8,128)S(1)}, f32[5,8,128]{2,1,0:T(8,128)S(1)}, u32[]{:S(2)}, u32[]{:S(2)}) collective-permute-start(f32[5,8,128]{2,1,0:T(8,128)S(1)} %get-tuple-element.21), channel_id=1, source_target_pairs={{1,0},{2,1},{3,2},{5,4},{6,5},{7,6},{9,8},{10,9},{11,10},{13,12},{... | collective-permute-start | bytes 61448 | tf_op jit(solution)/shard_map/ppermute | solution.py:646
  2.9 5.7 %collective-permute-start.1 = (f32[5,8,128]{2,1,0:T(8,128)S(1)}, f32[5,8,128]{2,1,0:T(8,128)S(1)}, u32[]{:S(2)}, u32[]{:S(2)}) collective-permute-start(f32[5,8,128]{2,1,0:T(8,128)S(1)} %get-tuple-element.22), channel_id=1, source_target_pairs={{0,1},{1,2},{2,3},{4,5},{5,6},{6,7},{8,9},{9,10},{10,11},{12,13},{... | collective-permute-start | bytes 61448 | tf_op jit(solution)/shard_map/ppermute | solution.py:646
  8.6 0.0 collective-permute-done.mr
  8.6 0.9 collective-permute-done.1.ml
  9.5 3.2 %collective-permute-start.2 = (f32[25,8,128]{2,1,0:T(8,128)S(1)}, f32[25,8,128]{2,1,0:T(8,128)S(1)}, u32[]{:S(2)}, u32[]{:S(2)}) collective-permute-start(f32[25,8,128]{2,1,0:T(8,128)S(1)} %get-tuple-element.23), channel_id=1, source_target_pairs={{0,64},{64,128},{128,192},{192,256},{256,320},{320,384},{384,448},... | collective-permute-start | bytes 307208 | tf_op jit(solution)/shard_map/ppermute | solution.py:646
  12.7 1.3 %collective-permute-start.3 = (f32[25,8,128]{2,1,0:T(8,128)S(1)}, f32[25,8,128]{2,1,0:T(8,128)S(1)}, u32[]{:S(2)}, u32[]{:S(2)}) collective-permute-start(f32[25,8,128]{2,1,0:T(8,128)S(1)} %get-tuple-element.25), channel_id=1, source_target_pairs={{64,0},{128,64},{192,128},{256,192},{320,256},{384,320},{448,384},... | collective-permute-start | bytes 307208 | tf_op jit(solution)/shard_map/ppermute | solution.py:646
  14.0 0.4 collective-permute-done.2.low
  14.4 3.7 %collective-permute-done.3.high = f32[25,8,128]{2,1,0:T(8,128)S(1)} collective-permute-done((f32[25,8,128]{2,1,0:T(8,128)S(1)}, f32[25,8,128]{2,1,0:T(8,128)S(1)}, u32[]{:S(2)}, u32[]{:S(2)}) %collective-permute-start.3) | collective-permute-done | bytes 102432 | tf_op jit(solution)/shard_map/ppermute | solution.py:646
  18.1 0.1 shard_map.70
  18.2 5.2 %collective-permute-start.4 = (f32[53,8,128]{2,1,0:T(8,128)S(1)}, f32[53,8,128]{2,1,0:T(8,128)S(1)}, u32[]{:S(2)}, u32[]{:S(2)}) collective-permute-start(f32[53,8,128]{2,1,0:T(8,128)S(1)} %get-tuple-element.26), channel_id=1, source_target_pairs={{0,4},{4,8},{8,12},{12,16},{16,20},{20,24},{24,28},{28,32},{32,36}... | collective-permute-start | bytes 651272 | tf_op jit(solution)/shard_map/ppermute | solution.py:646
  23.4 1.3 %collective-permute-start.5 = (f32[53,8,128]{2,1,0:T(8,128)S(1)}, f32[53,8,128]{2,1,0:T(8,128)S(1)}, u32[]{:S(2)}, u32[]{:S(2)}) collective-permute-start(f32[53,8,128]{2,1,0:T(8,128)S(1)} %get-tuple-element.27), channel_id=1, source_target_pairs={{0,60},{4,0},{8,4},{12,8},{16,12},{20,16},{24,20},{28,24},{32,28},... | collective-permute-start | bytes 651272 | tf_op jit(solution)/shard_map/ppermute | solution.py:646
  24.7 0.2 shard_map.71
  24.9 1.3 %collective-permute-done.4.below = f32[53,8,128]{2,1,0:T(8,128)S(1)} collective-permute-done((f32[53,8,128]{2,1,0:T(8,128)S(1)}, f32[53,8,128]{2,1,0:T(8,128)S(1)}, u32[]{:S(2)}, u32[]{:S(2)}) %collective-permute-start.4) | collective-permute-done | bytes 217120 | tf_op jit(solution)/shard_map/ppermute | solution.py:646
  26.2 2.8 %collective-permute-done.5.above = f32[53,8,128]{2,1,0:T(8,128)S(1)} collective-permute-done((f32[53,8,128]{2,1,0:T(8,128)S(1)}, f32[53,8,128]{2,1,0:T(8,128)S(1)}, u32[]{:S(2)}, u32[]{:S(2)}) %collective-permute-start.5) | collective-permute-done | bytes 217120 | tf_op jit(solution)/shard_map/ppermute | solution.py:646
  29.0 4.1 %shard_map.72 = (f32[6,24,24,256]{3,2,1,0:T(8,128)S(1)}, s32[24,24,256]{2,1,0:T(8,128)S(1)}, f32[64,2,128]{2,1,0:T(2,128)S(1)}, f32[24,8,128]{2,1,0:T(8,128)S(1)...) custom-call(f32[25,8,128]{2,1,0:T(8,128)S(1)} %collective-permute-done.2.low, ...), custom_call_target="tpu_custom_call" | custom-call | tf_op jit(solution)/shard_map/pallas_call | solution.py:673
  33.1 28.6 %all_to_all.20.values.first = f32[64,2,128]{2,1,0:T(2,128)S(1)} all-to-all(f32[64,2,128]{2,1,0:T(2,128)S(1)} %get-tuple-element.32), channel_id=1, replica_groups=mesh['gx'=8,'gy'=16,'col'=4] {'gy','col'}, dimensions={0} | all-to-all | bytes 131072 | tf_op jit(solution)/shard_map/all_to_all | solution.py:685
  61.7 0.8 shard_map.73
  62.5 10.9 %all_to_all.21.parts = f32[8,16,128]{2,1,0:T(8,128)S(1)} all-to-all(f32[8,16,128]{2,1,0:T(8,128)S(1)} %shard_map.73), channel_id=1, replica_groups=mesh['gx'=8,'gy'=16,'col'=4] {'gx'}, dimensions={0} | all-to-all | bytes 131072 | tf_op jit(solution)/shard_map/all_to_all | solution.py:689
  73.4 6.2 %shard_map.74 = f32[64,4,128]{2,1,0:T(4,128)S(1)} custom-call(f32[8,16,128]{2,1,0:T(8,128)S(1)} %all_to_all.21.parts, f32[6,24,24,256]{3,2,1,0:T(8,128)S(1)} %get-tuple-element.33.weights, s32[24,24,256]{2,1,0:T(8,128)S(1)} %get-tuple-element.34.labels, s32[3,3,8,128]{3,2,1,0:T(8,128)S(1)} %get-tuple-element.35.asg, ...), custom_call_target="tpu_custom_call" | custom-call | tf_op jit(solution)/shard_map/pallas_call | solution.py:691
  79.6 18.2 %all_to_all.22.values = f32[64,4,128]{2,1,0:T(4,128)S(1)} all-to-all(f32[64,4,128]{2,1,0:T(4,128)S(1)} %shard_map.74), channel_id=1, replica_groups=mesh['gx'=8,'gy'=16,'col'=4] {'gy','col'}, dimensions={0} | all-to-all | bytes 262144 | tf_op jit(solution)/shard_map/all_to_all | solution.py:697
  97.8 1.1 shard_map.75
  98.9 7.7 %all_to_all.23.images = f32[8,24,128]{2,1,0:T(8,128)S(1)} all-to-all(f32[8,24,128]{2,1,0:T(8,128)S(1)} %shard_map.75), channel_id=1, replica_groups=mesh['gx'=8,'gy'=16,'col'=4] {'gx'}, dimensions={0} | all-to-all | bytes 196608 | tf_op jit(solution)/shard_map/all_to_all | solution.py:701
  106.6 3.0 %shard_map.76 = (f32[8,8,128]{2,1,0:T(8,128)}, f32[1,16]{1,0:T(1,128)}) custom-call(f32[8,16,128]{2,1,0:T(8,128)S(1)} %all_to_all.21.parts, f32[8,24,128]{2,1,0:T(8,128)S(1)} %all_to_all.23.images, f32[6,24,24,256]{3,2,1,0:T(8,128)S(1)} %get-tuple-element.33.weights, s32[24,24,256]{2,1,0:T(8,128)S(1)} %get-tuple-element.34.labels, ...), custom_call_target="tpu_custom_call" | custom-call | tf_op jit(solution)/shard_map/pallas_call | solution.py:702
  (1 shorter events, 0.0 us)
Async XLA Ops:
  1.6 7.0 %collective-permute-start = (f32[5,8,128]{2,1,0:T(8,128)S(1)}, f32[5,8,128]{2,1,0:T(8,128)S(1)}, u32[]{:S(2)}, u32[]{:S(2)}) collective-permute-start(f32[5,8,128]{2,1,0:T(8,128)S(1)} %get-tuple-element.21), channel_id=1, source_target_pairs={{1,0},{2,1},{3,2},{5,4},{6,5},{7,6},{9,8},{10,9},{11,10},{13,12},{... | collective-permute-start | bytes 61448 | tf_op jit(solution)/shard_map/ppermute | solution.py:646
  2.9 6.6 %collective-permute-start.1 = (f32[5,8,128]{2,1,0:T(8,128)S(1)}, f32[5,8,128]{2,1,0:T(8,128)S(1)}, u32[]{:S(2)}, u32[]{:S(2)}) collective-permute-start(f32[5,8,128]{2,1,0:T(8,128)S(1)} %get-tuple-element.22), channel_id=1, source_target_pairs={{0,1},{1,2},{2,3},{4,5},{5,6},{6,7},{8,9},{9,10},{10,11},{12,13},{... | collective-permute-start | bytes 61448 | tf_op jit(solution)/shard_map/ppermute | solution.py:646
  9.5 4.8 %collective-permute-start.2 = (f32[25,8,128]{2,1,0:T(8,128)S(1)}, f32[25,8,128]{2,1,0:T(8,128)S(1)}, u32[]{:S(2)}, u32[]{:S(2)}) collective-permute-start(f32[25,8,128]{2,1,0:T(8,128)S(1)} %get-tuple-element.23), channel_id=1, source_target_pairs={{0,64},{64,128},{128,192},{192,256},{256,320},{320,384},{384,448},... | collective-permute-start | bytes 307208 | tf_op jit(solution)/shard_map/ppermute | solution.py:646
  12.7 5.4 %collective-permute-start.3 = (f32[25,8,128]{2,1,0:T(8,128)S(1)}, f32[25,8,128]{2,1,0:T(8,128)S(1)}, u32[]{:S(2)}, u32[]{:S(2)}) collective-permute-start(f32[25,8,128]{2,1,0:T(8,128)S(1)} %get-tuple-element.25), channel_id=1, source_target_pairs={{64,0},{128,64},{192,128},{256,192},{320,256},{384,320},{448,384},... | collective-permute-start | bytes 307208 | tf_op jit(solution)/shard_map/ppermute | solution.py:646
  18.2 8.1 %collective-permute-start.4 = (f32[53,8,128]{2,1,0:T(8,128)S(1)}, f32[53,8,128]{2,1,0:T(8,128)S(1)}, u32[]{:S(2)}, u32[]{:S(2)}) collective-permute-start(f32[53,8,128]{2,1,0:T(8,128)S(1)} %get-tuple-element.26), channel_id=1, source_target_pairs={{0,4},{4,8},{8,12},{12,16},{16,20},{20,24},{24,28},{28,32},{32,36}... | collective-permute-start | bytes 651272 | tf_op jit(solution)/shard_map/ppermute | solution.py:646
  23.4 5.6 %collective-permute-start.5 = (f32[53,8,128]{2,1,0:T(8,128)S(1)}, f32[53,8,128]{2,1,0:T(8,128)S(1)}, u32[]{:S(2)}, u32[]{:S(2)}) collective-permute-start(f32[53,8,128]{2,1,0:T(8,128)S(1)} %get-tuple-element.27), channel_id=1, source_target_pairs={{0,60},{4,0},{8,4},{12,8},{16,12},{20,16},{24,20},{28,24},{32,28},... | collective-permute-start | bytes 651272 | tf_op jit(solution)/shard_map/ppermute | solution.py:646

commit v7 on v6

--- a/solution.py
+++ b/solution.py
@@ -453,7 +453,7 @@
 GROUP = 64
 
 
-def first_coarse(n_bricks, n_out, values, out):
+def first_coarse(n_bricks, values, out):
     def one(i, total):
         lefts, lows = [], []
         for j in range(min(GROUP, n_bricks)):
@@ -464,9 +464,7 @@
         return total + one_hot_product(lefts, lows)
 
     total = lax.fori_loop(0, n_bricks // min(GROUP, n_bricks), one, jnp.zeros((6 * B, LZ), f32))
-    total = joined(total)
-    for d in range(n_out):
-        out[d] = total
+    out[...] = joined(total)
 
 
 def second_coarse(n_gy, n_col, n_out, values, first, out):
@@ -523,11 +521,9 @@
     return jnp.where((g >= 0) & (g < n_gx), total, 0.0)
 
 
-def guess(parts, g, n_gx):
-    total = slab_total(parts, g, n_gx, 0, 2 * B)
-    exists = (g >= 0) & (g < n_gx)
+def guess(total, exists):
     rhs, diag = total[0:B], jnp.where(exists, total[B : 2 * B], 1.0)
-    return rhs, diag, coarse_relax * rhs / diag
+    return rhs, diag, jnp.where(exists, coarse_relax * rhs / diag, 0.0)
 
 
 def expand(coarse, asg, labels, u, tables, first, last):
@@ -553,13 +549,14 @@
     lax.fori_loop(first, last + 1, one, 0, unroll=8)
 
 
-def second_sums(n_gx, n_gy, n_col, parts, weights, labels, asg, dvals, paths,
+def second_sums(n_gx, n_gy, n_col, below, here, above, weights, labels, asg, dvals, paths,
                 chunk, both, coarse, tables, ends, sums):
     gx = lax.axis_index("gx")
     row = rows((B, LZ))
     r = slice(B, 2 * B)
-    for i in range(3):
-        coarse[i] = guess(parts, gx + i - 1, n_gx)[2]
+    for i, total in enumerate((below, here, above)):
+        g = gx + i - 1
+        coarse[i] = guess(total, (g >= 0) & (g < n_gx))[2]
     expand(coarse, asg, labels, both.at[0], tables, 0, NP - 1)
 
     def after(k):
@@ -604,19 +601,20 @@
         chunk[d] = tile
 
 
-def last_sweeps(n_gx, n_gy, n_col, parts, images, weights, labels, asg,
+def last_sweeps(n_gx, n_gy, n_col, below, here, above, images, weights, labels, asg,
                 pressure, coarse_out, both, coarse, tables):
     gx, gy, col = (lax.axis_index(a) for a in ("gx", "gy", "col"))
-    for i in range(3):
+    for i, total in enumerate((below, here, above)):
         g = gx + i - 1
-        rhs, diag, start = guess(parts, g, n_gx)
+        exists = (g >= 0) & (g < n_gx)
+        rhs, diag, start = guess(total, exists)
         image = (
             slab_total(images, g, n_gx, 0, B)
             + slab_total(images, g - 1, n_gx, B, B)
             + slab_total(images, g + 1, n_gx, 2 * B, B)
         )
         second = start + coarse_relax * (rhs - image) / diag
-        coarse[i] = jnp.where((g >= 0) & (g < n_gx), second, 0.0)
+        coarse[i] = jnp.where(exists, second, 0.0)
     share = B * LZ // (n_gy * n_col)
     per_row = LZ // share
     mine = gy * n_col + col
@@ -683,17 +681,15 @@
         ],
     )(low, mid, high, below, above, flags, *middle)
     bricks = lax.all_to_all(chunk, ("gy", "col"), 0, 0, tiled=True)
-    parts = call(
-        functools.partial(first_coarse, n_bricks, n_gx), sds(n_gx, 2 * B, LZ), 1
-    )(bricks)
-    parts = lax.all_to_all(parts, "gx", 0, 0, tiled=True)
+    here = call(functools.partial(first_coarse, n_bricks), sds(2 * B, LZ), 1)(bricks)
+    parts = (send(here, "gx", 1), here, send(here, "gx", -1))
     tables = [vm((3, B, LZ), f32), vm((3, 3, B, LZ), f32)]
     chunk = call(
         functools.partial(second_sums, *sizes),
         sds(n_bricks, 4, LZ),
-        6,
+        8,
         scratch=[fields, *tables, vm((4, B, LZ), f32), vm((6 * NSUB, LZ), f32)],
-    )(parts, weights, labels, asg, dvals, paths)
+    )(*parts, weights, labels, asg, dvals, paths)
     images = lax.all_to_all(chunk, ("gy", "col"), 0, 0, tiled=True)
     images = call(
         functools.partial(second_coarse, n_gy, n_col, n_gx), sds(n_gx, 3 * B, LZ), 2
@@ -702,9 +698,9 @@
     return call(
         functools.partial(last_sweeps, *sizes),
         [sds(*plane), sds(1, B * LZ // (n_gy * n_col))],
-        5,
+        7,
         scratch=[fields, *tables],
-    )(parts, images, weights, labels, asg)
+    )(*parts, images, weights, labels, asg)
 
 
 def solution(mesh):

time: 110 us -> 112 us (1.018)
  starting transfers between devices: 17.9 us -> 23.2 us
  blocking collectives: 65.4 us -> 61.1 us
    all_to_all x1 -> x0, blocking collectives: 10.9 us -> none  [on_device(): parts = lax.all_to_all(parts, 'gx', 0, 0, tiled=True)]
    all_to_all x1, blocking collectives: 7.68 us -> 14.6 us  [on_device(): images = lax.all_to_all(images, 'gx', 0, 0, tiled=True)]
    ppermute x6 -> x8, starting transfers between devices: 17.9 us -> 23.2 us  [send(): return lax.ppermute(x, axis, steps(lax.axis_size(axis), by, wrap))]
    ppermute x6 -> x8, waiting for transfers between devices: 9.08 us -> 9.85 us  [send(): return lax.ppermute(x, axis, steps(lax.axis_size(axis), by, wrap))]
  transfers between devices with their start and end apart: 6 -> 8, of which waited for: 5 -> 6; matrix products, arithmetic and copies ran while one was open for 0% -> 0% of each run, Pallas kernels for 0% -> 0%
where the time goes in v7:
time: 112 us; the launch traced here: 111 us
  blocking collectives  61.1 us (55%)
  starting transfers between devices  23.2 us (21%)
  Pallas kernels  16.4 us (15%)
  waiting for transfers between devices  9.85 us (9%)
    all_to_all x1, blocking collectives, on_device(): bricks = lax.all_to_all(chunk, ('gy', 'col'), 0, 0, tiled=True)  28.6 us
    ppermute x8, starting transfers between devices, send(): return lax.ppermute(x, axis, steps(lax.axis_size(axis), by, wrap))  23.2 us
    all_to_all x1, blocking collectives, on_device(): images = lax.all_to_all(chunk, ('gy', 'col'), 0, 0, tiled=True)  17.9 us
    all_to_all x1, blocking collectives, on_device(): images = lax.all_to_all(images, 'gx', 0, 0, tiled=True)  14.6 us
    ppermute x8, waiting for transfers between devices, send(): return lax.ppermute(x, axis, steps(lax.axis_size(axis), by, wrap))  9.85 us
    pallas_call x1, Pallas kernels, on_device(): call(functools.partial(second_sums, *sizes), sds(n_bricks, 4, LZ), 8, scr...  6.2 us
    pallas_call x1, Pallas kernels, on_device(): call(functools.partial(first_sums, *sizes), [sds(6, NP, *FULL), sds(NP, *...  4.1 us
    pallas_call x1, Pallas kernels, on_device(): call(functools.partial(last_sweeps, *sizes), [sds(*plane), sds(1, B * LZ...  2.97 us
  transfers between devices with their start and end apart: 8, of which 6 were waited for; matrix products, arithmetic and copies ran while one was open for 0% of the time, Pallas kernels for 0%

profile of v7, /device:TPU:1, one launch (start us, length us, event | category | flops | bytes accessed | tf_op | source)
XLA Modules:
  0.0 111.3 jit_solution(1919864123116566359)
XLA Ops:
  0.6 1.0 shard_map.68
  1.6 1.3 %collective-permute-start = (f32[5,8,128]{2,1,0:T(8,128)S(1)}, f32[5,8,128]{2,1,0:T(8,128)S(1)}, u32[]{:S(2)}, u32[]{:S(2)}) collective-permute-start(f32[5,8,128]{2,1,0:T(8,128)S(1)} %get-tuple-element.21), channel_id=1, source_target_pairs={{1,0},{2,1},{3,2},{5,4},{6,5},{7,6},{9,8},{10,9},{11,10},{13,12},{... | collective-permute-start | bytes 61448 | tf_op jit(solution)/shard_map/ppermute | solution.py:644
  2.9 5.7 %collective-permute-start.1 = (f32[5,8,128]{2,1,0:T(8,128)S(1)}, f32[5,8,128]{2,1,0:T(8,128)S(1)}, u32[]{:S(2)}, u32[]{:S(2)}) collective-permute-start(f32[5,8,128]{2,1,0:T(8,128)S(1)} %get-tuple-element.22), channel_id=1, source_target_pairs={{0,1},{1,2},{2,3},{4,5},{5,6},{6,7},{8,9},{9,10},{10,11},{12,13},{... | collective-permute-start | bytes 61448 | tf_op jit(solution)/shard_map/ppermute | solution.py:644
  8.6 0.0 collective-permute-done.mr
  8.6 0.9 collective-permute-done.1.ml
  9.5 3.2 %collective-permute-start.2 = (f32[25,8,128]{2,1,0:T(8,128)S(1)}, f32[25,8,128]{2,1,0:T(8,128)S(1)}, u32[]{:S(2)}, u32[]{:S(2)}) collective-permute-start(f32[25,8,128]{2,1,0:T(8,128)S(1)} %get-tuple-element.23), channel_id=1, source_target_pairs={{0,64},{64,128},{128,192},{192,256},{256,320},{320,384},{384,448},... | collective-permute-start | bytes 307208 | tf_op jit(solution)/shard_map/ppermute | solution.py:644
  12.7 1.3 %collective-permute-start.3 = (f32[25,8,128]{2,1,0:T(8,128)S(1)}, f32[25,8,128]{2,1,0:T(8,128)S(1)}, u32[]{:S(2)}, u32[]{:S(2)}) collective-permute-start(f32[25,8,128]{2,1,0:T(8,128)S(1)} %get-tuple-element.25), channel_id=1, source_target_pairs={{64,0},{128,64},{192,128},{256,192},{320,256},{384,320},{448,384},... | collective-permute-start | bytes 307208 | tf_op jit(solution)/shard_map/ppermute | solution.py:644
  14.0 0.4 collective-permute-done.2.low
  14.4 3.7 %collective-permute-done.3.high = f32[25,8,128]{2,1,0:T(8,128)S(1)} collective-permute-done((f32[25,8,128]{2,1,0:T(8,128)S(1)}, f32[25,8,128]{2,1,0:T(8,128)S(1)}, u32[]{:S(2)}, u32[]{:S(2)}) %collective-permute-start.3) | collective-permute-done | bytes 102432 | tf_op jit(solution)/shard_map/ppermute | solution.py:644
  18.1 0.1 shard_map.70
  18.2 5.2 %collective-permute-start.4 = (f32[53,8,128]{2,1,0:T(8,128)S(1)}, f32[53,8,128]{2,1,0:T(8,128)S(1)}, u32[]{:S(2)}, u32[]{:S(2)}) collective-permute-start(f32[53,8,128]{2,1,0:T(8,128)S(1)} %get-tuple-element.26), channel_id=1, source_target_pairs={{0,4},{4,8},{8,12},{12,16},{16,20},{20,24},{24,28},{28,32},{32,36}... | collective-permute-start | bytes 651272 | tf_op jit(solution)/shard_map/ppermute | solution.py:644
  23.4 1.3 %collective-permute-start.5 = (f32[53,8,128]{2,1,0:T(8,128)S(1)}, f32[53,8,128]{2,1,0:T(8,128)S(1)}, u32[]{:S(2)}, u32[]{:S(2)}) collective-permute-start(f32[53,8,128]{2,1,0:T(8,128)S(1)} %get-tuple-element.27), channel_id=1, source_target_pairs={{0,60},{4,0},{8,4},{12,8},{16,12},{20,16},{24,20},{28,24},{32,28},... | collective-permute-start | bytes 651272 | tf_op jit(solution)/shard_map/ppermute | solution.py:644
  24.7 0.2 shard_map.71
  24.9 1.3 %collective-permute-done.4.below = f32[53,8,128]{2,1,0:T(8,128)S(1)} collective-permute-done((f32[53,8,128]{2,1,0:T(8,128)S(1)}, f32[53,8,128]{2,1,0:T(8,128)S(1)}, u32[]{:S(2)}, u32[]{:S(2)}) %collective-permute-start.4) | collective-permute-done | bytes 217120 | tf_op jit(solution)/shard_map/ppermute | solution.py:644
  26.2 2.8 %collective-permute-done.5.above = f32[53,8,128]{2,1,0:T(8,128)S(1)} collective-permute-done((f32[53,8,128]{2,1,0:T(8,128)S(1)}, f32[53,8,128]{2,1,0:T(8,128)S(1)}, u32[]{:S(2)}, u32[]{:S(2)}) %collective-permute-start.5) | collective-permute-done | bytes 217120 | tf_op jit(solution)/shard_map/ppermute | solution.py:644
  29.0 4.1 %shard_map.72 = (f32[6,24,24,256]{3,2,1,0:T(8,128)S(1)}, s32[24,24,256]{2,1,0:T(8,128)S(1)}, f32[64,2,128]{2,1,0:T(2,128)S(1)}, f32[24,8,128]{2,1,0:T(8,128)S(1)...) custom-call(f32[25,8,128]{2,1,0:T(8,128)S(1)} %collective-permute-done.2.low, ...), custom_call_target="tpu_custom_call" | custom-call | tf_op jit(solution)/shard_map/pallas_call | solution.py:671
  33.1 28.6 %all_to_all.15.values.first = f32[64,2,128]{2,1,0:T(2,128)S(1)} all-to-all(f32[64,2,128]{2,1,0:T(2,128)S(1)} %get-tuple-element.32), channel_id=1, replica_groups=mesh['gx'=8,'gy'=16,'col'=4] {'gy','col'}, dimensions={0} | all-to-all | bytes 131072 | tf_op jit(solution)/shard_map/all_to_all | solution.py:683
  61.7 0.7 shard_map.73.here
  62.5 1.3 %collective-permute-start.7 = (f32[16,128]{1,0:T(8,128)S(1)}, f32[16,128]{1,0:T(8,128)S(1)}, u32[]{:S(2)}, u32[]{:S(2)}) collective-permute-start(f32[16,128]{1,0:T(8,128)S(1)} %shard_map.73.here), channel_id=1, source_target_pairs={{64,0},{128,64},{192,128},{256,192},{320,256},{384,320},{448,384},... | collective-permute-start | bytes 24584 | tf_op jit(solution)/shard_map/ppermute | solution.py:644
  63.8 4.0 %collective-permute-start.6 = (f32[16,128]{1,0:T(8,128)S(1)}, f32[16,128]{1,0:T(8,128)S(1)}, u32[]{:S(2)}, u32[]{:S(2)}) collective-permute-start(f32[16,128]{1,0:T(8,128)S(1)} %shard_map.73.here), channel_id=1, source_target_pairs={{0,64},{64,128},{128,192},{192,256},{256,320},{320,384},{384,448},... | collective-permute-start | bytes 24584 | tf_op jit(solution)/shard_map/ppermute | solution.py:644
  67.8 0.0 collective-permute-done.7.above
  67.8 0.8 collective-permute-done.6.below
  68.6 6.2 %shard_map.74 = f32[64,4,128]{2,1,0:T(4,128)S(1)} custom-call(f32[16,128]{1,0:T(8,128)S(1)} %collective-permute-done.6.below, f32[16,128]{1,0:T(8,128)S(1)} %shard_map.73.here, f32[16,128]{1,0:T(8,128)S(1)} %collective-permute-done.7.above, f32[6,24,24,256]{3,2,1,0:T(8,128)S(1)} %get-tuple-element.33.weights, s32[24,24,256]{2,1,0:T(8,128)S(1)} %get-tuple-element.34.labels, ...), custom_call_target="tpu_custom_call" | custom-call | tf_op jit(solution)/shard_map/pallas_call | solution.py:687
  74.8 17.9 %all_to_all.16.values = f32[64,4,128]{2,1,0:T(4,128)S(1)} all-to-all(f32[64,4,128]{2,1,0:T(4,128)S(1)} %shard_map.74), channel_id=1, replica_groups=mesh['gx'=8,'gy'=16,'col'=4] {'gy','col'}, dimensions={0} | all-to-all | bytes 262144 | tf_op jit(solution)/shard_map/all_to_all | solution.py:693
  92.7 1.1 shard_map.75
  93.8 14.6 %all_to_all.17.images = f32[8,24,128]{2,1,0:T(8,128)S(1)} all-to-all(f32[8,24,128]{2,1,0:T(8,128)S(1)} %shard_map.75), channel_id=1, replica_groups=mesh['gx'=8,'gy'=16,'col'=4] {'gx'}, dimensions={0} | all-to-all | bytes 196608 | tf_op jit(solution)/shard_map/all_to_all | solution.py:697
  108.4 3.0 %shard_map.76 = (f32[8,8,128]{2,1,0:T(8,128)}, f32[1,16]{1,0:T(1,128)}) custom-call(f32[16,128]{1,0:T(8,128)S(1)} %collective-permute-done.6.below, f32[16,128]{1,0:T(8,128)S(1)} %shard_map.73.here, f32[16,128]{1,0:T(8,128)S(1)} %collective-permute-done.7.above, f32[8,24,128]{2,1,0:T(8,128)S(1)} %all_to_all.17.images, ...), custom_call_target="tpu_custom_call" | custom-call | tf_op jit(solution)/shard_map/pallas_call | solution.py:698
  (1 shorter events, 0.0 us)
Async XLA Ops:
  1.6 7.0 %collective-permute-start = (f32[5,8,128]{2,1,0:T(8,128)S(1)}, f32[5,8,128]{2,1,0:T(8,128)S(1)}, u32[]{:S(2)}, u32[]{:S(2)}) collective-permute-start(f32[5,8,128]{2,1,0:T(8,128)S(1)} %get-tuple-element.21), channel_id=1, source_target_pairs={{1,0},{2,1},{3,2},{5,4},{6,5},{7,6},{9,8},{10,9},{11,10},{13,12},{... | collective-permute-start | bytes 61448 | tf_op jit(solution)/shard_map/ppermute | solution.py:644
  2.9 6.6 %collective-permute-start.1 = (f32[5,8,128]{2,1,0:T(8,128)S(1)}, f32[5,8,128]{2,1,0:T(8,128)S(1)}, u32[]{:S(2)}, u32[]{:S(2)}) collective-permute-start(f32[5,8,128]{2,1,0:T(8,128)S(1)} %get-tuple-element.22), channel_id=1, source_target_pairs={{0,1},{1,2},{2,3},{4,5},{5,6},{6,7},{8,9},{9,10},{10,11},{12,13},{... | collective-permute-start | bytes 61448 | tf_op jit(solution)/shard_map/ppermute | solution.py:644
  9.5 4.8 %collective-permute-start.2 = (f32[25,8,128]{2,1,0:T(8,128)S(1)}, f32[25,8,128]{2,1,0:T(8,128)S(1)}, u32[]{:S(2)}, u32[]{:S(2)}) collective-permute-start(f32[25,8,128]{2,1,0:T(8,128)S(1)} %get-tuple-element.23), channel_id=1, source_target_pairs={{0,64},{64,128},{128,192},{192,256},{256,320},{320,384},{384,448},... | collective-permute-start | bytes 307208 | tf_op jit(solution)/shard_map/ppermute | solution.py:644
  12.7 5.4 %collective-permute-start.3 = (f32[25,8,128]{2,1,0:T(8,128)S(1)}, f32[25,8,128]{2,1,0:T(8,128)S(1)}, u32[]{:S(2)}, u32[]{:S(2)}) collective-permute-start(f32[25,8,128]{2,1,0:T(8,128)S(1)} %get-tuple-element.25), channel_id=1, source_target_pairs={{64,0},{128,64},{192,128},{256,192},{320,256},{384,320},{448,384},... | collective-permute-start | bytes 307208 | tf_op jit(solution)/shard_map/ppermute | solution.py:644
  18.2 8.1 %collective-permute-start.4 = (f32[53,8,128]{2,1,0:T(8,128)S(1)}, f32[53,8,128]{2,1,0:T(8,128)S(1)}, u32[]{:S(2)}, u32[]{:S(2)}) collective-permute-start(f32[53,8,128]{2,1,0:T(8,128)S(1)} %get-tuple-element.26), channel_id=1, source_target_pairs={{0,4},{4,8},{8,12},{12,16},{16,20},{20,24},{24,28},{28,32},{32,36}... | collective-permute-start | bytes 651272 | tf_op jit(solution)/shard_map/ppermute | solution.py:644
  23.4 5.6 %collective-permute-start.5 = (f32[53,8,128]{2,1,0:T(8,128)S(1)}, f32[53,8,128]{2,1,0:T(8,128)S(1)}, u32[]{:S(2)}, u32[]{:S(2)}) collective-permute-start(f32[53,8,128]{2,1,0:T(8,128)S(1)} %get-tuple-element.27), channel_id=1, source_target_pairs={{0,60},{4,0},{8,4},{12,8},{16,12},{20,16},{24,20},{28,24},{32,28},... | collective-permute-start | bytes 651272 | tf_op jit(solution)/shard_map/ppermute | solution.py:644
  62.5 5.3 %collective-permute-start.7 = (f32[16,128]{1,0:T(8,128)S(1)}, f32[16,128]{1,0:T(8,128)S(1)}, u32[]{:S(2)}, u32[]{:S(2)}) collective-permute-start(f32[16,128]{1,0:T(8,128)S(1)} %shard_map.73.here), channel_id=1, source_target_pairs={{64,0},{128,64},{192,128},{256,192},{320,256},{384,320},{448,384},... | collective-permute-start | bytes 24584 | tf_op jit(solution)/shard_map/ppermute | solution.py:644
  63.8 4.8 %collective-permute-start.6 = (f32[16,128]{1,0:T(8,128)S(1)}, f32[16,128]{1,0:T(8,128)S(1)}, u32[]{:S(2)}, u32[]{:S(2)}) collective-permute-start(f32[16,128]{1,0:T(8,128)S(1)} %shard_map.73.here), channel_id=1, source_target_pairs={{0,64},{64,128},{128,192},{192,256},{256,320},{320,384},{384,448},... | collective-permute-start | bytes 24584 | tf_op jit(solution)/shard_map/ppermute | solution.py:644

commit v8 on v6

--- a/solution.py
+++ b/solution.py
@@ -222,6 +222,21 @@
     lax.fori_loop(first, last + 1, one_sweep, 0)
 
 
+def own_tile(u_ref, w_ref, p):
+    r, z = slice(B, 2 * B), slice(0, LZ)
+    u, beyond = u_ref[p + 1, r, z], u_ref[p + 1, r, LZ:]
+    lane = lanes((B, LZ))
+    right = jnp.where(lane == LZ - 1, pltpu.roll(beyond, LZ - 1, 1), pltpu.roll(u, LZ - 1, 1))
+    left = jnp.where(lane == 0, pltpu.roll(beyond, 1, 1), pltpu.roll(u, 1, 1))
+    w = [w_ref[i, p, r, z] for i in range(6)]
+    near = (
+        (w[0] * u_ref[p + 2, r, z] + w[1] * u_ref[p, r, z])
+        + (w[2] * u_ref[p + 1, B + 1 : 2 * B + 1, z] + w[3] * u_ref[p + 1, B - 1 : 2 * B - 1, z])
+        + (w[4] * right + w[5] * left)
+    )
+    return (1.0 - fine_relax) * u + near
+
+
 def label_sums(groups, sums):
     def one(s, carry):
         for first, labels, fields in groups:
@@ -407,8 +422,8 @@
     paths[0] = rise
     paths[1] = fall
 
-    sweeps(both, weights, 5, 8)
-    tiles = [both[1, B + 1 + q, B : 2 * B, 0:LZ] * dvals[B + q] for q in range(B)]
+    sweeps(both, weights, 5, 7)
+    tiles = [own_tile(both.at[0], weights, B + q) * dvals[B + q] for q in range(B)]
     diag_tiles = [dvals[B + q] for q in range(B)]
     label_tiles = [labels[B + q, B : 2 * B, 0:LZ] for q in range(B)]
     label_sums([(0, label_tiles, (tiles, diag_tiles))], sums)
@@ -578,8 +593,8 @@
                 ends[2, q : q + 1, :] = plane[0:1] * -paths[2, q : q + 1, :]
                 ends[3, q : q + 1, :] = plane[B - 1 : B] * -paths[3, q : q + 1, :]
 
-    sweeps(both, weights, 0, 8, after=after, operator_at=4)
-    tiles = [both[1, B + 1 + q, r, 0:LZ] * dvals[B + q] for q in range(B)]
+    sweeps(both, weights, 0, 7, after=after, operator_at=4)
+    tiles = [own_tile(both.at[0], weights, B + q) * dvals[B + q] for q in range(B)]
     label_tiles = [labels[B + q, r, 0:LZ] for q in range(B)]
     beyond = [labels[2 * B, r, 0:LZ], labels[B - 1, r, 0:LZ]]
     for at in (2 * B, B - 1):
@@ -624,9 +639,9 @@
     turned = pltpu.roll(spread(row), lax.rem(LZ - lax.rem(mine, per_row) * share, LZ), 1)
     coarse_out[...] = turned[0:1, 0:share]
     expand(coarse, asg, labels, both.at[1], tables, 4, 19)
-    sweeps(both, weights, 5, 8)
+    sweeps(both, weights, 5, 7)
     for q in range(B):
-        pressure[q] = both[1, B + 1 + q, B : 2 * B, 0:LZ]
+        pressure[q] = own_tile(both.at[0], weights, B + q)
 
 
 def steps(count, by, wrap):

time: 110 us -> 110 us (level)
  no operation moved by 1% of the time
where the time goes in v8:
time: 110 us; the launch traced here: 109 us
  blocking collectives  65.4 us (59%)
  starting transfers between devices  17.9 us (16%)
  Pallas kernels  15.9 us (14%)
  waiting for transfers between devices  9.08 us (8%)
    all_to_all x1, blocking collectives, on_device(): bricks = lax.all_to_all(chunk, ('gy', 'col'), 0, 0, tiled=True)  28.6 us
    all_to_all x1, blocking collectives, on_device(): images = lax.all_to_all(chunk, ('gy', 'col'), 0, 0, tiled=True)  18.2 us
    ppermute x6, starting transfers between devices, send(): return lax.ppermute(x, axis, steps(lax.axis_size(axis), by, wrap))  17.9 us
    all_to_all x1, blocking collectives, on_device(): parts = lax.all_to_all(parts, 'gx', 0, 0, tiled=True)  10.9 us
    ppermute x6, waiting for transfers between devices, send(): return lax.ppermute(x, axis, steps(lax.axis_size(axis), by, wrap))  9.08 us
    all_to_all x1, blocking collectives, on_device(): images = lax.all_to_all(images, 'gx', 0, 0, tiled=True)  7.68 us
    pallas_call x1, Pallas kernels, on_device(): call(functools.partial(second_sums, *sizes), sds(n_bricks, 4, LZ), 6, scr...  6.05 us
    pallas_call x1, Pallas kernels, on_device(): call(functools.partial(first_sums, *sizes), [sds(6, NP, *FULL), sds(NP, *...  3.92 us
  transfers between devices with their start and end apart: 6, of which 5 were waited for; matrix products, arithmetic and copies ran while one was open for 0% of the time, Pallas kernels for 0%

profile of v8, /device:TPU:1, one launch (start us, length us, event | category | flops | bytes accessed | tf_op | source)
XLA Modules:
  0.0 109.1 jit_solution(15163258276100033051)
XLA Ops:
  0.6 1.0 shard_map.68
  1.6 1.3 %collective-permute-start = (f32[5,8,128]{2,1,0:T(8,128)S(1)}, f32[5,8,128]{2,1,0:T(8,128)S(1)}, u32[]{:S(2)}, u32[]{:S(2)}) collective-permute-start(f32[5,8,128]{2,1,0:T(8,128)S(1)} %get-tuple-element.21), channel_id=1, source_target_pairs={{1,0},{2,1},{3,2},{5,4},{6,5},{7,6},{9,8},{10,9},{11,10},{13,12},{... | collective-permute-start | bytes 61448 | tf_op jit(solution)/shard_map/ppermute | solution.py:661
  2.9 5.7 %collective-permute-start.1 = (f32[5,8,128]{2,1,0:T(8,128)S(1)}, f32[5,8,128]{2,1,0:T(8,128)S(1)}, u32[]{:S(2)}, u32[]{:S(2)}) collective-permute-start(f32[5,8,128]{2,1,0:T(8,128)S(1)} %get-tuple-element.22), channel_id=1, source_target_pairs={{0,1},{1,2},{2,3},{4,5},{5,6},{6,7},{8,9},{9,10},{10,11},{12,13},{... | collective-permute-start | bytes 61448 | tf_op jit(solution)/shard_map/ppermute | solution.py:661
  8.6 0.0 collective-permute-done.mr
  8.6 0.9 collective-permute-done.1.ml
  9.5 3.2 %collective-permute-start.2 = (f32[25,8,128]{2,1,0:T(8,128)S(1)}, f32[25,8,128]{2,1,0:T(8,128)S(1)}, u32[]{:S(2)}, u32[]{:S(2)}) collective-permute-start(f32[25,8,128]{2,1,0:T(8,128)S(1)} %get-tuple-element.23), channel_id=1, source_target_pairs={{0,64},{64,128},{128,192},{192,256},{256,320},{320,384},{384,448},... | collective-permute-start | bytes 307208 | tf_op jit(solution)/shard_map/ppermute | solution.py:661
  12.7 1.3 %collective-permute-start.3 = (f32[25,8,128]{2,1,0:T(8,128)S(1)}, f32[25,8,128]{2,1,0:T(8,128)S(1)}, u32[]{:S(2)}, u32[]{:S(2)}) collective-permute-start(f32[25,8,128]{2,1,0:T(8,128)S(1)} %get-tuple-element.25), channel_id=1, source_target_pairs={{64,0},{128,64},{192,128},{256,192},{320,256},{384,320},{448,384},... | collective-permute-start | bytes 307208 | tf_op jit(solution)/shard_map/ppermute | solution.py:661
  14.0 0.4 collective-permute-done.2.low
  14.4 3.7 %collective-permute-done.3.high = f32[25,8,128]{2,1,0:T(8,128)S(1)} collective-permute-done((f32[25,8,128]{2,1,0:T(8,128)S(1)}, f32[25,8,128]{2,1,0:T(8,128)S(1)}, u32[]{:S(2)}, u32[]{:S(2)}) %collective-permute-start.3) | collective-permute-done | bytes 102432 | tf_op jit(solution)/shard_map/ppermute | solution.py:661
  18.1 0.1 shard_map.70
  18.2 5.2 %collective-permute-start.4 = (f32[53,8,128]{2,1,0:T(8,128)S(1)}, f32[53,8,128]{2,1,0:T(8,128)S(1)}, u32[]{:S(2)}, u32[]{:S(2)}) collective-permute-start(f32[53,8,128]{2,1,0:T(8,128)S(1)} %get-tuple-element.26), channel_id=1, source_target_pairs={{0,4},{4,8},{8,12},{12,16},{16,20},{20,24},{24,28},{28,32},{32,36}... | collective-permute-start | bytes 651272 | tf_op jit(solution)/shard_map/ppermute | solution.py:661
  23.4 1.3 %collective-permute-start.5 = (f32[53,8,128]{2,1,0:T(8,128)S(1)}, f32[53,8,128]{2,1,0:T(8,128)S(1)}, u32[]{:S(2)}, u32[]{:S(2)}) collective-permute-start(f32[53,8,128]{2,1,0:T(8,128)S(1)} %get-tuple-element.27), channel_id=1, source_target_pairs={{0,60},{4,0},{8,4},{12,8},{16,12},{20,16},{24,20},{28,24},{32,28},... | collective-permute-start | bytes 651272 | tf_op jit(solution)/shard_map/ppermute | solution.py:661
  24.7 0.2 shard_map.71
  24.9 1.3 %collective-permute-done.4.below = f32[53,8,128]{2,1,0:T(8,128)S(1)} collective-permute-done((f32[53,8,128]{2,1,0:T(8,128)S(1)}, f32[53,8,128]{2,1,0:T(8,128)S(1)}, u32[]{:S(2)}, u32[]{:S(2)}) %collective-permute-start.4) | collective-permute-done | bytes 217120 | tf_op jit(solution)/shard_map/ppermute | solution.py:661
  26.2 2.8 %collective-permute-done.5.above = f32[53,8,128]{2,1,0:T(8,128)S(1)} collective-permute-done((f32[53,8,128]{2,1,0:T(8,128)S(1)}, f32[53,8,128]{2,1,0:T(8,128)S(1)}, u32[]{:S(2)}, u32[]{:S(2)}) %collective-permute-start.5) | collective-permute-done | bytes 217120 | tf_op jit(solution)/shard_map/ppermute | solution.py:661
  29.0 3.9 %shard_map.72 = (f32[6,24,24,256]{3,2,1,0:T(8,128)S(1)}, s32[24,24,256]{2,1,0:T(8,128)S(1)}, f32[64,2,128]{2,1,0:T(2,128)S(1)}, f32[24,8,128]{2,1,0:T(8,128)S(1)...) custom-call(f32[25,8,128]{2,1,0:T(8,128)S(1)} %collective-permute-done.2.low, ...), custom_call_target="tpu_custom_call" | custom-call | tf_op jit(solution)/shard_map/pallas_call | solution.py:688
  32.9 28.6 %all_to_all.20.values.first = f32[64,2,128]{2,1,0:T(2,128)S(1)} all-to-all(f32[64,2,128]{2,1,0:T(2,128)S(1)} %get-tuple-element.32), channel_id=1, replica_groups=mesh['gx'=8,'gy'=16,'col'=4] {'gy','col'}, dimensions={0} | all-to-all | bytes 131072 | tf_op jit(solution)/shard_map/all_to_all | solution.py:700
  61.6 0.8 shard_map.73
  62.3 10.9 %all_to_all.21.parts = f32[8,16,128]{2,1,0:T(8,128)S(1)} all-to-all(f32[8,16,128]{2,1,0:T(8,128)S(1)} %shard_map.73), channel_id=1, replica_groups=mesh['gx'=8,'gy'=16,'col'=4] {'gx'}, dimensions={0} | all-to-all | bytes 131072 | tf_op jit(solution)/shard_map/all_to_all | solution.py:704
  73.2 6.1 %shard_map.74 = f32[64,4,128]{2,1,0:T(4,128)S(1)} custom-call(f32[8,16,128]{2,1,0:T(8,128)S(1)} %all_to_all.21.parts, f32[6,24,24,256]{3,2,1,0:T(8,128)S(1)} %get-tuple-element.33.weights, s32[24,24,256]{2,1,0:T(8,128)S(1)} %get-tuple-element.34.labels, s32[3,3,8,128]{3,2,1,0:T(8,128)S(1)} %get-tuple-element.35.asg, ...), custom_call_target="tpu_custom_call" | custom-call | tf_op jit(solution)/shard_map/pallas_call | solution.py:706
  79.3 18.2 %all_to_all.22.values = f32[64,4,128]{2,1,0:T(4,128)S(1)} all-to-all(f32[64,4,128]{2,1,0:T(4,128)S(1)} %shard_map.74), channel_id=1, replica_groups=mesh['gx'=8,'gy'=16,'col'=4] {'gy','col'}, dimensions={0} | all-to-all | bytes 262144 | tf_op jit(solution)/shard_map/all_to_all | solution.py:712
  97.5 1.1 shard_map.75
  98.6 7.7 %all_to_all.23.images = f32[8,24,128]{2,1,0:T(8,128)S(1)} all-to-all(f32[8,24,128]{2,1,0:T(8,128)S(1)} %shard_map.75), channel_id=1, replica_groups=mesh['gx'=8,'gy'=16,'col'=4] {'gx'}, dimensions={0} | all-to-all | bytes 196608 | tf_op jit(solution)/shard_map/all_to_all | solution.py:716
  106.3 2.8 %shard_map.76 = (f32[8,8,128]{2,1,0:T(8,128)}, f32[1,16]{1,0:T(1,128)}) custom-call(f32[8,16,128]{2,1,0:T(8,128)S(1)} %all_to_all.21.parts, f32[8,24,128]{2,1,0:T(8,128)S(1)} %all_to_all.23.images, f32[6,24,24,256]{3,2,1,0:T(8,128)S(1)} %get-tuple-element.33.weights, s32[24,24,256]{2,1,0:T(8,128)S(1)} %get-tuple-element.34.labels, ...), custom_call_target="tpu_custom_call" | custom-call | tf_op jit(solution)/shard_map/pallas_call | solution.py:717
  (1 shorter events, 0.0 us)
Async XLA Ops:
  1.6 7.0 %collective-permute-start = (f32[5,8,128]{2,1,0:T(8,128)S(1)}, f32[5,8,128]{2,1,0:T(8,128)S(1)}, u32[]{:S(2)}, u32[]{:S(2)}) collective-permute-start(f32[5,8,128]{2,1,0:T(8,128)S(1)} %get-tuple-element.21), channel_id=1, source_target_pairs={{1,0},{2,1},{3,2},{5,4},{6,5},{7,6},{9,8},{10,9},{11,10},{13,12},{... | collective-permute-start | bytes 61448 | tf_op jit(solution)/shard_map/ppermute | solution.py:661
  2.9 6.6 %collective-permute-start.1 = (f32[5,8,128]{2,1,0:T(8,128)S(1)}, f32[5,8,128]{2,1,0:T(8,128)S(1)}, u32[]{:S(2)}, u32[]{:S(2)}) collective-permute-start(f32[5,8,128]{2,1,0:T(8,128)S(1)} %get-tuple-element.22), channel_id=1, source_target_pairs={{0,1},{1,2},{2,3},{4,5},{5,6},{6,7},{8,9},{9,10},{10,11},{12,13},{... | collective-permute-start | bytes 61448 | tf_op jit(solution)/shard_map/ppermute | solution.py:661
  9.5 4.8 %collective-permute-start.2 = (f32[25,8,128]{2,1,0:T(8,128)S(1)}, f32[25,8,128]{2,1,0:T(8,128)S(1)}, u32[]{:S(2)}, u32[]{:S(2)}) collective-permute-start(f32[25,8,128]{2,1,0:T(8,128)S(1)} %get-tuple-element.23), channel_id=1, source_target_pairs={{0,64},{64,128},{128,192},{192,256},{256,320},{320,384},{384,448},... | collective-permute-start | bytes 307208 | tf_op jit(solution)/shard_map/ppermute | solution.py:661
  12.7 5.4 %collective-permute-start.3 = (f32[25,8,128]{2,1,0:T(8,128)S(1)}, f32[25,8,128]{2,1,0:T(8,128)S(1)}, u32[]{:S(2)}, u32[]{:S(2)}) collective-permute-start(f32[25,8,128]{2,1,0:T(8,128)S(1)} %get-tuple-element.25), channel_id=1, source_target_pairs={{64,0},{128,64},{192,128},{256,192},{320,256},{384,320},{448,384},... | collective-permute-start | bytes 307208 | tf_op jit(solution)/shard_map/ppermute | solution.py:661
  18.2 8.1 %collective-permute-start.4 = (f32[53,8,128]{2,1,0:T(8,128)S(1)}, f32[53,8,128]{2,1,0:T(8,128)S(1)}, u32[]{:S(2)}, u32[]{:S(2)}) collective-permute-start(f32[53,8,128]{2,1,0:T(8,128)S(1)} %get-tuple-element.26), channel_id=1, source_target_pairs={{0,4},{4,8},{8,12},{12,16},{16,20},{20,24},{24,28},{28,32},{32,36}... | collective-permute-start | bytes 651272 | tf_op jit(solution)/shard_map/ppermute | solution.py:661
  23.4 5.6 %collective-permute-start.5 = (f32[53,8,128]{2,1,0:T(8,128)S(1)}, f32[53,8,128]{2,1,0:T(8,128)S(1)}, u32[]{:S(2)}, u32[]{:S(2)}) collective-permute-start(f32[53,8,128]{2,1,0:T(8,128)S(1)} %get-tuple-element.27), channel_id=1, source_target_pairs={{0,60},{4,0},{8,4},{12,8},{16,12},{20,16},{24,20},{28,24},{32,28},... | collective-permute-start | bytes 651272 | tf_op jit(solution)/shard_map/ppermute | solution.py:661

commit v9 on v8

--- a/solution.py
+++ b/solution.py
@@ -16,7 +16,6 @@
 NP = 3 * B
 W = 9
 FULL = (NP, 2 * LZ)
-FILL_UNROLL = 8
 CHUNK = 12
 fine_relax = 0.6666667
 coarse_relax = 0.7
@@ -248,7 +247,7 @@
                 sums[pl.ds(first + i * NSUB + s, 1), :] = jnp.sum(parts[0], axis=0, keepdims=True)
         return carry
 
-    lax.fori_loop(0, NSUB, one, 0, unroll=8)
+    lax.fori_loop(0, NSUB, one, 0, unroll=16)
 
 
 def three_parts(x):
@@ -332,7 +331,7 @@
             kext[p + 1, r, LZ:], labels[p, r, LZ:], _ = beyond(ty, p)
         return carry
 
-    lax.fori_loop(0, NP, fill, 0, unroll=FILL_UNROLL)
+    lax.fori_loop(0, NP, fill, 0, unroll=12)
     for p in range(NP):
         for ty in (0, 2):
             r = slice(ty * B, (ty + 1) * B)
@@ -353,20 +352,6 @@
     closed = ((lane_all == LZ - 1) & (col == n_col - 1)) | ((lane_all == 2 * LZ - 1) & (col == 0))
     masks[1] = jnp.where(closed, 0.0, 1.0)
 
-    def x_face(p, carry):
-        fx[p] = harmonic(kext[p], kext[p + 1])
-        return carry
-
-    lax.fori_loop(0, NP + 1, x_face, 0, unroll=5)
-
-    @pl.when(gx == 0)
-    def _():
-        fx[B] = kext[B + 1]
-
-    @pl.when(gx == n_gx - 1)
-    def _():
-        fx[2 * B] = kext[2 * B]
-
     def terms(p, carry):
         b = p // B
         out = ((b == 0) & (gx == 0)) | ((b == 2) & (gx == n_gx - 1))
@@ -375,16 +360,20 @@
         fy_down = pltpu.roll(fy_up, 1, 0)
         fz_right = harmonic(k, pltpu.roll(k, 2 * LZ - 1, 1)) * masks[1]
         fz_left = pltpu.roll(fz_right, 1, 1)
-        fx_up, fx_down = fx[p + 1], fx[p]
+        k_next = kext[p + 2]
+        fx_up = jnp.where((p == B - 1) & (gx == 0), k_next, harmonic(k, k_next))
+        fx_up = jnp.where((p == 2 * B - 1) & (gx == n_gx - 1), k, fx_up)
+        fx_down = carry
         diag = fx_up + fx_down + fy_up + fy_down + fz_right + fz_left
         scale = jnp.where(out, 0.0, fine_relax) / diag
         for i, face in enumerate((fx_up, fx_down, fy_up, fy_down, fz_right, fz_left)):
             weights[i, p] = face * scale
         both[0, p + 1] = scale
         dvals[p] = diag[B : 2 * B, 0:LZ]
-        return carry
-
-    lax.fori_loop(0, NP, terms, 0, unroll=8)
+        fx[p + 1] = fx_up
+        return fx_up
+
+    lax.fori_loop(0, NP, terms, harmonic(kext[0], kext[1]), unroll=8)
 
 
     def start(i, carry):
@@ -396,7 +385,7 @@
             both[1, p + 1, r, LZ:] = beyond(ty, p)[2] * over[r, LZ:]
         return carry
 
-    lax.fori_loop(0, 2 * B, start, 0, unroll=8)
+    lax.fori_loop(0, 2 * B, start, 0, unroll=16)
     for p in range(B // 2, NP - B // 2):
         for ty in (0, 2):
             r = slice(ty * B, (ty + 1) * B)

time: 110 us -> 109 us (level)
  no operation moved by 1% of the time
where the time goes in v9:
time: 109 us
  blocking collectives  65.4 us (60%)
  starting transfers between devices  17.9 us (16%)
  Pallas kernels  15.4 us (14%)
  waiting for transfers between devices  9.08 us (8%)
    all_to_all x1, blocking collectives, on_device(): bricks = lax.all_to_all(chunk, ('gy', 'col'), 0, 0, tiled=True)  28.6 us
    all_to_all x1, blocking collectives, on_device(): images = lax.all_to_all(chunk, ('gy', 'col'), 0, 0, tiled=True)  18.2 us
    ppermute x6, starting transfers between devices, send(): return lax.ppermute(x, axis, steps(lax.axis_size(axis), by, wrap))  17.9 us
    all_to_all x1, blocking collectives, on_device(): parts = lax.all_to_all(parts, 'gx', 0, 0, tiled=True)  10.9 us
    ppermute x6, waiting for transfers between devices, send(): return lax.ppermute(x, axis, steps(lax.axis_size(axis), by, wrap))  9.08 us
    all_to_all x1, blocking collectives, on_device(): images = lax.all_to_all(images, 'gx', 0, 0, tiled=True)  7.68 us
    pallas_call x1, Pallas kernels, on_device(): call(functools.partial(second_sums, *sizes), sds(n_bricks, 4, LZ), 6, scr...  6.03 us
    pallas_call x1, Pallas kernels, on_device(): call(functools.partial(first_sums, *sizes), [sds(6, NP, *FULL), sds(NP, *...  3.41 us
  transfers between devices with their start and end apart: 6, of which 5 were waited for; matrix products, arithmetic and copies ran while one was open for 0% of the time, Pallas kernels for 0%

profile of v9, /device:TPU:1, one launch (start us, length us, event | category | flops | bytes accessed | tf_op | source)
XLA Modules:
  0.0 108.5 jit_solution(7902756835146160891)
XLA Ops:
  0.6 1.0 shard_map.68
  1.6 1.3 %collective-permute-start = (f32[5,8,128]{2,1,0:T(8,128)S(1)}, f32[5,8,128]{2,1,0:T(8,128)S(1)}, u32[]{:S(2)}, u32[]{:S(2)}) collective-permute-start(f32[5,8,128]{2,1,0:T(8,128)S(1)} %get-tuple-element.21), channel_id=1, source_target_pairs={{1,0},{2,1},{3,2},{5,4},{6,5},{7,6},{9,8},{10,9},{11,10},{13,12},{... | collective-permute-start | bytes 61448 | tf_op jit(solution)/shard_map/ppermute | solution.py:650
  2.9 5.7 %collective-permute-start.1 = (f32[5,8,128]{2,1,0:T(8,128)S(1)}, f32[5,8,128]{2,1,0:T(8,128)S(1)}, u32[]{:S(2)}, u32[]{:S(2)}) collective-permute-start(f32[5,8,128]{2,1,0:T(8,128)S(1)} %get-tuple-element.22), channel_id=1, source_target_pairs={{0,1},{1,2},{2,3},{4,5},{5,6},{6,7},{8,9},{9,10},{10,11},{12,13},{... | collective-permute-start | bytes 61448 | tf_op jit(solution)/shard_map/ppermute | solution.py:650
  8.6 0.0 collective-permute-done.mr
  8.6 0.9 collective-permute-done.1.ml
  9.5 3.2 %collective-permute-start.2 = (f32[25,8,128]{2,1,0:T(8,128)S(1)}, f32[25,8,128]{2,1,0:T(8,128)S(1)}, u32[]{:S(2)}, u32[]{:S(2)}) collective-permute-start(f32[25,8,128]{2,1,0:T(8,128)S(1)} %get-tuple-element.23), channel_id=1, source_target_pairs={{0,64},{64,128},{128,192},{192,256},{256,320},{320,384},{384,448},... | collective-permute-start | bytes 307208 | tf_op jit(solution)/shard_map/ppermute | solution.py:650
  12.7 1.3 %collective-permute-start.3 = (f32[25,8,128]{2,1,0:T(8,128)S(1)}, f32[25,8,128]{2,1,0:T(8,128)S(1)}, u32[]{:S(2)}, u32[]{:S(2)}) collective-permute-start(f32[25,8,128]{2,1,0:T(8,128)S(1)} %get-tuple-element.25), channel_id=1, source_target_pairs={{64,0},{128,64},{192,128},{256,192},{320,256},{384,320},{448,384},... | collective-permute-start | bytes 307208 | tf_op jit(solution)/shard_map/ppermute | solution.py:650
  14.0 0.4 collective-permute-done.2.low
  14.4 3.7 %collective-permute-done.3.high = f32[25,8,128]{2,1,0:T(8,128)S(1)} collective-permute-done((f32[25,8,128]{2,1,0:T(8,128)S(1)}, f32[25,8,128]{2,1,0:T(8,128)S(1)}, u32[]{:S(2)}, u32[]{:S(2)}) %collective-permute-start.3) | collective-permute-done | bytes 102432 | tf_op jit(solution)/shard_map/ppermute | solution.py:650
  18.1 0.1 shard_map.70
  18.2 5.2 %collective-permute-start.4 = (f32[53,8,128]{2,1,0:T(8,128)S(1)}, f32[53,8,128]{2,1,0:T(8,128)S(1)}, u32[]{:S(2)}, u32[]{:S(2)}) collective-permute-start(f32[53,8,128]{2,1,0:T(8,128)S(1)} %get-tuple-element.26), channel_id=1, source_target_pairs={{0,4},{4,8},{8,12},{12,16},{16,20},{20,24},{24,28},{28,32},{32,36}... | collective-permute-start | bytes 651272 | tf_op jit(solution)/shard_map/ppermute | solution.py:650
  23.4 1.3 %collective-permute-start.5 = (f32[53,8,128]{2,1,0:T(8,128)S(1)}, f32[53,8,128]{2,1,0:T(8,128)S(1)}, u32[]{:S(2)}, u32[]{:S(2)}) collective-permute-start(f32[53,8,128]{2,1,0:T(8,128)S(1)} %get-tuple-element.27), channel_id=1, source_target_pairs={{0,60},{4,0},{8,4},{12,8},{16,12},{20,16},{24,20},{28,24},{32,28},... | collective-permute-start | bytes 651272 | tf_op jit(solution)/shard_map/ppermute | solution.py:650
  24.7 0.2 shard_map.71
  24.9 1.3 %collective-permute-done.4.below = f32[53,8,128]{2,1,0:T(8,128)S(1)} collective-permute-done((f32[53,8,128]{2,1,0:T(8,128)S(1)}, f32[53,8,128]{2,1,0:T(8,128)S(1)}, u32[]{:S(2)}, u32[]{:S(2)}) %collective-permute-start.4) | collective-permute-done | bytes 217120 | tf_op jit(solution)/shard_map/ppermute | solution.py:650
  26.2 2.8 %collective-permute-done.5.above = f32[53,8,128]{2,1,0:T(8,128)S(1)} collective-permute-done((f32[53,8,128]{2,1,0:T(8,128)S(1)}, f32[53,8,128]{2,1,0:T(8,128)S(1)}, u32[]{:S(2)}, u32[]{:S(2)}) %collective-permute-start.5) | collective-permute-done | bytes 217120 | tf_op jit(solution)/shard_map/ppermute | solution.py:650
  29.0 3.4 %shard_map.72 = (f32[6,24,24,256]{3,2,1,0:T(8,128)S(1)}, s32[24,24,256]{2,1,0:T(8,128)S(1)}, f32[64,2,128]{2,1,0:T(2,128)S(1)}, f32[24,8,128]{2,1,0:T(8,128)S(1)...) custom-call(f32[25,8,128]{2,1,0:T(8,128)S(1)} %collective-permute-done.2.low, ...), custom_call_target="tpu_custom_call" | custom-call | tf_op jit(solution)/shard_map/pallas_call | solution.py:677
  32.4 28.6 %all_to_all.20.values.first = f32[64,2,128]{2,1,0:T(2,128)S(1)} all-to-all(f32[64,2,128]{2,1,0:T(2,128)S(1)} %get-tuple-element.32), channel_id=1, replica_groups=mesh['gx'=8,'gy'=16,'col'=4] {'gy','col'}, dimensions={0} | all-to-all | bytes 131072 | tf_op jit(solution)/shard_map/all_to_all | solution.py:689
  61.1 0.7 shard_map.73
  61.8 10.9 %all_to_all.21.parts = f32[8,16,128]{2,1,0:T(8,128)S(1)} all-to-all(f32[8,16,128]{2,1,0:T(8,128)S(1)} %shard_map.73), channel_id=1, replica_groups=mesh['gx'=8,'gy'=16,'col'=4] {'gx'}, dimensions={0} | all-to-all | bytes 131072 | tf_op jit(solution)/shard_map/all_to_all | solution.py:693
  72.7 6.0 %shard_map.74 = f32[64,4,128]{2,1,0:T(4,128)S(1)} custom-call(f32[8,16,128]{2,1,0:T(8,128)S(1)} %all_to_all.21.parts, f32[6,24,24,256]{3,2,1,0:T(8,128)S(1)} %get-tuple-element.33.weights, s32[24,24,256]{2,1,0:T(8,128)S(1)} %get-tuple-element.34.labels, s32[3,3,8,128]{3,2,1,0:T(8,128)S(1)} %get-tuple-element.35.asg, ...), custom_call_target="tpu_custom_call" | custom-call | tf_op jit(solution)/shard_map/pallas_call | solution.py:695
  78.8 18.2 %all_to_all.22.values = f32[64,4,128]{2,1,0:T(4,128)S(1)} all-to-all(f32[64,4,128]{2,1,0:T(4,128)S(1)} %shard_map.74), channel_id=1, replica_groups=mesh['gx'=8,'gy'=16,'col'=4] {'gy','col'}, dimensions={0} | all-to-all | bytes 262144 | tf_op jit(solution)/shard_map/all_to_all | solution.py:701
  97.0 1.1 %shard_map.75 = f32[8,24,128]{2,1,0:T(8,128)S(1)} custom-call(f32[64,4,128]{2,1,0:T(4,128)S(1)} %all_to_all.22.values, f32[64,2,128]{2,1,0:T(2,128)S(1)} %all_to_all.20.values.first), custom_call_target="tpu_custom_call" | custom-call | tf_op jit(solution)/shard_map/pallas_call | solution.py:702
  98.0 7.7 %all_to_all.23.images = f32[8,24,128]{2,1,0:T(8,128)S(1)} all-to-all(f32[8,24,128]{2,1,0:T(8,128)S(1)} %shard_map.75), channel_id=1, replica_groups=mesh['gx'=8,'gy'=16,'col'=4] {'gx'}, dimensions={0} | all-to-all | bytes 196608 | tf_op jit(solution)/shard_map/all_to_all | solution.py:705
  105.7 2.8 %shard_map.76 = (f32[8,8,128]{2,1,0:T(8,128)}, f32[1,16]{1,0:T(1,128)}) custom-call(f32[8,16,128]{2,1,0:T(8,128)S(1)} %all_to_all.21.parts, f32[8,24,128]{2,1,0:T(8,128)S(1)} %all_to_all.23.images, f32[6,24,24,256]{3,2,1,0:T(8,128)S(1)} %get-tuple-element.33.weights, s32[24,24,256]{2,1,0:T(8,128)S(1)} %get-tuple-element.34.labels, ...), custom_call_target="tpu_custom_call" | custom-call | tf_op jit(solution)/shard_map/pallas_call | solution.py:706
  (1 shorter events, 0.0 us)
Async XLA Ops:
  1.6 7.0 %collective-permute-start = (f32[5,8,128]{2,1,0:T(8,128)S(1)}, f32[5,8,128]{2,1,0:T(8,128)S(1)}, u32[]{:S(2)}, u32[]{:S(2)}) collective-permute-start(f32[5,8,128]{2,1,0:T(8,128)S(1)} %get-tuple-element.21), channel_id=1, source_target_pairs={{1,0},{2,1},{3,2},{5,4},{6,5},{7,6},{9,8},{10,9},{11,10},{13,12},{... | collective-permute-start | bytes 61448 | tf_op jit(solution)/shard_map/ppermute | solution.py:650
  2.9 6.6 %collective-permute-start.1 = (f32[5,8,128]{2,1,0:T(8,128)S(1)}, f32[5,8,128]{2,1,0:T(8,128)S(1)}, u32[]{:S(2)}, u32[]{:S(2)}) collective-permute-start(f32[5,8,128]{2,1,0:T(8,128)S(1)} %get-tuple-element.22), channel_id=1, source_target_pairs={{0,1},{1,2},{2,3},{4,5},{5,6},{6,7},{8,9},{9,10},{10,11},{12,13},{... | collective-permute-start | bytes 61448 | tf_op jit(solution)/shard_map/ppermute | solution.py:650
  9.5 4.8 %collective-permute-start.2 = (f32[25,8,128]{2,1,0:T(8,128)S(1)}, f32[25,8,128]{2,1,0:T(8,128)S(1)}, u32[]{:S(2)}, u32[]{:S(2)}) collective-permute-start(f32[25,8,128]{2,1,0:T(8,128)S(1)} %get-tuple-element.23), channel_id=1, source_target_pairs={{0,64},{64,128},{128,192},{192,256},{256,320},{320,384},{384,448},... | collective-permute-start | bytes 307208 | tf_op jit(solution)/shard_map/ppermute | solution.py:650
  12.7 5.4 %collective-permute-start.3 = (f32[25,8,128]{2,1,0:T(8,128)S(1)}, f32[25,8,128]{2,1,0:T(8,128)S(1)}, u32[]{:S(2)}, u32[]{:S(2)}) collective-permute-start(f32[25,8,128]{2,1,0:T(8,128)S(1)} %get-tuple-element.25), channel_id=1, source_target_pairs={{64,0},{128,64},{192,128},{256,192},{320,256},{384,320},{448,384},... | collective-permute-start | bytes 307208 | tf_op jit(solution)/shard_map/ppermute | solution.py:650
  18.2 8.1 %collective-permute-start.4 = (f32[53,8,128]{2,1,0:T(8,128)S(1)}, f32[53,8,128]{2,1,0:T(8,128)S(1)}, u32[]{:S(2)}, u32[]{:S(2)}) collective-permute-start(f32[53,8,128]{2,1,0:T(8,128)S(1)} %get-tuple-element.26), channel_id=1, source_target_pairs={{0,4},{4,8},{8,12},{12,16},{16,20},{20,24},{24,28},{28,32},{32,36}... | collective-permute-start | bytes 651272 | tf_op jit(solution)/shard_map/ppermute | solution.py:650
  23.4 5.6 %collective-permute-start.5 = (f32[53,8,128]{2,1,0:T(8,128)S(1)}, f32[53,8,128]{2,1,0:T(8,128)S(1)}, u32[]{:S(2)}, u32[]{:S(2)}) collective-permute-start(f32[53,8,128]{2,1,0:T(8,128)S(1)} %get-tuple-element.27), channel_id=1, source_target_pairs={{0,60},{4,0},{8,4},{12,8},{16,12},{20,16},{24,20},{28,24},{32,28},... | collective-permute-start | bytes 651272 | tf_op jit(solution)/shard_map/ppermute | solution.py:650

commit v10 on v9

--- a/solution.py
+++ b/solution.py
@@ -251,17 +251,19 @@
 
 
 def three_parts(x):
-    l1 = x.astype(bf16)
-    rest = x - l1.astype(f32)
-    l2 = rest.astype(bf16)
-    return l1, l2, (rest - l2.astype(f32)).astype(bf16)
+    high = x.astype(bf16).astype(f32)
+    rest = x - high
+    middle = rest.astype(bf16).astype(f32)
+    return high, middle, rest - middle
 
 
 def lane_sums(sums):
-    return lax.dot_general(
-        jnp.ones((B, 3 * LZ), bf16), jnp.concatenate(three_parts(sums), axis=1),
+    parts = jnp.concatenate(three_parts(sums), axis=1).astype(bf16)
+    total = lax.dot_general(
+        jnp.ones((2 * B, 3 * LZ), bf16), parts,
         (((1,), (1,)), ((), ())), preferred_element_type=f32,
     )
+    return total[0:B]
 
 
 def harmonic(a, b):
@@ -435,15 +437,17 @@
         ],
         axis=1,
     )
+    parts = three_parts(left)
+    if left.shape[0] % (2 * B):
+        parts += (jnp.zeros_like(left),)
     return lax.dot_general(
-        jnp.concatenate(three_parts(left), axis=0), right, (((1,), (1,)), ((), ())),
+        jnp.concatenate(parts, axis=0).astype(bf16), right, (((1,), (1,)), ((), ())),
         preferred_element_type=f32,
     )
 
 
-def joined(total):
-    n = total.shape[0] // 3
-    return (total[2 * n :] + total[n : 2 * n]) + total[:n]
+def joined(total, n):
+    return (total[2 * n : 3 * n] + total[n : 2 * n]) + total[:n]
 
 
 def halves(value, high):
@@ -468,7 +472,7 @@
         return total + one_hot_product(lefts, lows)
 
     total = lax.fori_loop(0, n_bricks // min(GROUP, n_bricks), one, jnp.zeros((6 * B, LZ), f32))
-    total = joined(total)
+    total = joined(total, 2 * B)
     for d in range(n_out):
         out[d] = total
 
@@ -502,9 +506,9 @@
         )
 
     mine, edges = lax.fori_loop(
-        0, n_bricks // min(GROUP, n_bricks), one, (jnp.zeros((3 * B, LZ), f32), jnp.zeros((6 * B, LZ), f32))
-    )
-    total = jnp.concatenate([joined(mine), joined(edges)], axis=0)
+        0, n_bricks // min(GROUP, n_bricks), one, (jnp.zeros((4 * B, LZ), f32), jnp.zeros((6 * B, LZ), f32))
+    )
+    total = jnp.concatenate([joined(mine, B), joined(edges, 2 * B)], axis=0)
     for d in range(n_out):
         out[d] = total
 

time: 109 us -> 109 us (level)
  no operation moved by 1% of the time
where the time goes in v10:
time: 109 us
  blocking collectives  65.4 us (60%)
  starting transfers between devices  17.9 us (16%)
  Pallas kernels  15.4 us (14%)
  waiting for transfers between devices  9.08 us (8%)
    all_to_all x1, blocking collectives, on_device(): bricks = lax.all_to_all(chunk, ('gy', 'col'), 0, 0, tiled=True)  28.6 us
    all_to_all x1, blocking collectives, on_device(): images = lax.all_to_all(chunk, ('gy', 'col'), 0, 0, tiled=True)  18.2 us
    ppermute x6, starting transfers between devices, send(): return lax.ppermute(x, axis, steps(lax.axis_size(axis), by, wrap))  17.9 us
    all_to_all x1, blocking collectives, on_device(): parts = lax.all_to_all(parts, 'gx', 0, 0, tiled=True)  10.9 us
    ppermute x6, waiting for transfers between devices, send(): return lax.ppermute(x, axis, steps(lax.axis_size(axis), by, wrap))  9.08 us
    all_to_all x1, blocking collectives, on_device(): images = lax.all_to_all(images, 'gx', 0, 0, tiled=True)  7.68 us
    pallas_call x1, Pallas kernels, on_device(): call(functools.partial(second_sums, *sizes), sds(n_bricks, 4, LZ), 6, scr...  6.03 us
    pallas_call x1, Pallas kernels, on_device(): call(functools.partial(first_sums, *sizes), [sds(6, NP, *FULL), sds(NP, *...  3.41 us
  transfers between devices with their start and end apart: 6, of which 5 were waited for; matrix products, arithmetic and copies ran while one was open for 0% of the time, Pallas kernels for 0%

profile of v10, /device:TPU:1, one launch (start us, length us, event | category | flops | bytes accessed | tf_op | source)
XLA Modules:
  0.0 108.5 jit_solution(9538521741465375465)
XLA Ops:
  0.6 1.0 shard_map.68
  1.6 1.3 %collective-permute-start = (f32[5,8,128]{2,1,0:T(8,128)S(1)}, f32[5,8,128]{2,1,0:T(8,128)S(1)}, u32[]{:S(2)}, u32[]{:S(2)}) collective-permute-start(f32[5,8,128]{2,1,0:T(8,128)S(1)} %get-tuple-element.21), channel_id=1, source_target_pairs={{1,0},{2,1},{3,2},{5,4},{6,5},{7,6},{9,8},{10,9},{11,10},{13,12},{... | collective-permute-start | bytes 61448 | tf_op jit(solution)/shard_map/ppermute | solution.py:654
  2.9 5.7 %collective-permute-start.1 = (f32[5,8,128]{2,1,0:T(8,128)S(1)}, f32[5,8,128]{2,1,0:T(8,128)S(1)}, u32[]{:S(2)}, u32[]{:S(2)}) collective-permute-start(f32[5,8,128]{2,1,0:T(8,128)S(1)} %get-tuple-element.22), channel_id=1, source_target_pairs={{0,1},{1,2},{2,3},{4,5},{5,6},{6,7},{8,9},{9,10},{10,11},{12,13},{... | collective-permute-start | bytes 61448 | tf_op jit(solution)/shard_map/ppermute | solution.py:654
  8.6 0.0 collective-permute-done.mr
  8.6 0.9 collective-permute-done.1.ml
  9.5 3.2 %collective-permute-start.2 = (f32[25,8,128]{2,1,0:T(8,128)S(1)}, f32[25,8,128]{2,1,0:T(8,128)S(1)}, u32[]{:S(2)}, u32[]{:S(2)}) collective-permute-start(f32[25,8,128]{2,1,0:T(8,128)S(1)} %get-tuple-element.23), channel_id=1, source_target_pairs={{0,64},{64,128},{128,192},{192,256},{256,320},{320,384},{384,448},... | collective-permute-start | bytes 307208 | tf_op jit(solution)/shard_map/ppermute | solution.py:654
  12.7 1.3 %collective-permute-start.3 = (f32[25,8,128]{2,1,0:T(8,128)S(1)}, f32[25,8,128]{2,1,0:T(8,128)S(1)}, u32[]{:S(2)}, u32[]{:S(2)}) collective-permute-start(f32[25,8,128]{2,1,0:T(8,128)S(1)} %get-tuple-element.25), channel_id=1, source_target_pairs={{64,0},{128,64},{192,128},{256,192},{320,256},{384,320},{448,384},... | collective-permute-start | bytes 307208 | tf_op jit(solution)/shard_map/ppermute | solution.py:654
  14.0 0.4 collective-permute-done.2.low
  14.4 3.7 %collective-permute-done.3.high = f32[25,8,128]{2,1,0:T(8,128)S(1)} collective-permute-done((f32[25,8,128]{2,1,0:T(8,128)S(1)}, f32[25,8,128]{2,1,0:T(8,128)S(1)}, u32[]{:S(2)}, u32[]{:S(2)}) %collective-permute-start.3) | collective-permute-done | bytes 102432 | tf_op jit(solution)/shard_map/ppermute | solution.py:654
  18.1 0.1 shard_map.70
  18.2 5.2 %collective-permute-start.4 = (f32[53,8,128]{2,1,0:T(8,128)S(1)}, f32[53,8,128]{2,1,0:T(8,128)S(1)}, u32[]{:S(2)}, u32[]{:S(2)}) collective-permute-start(f32[53,8,128]{2,1,0:T(8,128)S(1)} %get-tuple-element.26), channel_id=1, source_target_pairs={{0,4},{4,8},{8,12},{12,16},{16,20},{20,24},{24,28},{28,32},{32,36}... | collective-permute-start | bytes 651272 | tf_op jit(solution)/shard_map/ppermute | solution.py:654
  23.4 1.3 %collective-permute-start.5 = (f32[53,8,128]{2,1,0:T(8,128)S(1)}, f32[53,8,128]{2,1,0:T(8,128)S(1)}, u32[]{:S(2)}, u32[]{:S(2)}) collective-permute-start(f32[53,8,128]{2,1,0:T(8,128)S(1)} %get-tuple-element.27), channel_id=1, source_target_pairs={{0,60},{4,0},{8,4},{12,8},{16,12},{20,16},{24,20},{28,24},{32,28},... | collective-permute-start | bytes 651272 | tf_op jit(solution)/shard_map/ppermute | solution.py:654
  24.7 0.2 shard_map.71
  24.9 1.3 %collective-permute-done.4.below = f32[53,8,128]{2,1,0:T(8,128)S(1)} collective-permute-done((f32[53,8,128]{2,1,0:T(8,128)S(1)}, f32[53,8,128]{2,1,0:T(8,128)S(1)}, u32[]{:S(2)}, u32[]{:S(2)}) %collective-permute-start.4) | collective-permute-done | bytes 217120 | tf_op jit(solution)/shard_map/ppermute | solution.py:654
  26.2 2.8 %collective-permute-done.5.above = f32[53,8,128]{2,1,0:T(8,128)S(1)} collective-permute-done((f32[53,8,128]{2,1,0:T(8,128)S(1)}, f32[53,8,128]{2,1,0:T(8,128)S(1)}, u32[]{:S(2)}, u32[]{:S(2)}) %collective-permute-start.5) | collective-permute-done | bytes 217120 | tf_op jit(solution)/shard_map/ppermute | solution.py:654
  29.0 3.4 %shard_map.72 = (f32[6,24,24,256]{3,2,1,0:T(8,128)S(1)}, s32[24,24,256]{2,1,0:T(8,128)S(1)}, f32[64,2,128]{2,1,0:T(2,128)S(1)}, f32[24,8,128]{2,1,0:T(8,128)S(1)...) custom-call(f32[25,8,128]{2,1,0:T(8,128)S(1)} %collective-permute-done.2.low, ...), custom_call_target="tpu_custom_call" | custom-call | tf_op jit(solution)/shard_map/pallas_call | solution.py:681
  32.4 28.6 %all_to_all.20.values.first = f32[64,2,128]{2,1,0:T(2,128)S(1)} all-to-all(f32[64,2,128]{2,1,0:T(2,128)S(1)} %get-tuple-element.32), channel_id=1, replica_groups=mesh['gx'=8,'gy'=16,'col'=4] {'gy','col'}, dimensions={0} | all-to-all | bytes 131072 | tf_op jit(solution)/shard_map/all_to_all | solution.py:693
  61.1 0.7 shard_map.73
  61.8 10.9 %all_to_all.21.parts = f32[8,16,128]{2,1,0:T(8,128)S(1)} all-to-all(f32[8,16,128]{2,1,0:T(8,128)S(1)} %shard_map.73), channel_id=1, replica_groups=mesh['gx'=8,'gy'=16,'col'=4] {'gx'}, dimensions={0} | all-to-all | bytes 131072 | tf_op jit(solution)/shard_map/all_to_all | solution.py:697
  72.7 6.0 %shard_map.74 = f32[64,4,128]{2,1,0:T(4,128)S(1)} custom-call(f32[8,16,128]{2,1,0:T(8,128)S(1)} %all_to_all.21.parts, f32[6,24,24,256]{3,2,1,0:T(8,128)S(1)} %get-tuple-element.33.weights, s32[24,24,256]{2,1,0:T(8,128)S(1)} %get-tuple-element.34.labels, s32[3,3,8,128]{3,2,1,0:T(8,128)S(1)} %get-tuple-element.35.asg, ...), custom_call_target="tpu_custom_call" | custom-call | tf_op jit(solution)/shard_map/pallas_call | solution.py:699
  78.8 18.2 %all_to_all.22.values = f32[64,4,128]{2,1,0:T(4,128)S(1)} all-to-all(f32[64,4,128]{2,1,0:T(4,128)S(1)} %shard_map.74), channel_id=1, replica_groups=mesh['gx'=8,'gy'=16,'col'=4] {'gy','col'}, dimensions={0} | all-to-all | bytes 262144 | tf_op jit(solution)/shard_map/all_to_all | solution.py:705
  97.0 1.1 %shard_map.75 = f32[8,24,128]{2,1,0:T(8,128)S(1)} custom-call(f32[64,4,128]{2,1,0:T(4,128)S(1)} %all_to_all.22.values, f32[64,2,128]{2,1,0:T(2,128)S(1)} %all_to_all.20.values.first), custom_call_target="tpu_custom_call" | custom-call | tf_op jit(solution)/shard_map/pallas_call | solution.py:706
  98.1 7.7 %all_to_all.23.images = f32[8,24,128]{2,1,0:T(8,128)S(1)} all-to-all(f32[8,24,128]{2,1,0:T(8,128)S(1)} %shard_map.75), channel_id=1, replica_groups=mesh['gx'=8,'gy'=16,'col'=4] {'gx'}, dimensions={0} | all-to-all | bytes 196608 | tf_op jit(solution)/shard_map/all_to_all | solution.py:709
  105.7 2.8 %shard_map.76 = (f32[8,8,128]{2,1,0:T(8,128)}, f32[1,16]{1,0:T(1,128)}) custom-call(f32[8,16,128]{2,1,0:T(8,128)S(1)} %all_to_all.21.parts, f32[8,24,128]{2,1,0:T(8,128)S(1)} %all_to_all.23.images, f32[6,24,24,256]{3,2,1,0:T(8,128)S(1)} %get-tuple-element.33.weights, s32[24,24,256]{2,1,0:T(8,128)S(1)} %get-tuple-element.34.labels, ...), custom_call_target="tpu_custom_call" | custom-call | tf_op jit(solution)/shard_map/pallas_call | solution.py:710
  (1 shorter events, 0.0 us)
Async XLA Ops:
  1.6 7.0 %collective-permute-start = (f32[5,8,128]{2,1,0:T(8,128)S(1)}, f32[5,8,128]{2,1,0:T(8,128)S(1)}, u32[]{:S(2)}, u32[]{:S(2)}) collective-permute-start(f32[5,8,128]{2,1,0:T(8,128)S(1)} %get-tuple-element.21), channel_id=1, source_target_pairs={{1,0},{2,1},{3,2},{5,4},{6,5},{7,6},{9,8},{10,9},{11,10},{13,12},{... | collective-permute-start | bytes 61448 | tf_op jit(solution)/shard_map/ppermute | solution.py:654
  2.9 6.6 %collective-permute-start.1 = (f32[5,8,128]{2,1,0:T(8,128)S(1)}, f32[5,8,128]{2,1,0:T(8,128)S(1)}, u32[]{:S(2)}, u32[]{:S(2)}) collective-permute-start(f32[5,8,128]{2,1,0:T(8,128)S(1)} %get-tuple-element.22), channel_id=1, source_target_pairs={{0,1},{1,2},{2,3},{4,5},{5,6},{6,7},{8,9},{9,10},{10,11},{12,13},{... | collective-permute-start | bytes 61448 | tf_op jit(solution)/shard_map/ppermute | solution.py:654
  9.5 4.8 %collective-permute-start.2 = (f32[25,8,128]{2,1,0:T(8,128)S(1)}, f32[25,8,128]{2,1,0:T(8,128)S(1)}, u32[]{:S(2)}, u32[]{:S(2)}) collective-permute-start(f32[25,8,128]{2,1,0:T(8,128)S(1)} %get-tuple-element.23), channel_id=1, source_target_pairs={{0,64},{64,128},{128,192},{192,256},{256,320},{320,384},{384,448},... | collective-permute-start | bytes 307208 | tf_op jit(solution)/shard_map/ppermute | solution.py:654
  12.7 5.4 %collective-permute-start.3 = (f32[25,8,128]{2,1,0:T(8,128)S(1)}, f32[25,8,128]{2,1,0:T(8,128)S(1)}, u32[]{:S(2)}, u32[]{:S(2)}) collective-permute-start(f32[25,8,128]{2,1,0:T(8,128)S(1)} %get-tuple-element.25), channel_id=1, source_target_pairs={{64,0},{128,64},{192,128},{256,192},{320,256},{384,320},{448,384},... | collective-permute-start | bytes 307208 | tf_op jit(solution)/shard_map/ppermute | solution.py:654
  18.2 8.1 %collective-permute-start.4 = (f32[53,8,128]{2,1,0:T(8,128)S(1)}, f32[53,8,128]{2,1,0:T(8,128)S(1)}, u32[]{:S(2)}, u32[]{:S(2)}) collective-permute-start(f32[53,8,128]{2,1,0:T(8,128)S(1)} %get-tuple-element.26), channel_id=1, source_target_pairs={{0,4},{4,8},{8,12},{12,16},{16,20},{20,24},{24,28},{28,32},{32,36}... | collective-permute-start | bytes 651272 | tf_op jit(solution)/shard_map/ppermute | solution.py:654
  23.4 5.6 %collective-permute-start.5 = (f32[53,8,128]{2,1,0:T(8,128)S(1)}, f32[53,8,128]{2,1,0:T(8,128)S(1)}, u32[]{:S(2)}, u32[]{:S(2)}) collective-permute-start(f32[53,8,128]{2,1,0:T(8,128)S(1)} %get-tuple-element.27), channel_id=1, source_target_pairs={{0,60},{4,0},{8,4},{12,8},{16,12},{20,16},{24,20},{28,24},{32,28},... | collective-permute-start | bytes 651272 | tf_op jit(solution)/shard_map/ppermute | solution.py:654

commit v11 on v10

--- a/solution.py
+++ b/solution.py
@@ -195,7 +195,7 @@
     )
 
 
-def sweeps(both, w_ref, first, last, after=None, operator_at=-1):
+def sweeps(both, w_ref, first, last, after=None, operator_at=-1, size=CHUNK):
     def one_sweep(k, carry):
         now = lax.rem(k, 2)
         src, dst = both.at[now], both.at[1 - now]
@@ -204,16 +204,16 @@
         give = jnp.where(k == operator_at, -1.0 / fine_relax, 1.0)
 
         def chunk(i, carry):
-            start = jnp.minimum(k + CHUNK * i, k + count - CHUNK)
+            start = jnp.minimum(k + size * i, k + count - size)
             moved = []
-            for j in range(CHUNK):
+            for j in range(size):
                 u, near = around(src, w_ref, start + j)
                 moved.append(keep * u + give * near)
-            for j in range(CHUNK):
+            for j in range(size):
                 dst[start + j + 1] = moved[j]
             return carry
 
-        lax.fori_loop(0, (count + CHUNK - 1) // CHUNK, chunk, 0)
+        lax.fori_loop(0, (count + size - 1) // size, chunk, 0)
         if after is not None:
             after(k)
         return carry
@@ -413,7 +413,7 @@
     paths[0] = rise
     paths[1] = fall
 
-    sweeps(both, weights, 5, 7)
+    sweeps(both, weights, 5, 7, size=NP - 10)
     tiles = [own_tile(both.at[0], weights, B + q) * dvals[B + q] for q in range(B)]
     diag_tiles = [dvals[B + q] for q in range(B)]
     label_tiles = [labels[B + q, B : 2 * B, 0:LZ] for q in range(B)]
@@ -632,7 +632,7 @@
     turned = pltpu.roll(spread(row), lax.rem(LZ - lax.rem(mine, per_row) * share, LZ), 1)
     coarse_out[...] = turned[0:1, 0:share]
     expand(coarse, asg, labels, both.at[1], tables, 4, 19)
-    sweeps(both, weights, 5, 7)
+    sweeps(both, weights, 5, 7, size=NP - 10)
     for q in range(B):
         pressure[q] = own_tile(both.at[0], weights, B + q)
 

time: 109 us -> 109 us (level)
  no operation moved by 1% of the time
where the time goes in v11:
time: 109 us; the launch traced here: 108 us
  blocking collectives  65.4 us (60%)
  starting transfers between devices  17.9 us (16%)
  Pallas kernels  15.1 us (14%)
  waiting for transfers between devices  9.08 us (8%)
    all_to_all x1, blocking collectives, on_device(): bricks = lax.all_to_all(chunk, ('gy', 'col'), 0, 0, tiled=True)  28.6 us
    all_to_all x1, blocking collectives, on_device(): images = lax.all_to_all(chunk, ('gy', 'col'), 0, 0, tiled=True)  18.2 us
    ppermute x6, starting transfers between devices, send(): return lax.ppermute(x, axis, steps(lax.axis_size(axis), by, wrap))  17.9 us
    all_to_all x1, blocking collectives, on_device(): parts = lax.all_to_all(parts, 'gx', 0, 0, tiled=True)  10.9 us
    ppermute x6, waiting for transfers between devices, send(): return lax.ppermute(x, axis, steps(lax.axis_size(axis), by, wrap))  9.08 us
    all_to_all x1, blocking collectives, on_device(): images = lax.all_to_all(images, 'gx', 0, 0, tiled=True)  7.68 us
    pallas_call x1, Pallas kernels, on_device(): call(functools.partial(second_sums, *sizes), sds(n_bricks, 4, LZ), 6, scr...  6.03 us
    pallas_call x1, Pallas kernels, on_device(): call(functools.partial(first_sums, *sizes), [sds(6, NP, *FULL), sds(NP, *...  3.25 us
  transfers between devices with their start and end apart: 6, of which 5 were waited for; matrix products, arithmetic and copies ran while one was open for 0% of the time, Pallas kernels for 0%

profile of v11, /device:TPU:1, one launch (start us, length us, event | category | flops | bytes accessed | tf_op | source)
XLA Modules:
  0.0 108.2 jit_solution(9747328987988797470)
XLA Ops:
  0.6 1.0 shard_map.68
  1.6 1.3 %collective-permute-start = (f32[5,8,128]{2,1,0:T(8,128)S(1)}, f32[5,8,128]{2,1,0:T(8,128)S(1)}, u32[]{:S(2)}, u32[]{:S(2)}) collective-permute-start(f32[5,8,128]{2,1,0:T(8,128)S(1)} %get-tuple-element.21), channel_id=1, source_target_pairs={{1,0},{2,1},{3,2},{5,4},{6,5},{7,6},{9,8},{10,9},{11,10},{13,12},{... | collective-permute-start | bytes 61448 | tf_op jit(solution)/shard_map/ppermute | solution.py:654
  2.9 5.7 %collective-permute-start.1 = (f32[5,8,128]{2,1,0:T(8,128)S(1)}, f32[5,8,128]{2,1,0:T(8,128)S(1)}, u32[]{:S(2)}, u32[]{:S(2)}) collective-permute-start(f32[5,8,128]{2,1,0:T(8,128)S(1)} %get-tuple-element.22), channel_id=1, source_target_pairs={{0,1},{1,2},{2,3},{4,5},{5,6},{6,7},{8,9},{9,10},{10,11},{12,13},{... | collective-permute-start | bytes 61448 | tf_op jit(solution)/shard_map/ppermute | solution.py:654
  8.6 0.0 collective-permute-done.mr
  8.6 0.9 collective-permute-done.1.ml
  9.5 3.2 %collective-permute-start.2 = (f32[25,8,128]{2,1,0:T(8,128)S(1)}, f32[25,8,128]{2,1,0:T(8,128)S(1)}, u32[]{:S(2)}, u32[]{:S(2)}) collective-permute-start(f32[25,8,128]{2,1,0:T(8,128)S(1)} %get-tuple-element.23), channel_id=1, source_target_pairs={{0,64},{64,128},{128,192},{192,256},{256,320},{320,384},{384,448},... | collective-permute-start | bytes 307208 | tf_op jit(solution)/shard_map/ppermute | solution.py:654
  12.7 1.3 %collective-permute-start.3 = (f32[25,8,128]{2,1,0:T(8,128)S(1)}, f32[25,8,128]{2,1,0:T(8,128)S(1)}, u32[]{:S(2)}, u32[]{:S(2)}) collective-permute-start(f32[25,8,128]{2,1,0:T(8,128)S(1)} %get-tuple-element.25), channel_id=1, source_target_pairs={{64,0},{128,64},{192,128},{256,192},{320,256},{384,320},{448,384},... | collective-permute-start | bytes 307208 | tf_op jit(solution)/shard_map/ppermute | solution.py:654
  14.0 0.4 collective-permute-done.2.low
  14.4 3.7 %collective-permute-done.3.high = f32[25,8,128]{2,1,0:T(8,128)S(1)} collective-permute-done((f32[25,8,128]{2,1,0:T(8,128)S(1)}, f32[25,8,128]{2,1,0:T(8,128)S(1)}, u32[]{:S(2)}, u32[]{:S(2)}) %collective-permute-start.3) | collective-permute-done | bytes 102432 | tf_op jit(solution)/shard_map/ppermute | solution.py:654
  18.1 0.1 shard_map.70
  18.2 5.2 %collective-permute-start.4 = (f32[53,8,128]{2,1,0:T(8,128)S(1)}, f32[53,8,128]{2,1,0:T(8,128)S(1)}, u32[]{:S(2)}, u32[]{:S(2)}) collective-permute-start(f32[53,8,128]{2,1,0:T(8,128)S(1)} %get-tuple-element.26), channel_id=1, source_target_pairs={{0,4},{4,8},{8,12},{12,16},{16,20},{20,24},{24,28},{28,32},{32,36}... | collective-permute-start | bytes 651272 | tf_op jit(solution)/shard_map/ppermute | solution.py:654
  23.4 1.3 %collective-permute-start.5 = (f32[53,8,128]{2,1,0:T(8,128)S(1)}, f32[53,8,128]{2,1,0:T(8,128)S(1)}, u32[]{:S(2)}, u32[]{:S(2)}) collective-permute-start(f32[53,8,128]{2,1,0:T(8,128)S(1)} %get-tuple-element.27), channel_id=1, source_target_pairs={{0,60},{4,0},{8,4},{12,8},{16,12},{20,16},{24,20},{28,24},{32,28},... | collective-permute-start | bytes 651272 | tf_op jit(solution)/shard_map/ppermute | solution.py:654
  24.7 0.2 shard_map.71
  24.9 1.3 %collective-permute-done.4.below = f32[53,8,128]{2,1,0:T(8,128)S(1)} collective-permute-done((f32[53,8,128]{2,1,0:T(8,128)S(1)}, f32[53,8,128]{2,1,0:T(8,128)S(1)}, u32[]{:S(2)}, u32[]{:S(2)}) %collective-permute-start.4) | collective-permute-done | bytes 217120 | tf_op jit(solution)/shard_map/ppermute | solution.py:654
  26.2 2.8 %collective-permute-done.5.above = f32[53,8,128]{2,1,0:T(8,128)S(1)} collective-permute-done((f32[53,8,128]{2,1,0:T(8,128)S(1)}, f32[53,8,128]{2,1,0:T(8,128)S(1)}, u32[]{:S(2)}, u32[]{:S(2)}) %collective-permute-start.5) | collective-permute-done | bytes 217120 | tf_op jit(solution)/shard_map/ppermute | solution.py:654
  29.0 3.3 %shard_map.72 = (f32[6,24,24,256]{3,2,1,0:T(8,128)S(1)}, s32[24,24,256]{2,1,0:T(8,128)S(1)}, f32[64,2,128]{2,1,0:T(2,128)S(1)}, f32[24,8,128]{2,1,0:T(8,128)S(1)...) custom-call(f32[25,8,128]{2,1,0:T(8,128)S(1)} %collective-permute-done.2.low, ...), custom_call_target="tpu_custom_call" | custom-call | tf_op jit(solution)/shard_map/pallas_call | solution.py:681
  32.3 28.6 %all_to_all.20.values.first = f32[64,2,128]{2,1,0:T(2,128)S(1)} all-to-all(f32[64,2,128]{2,1,0:T(2,128)S(1)} %get-tuple-element.32), channel_id=1, replica_groups=mesh['gx'=8,'gy'=16,'col'=4] {'gy','col'}, dimensions={0} | all-to-all | bytes 131072 | tf_op jit(solution)/shard_map/all_to_all | solution.py:693
  60.9 0.7 shard_map.73
  61.6 10.9 %all_to_all.21.parts = f32[8,16,128]{2,1,0:T(8,128)S(1)} all-to-all(f32[8,16,128]{2,1,0:T(8,128)S(1)} %shard_map.73), channel_id=1, replica_groups=mesh['gx'=8,'gy'=16,'col'=4] {'gx'}, dimensions={0} | all-to-all | bytes 131072 | tf_op jit(solution)/shard_map/all_to_all | solution.py:697
  72.6 6.0 %shard_map.74 = f32[64,4,128]{2,1,0:T(4,128)S(1)} custom-call(f32[8,16,128]{2,1,0:T(8,128)S(1)} %all_to_all.21.parts, f32[6,24,24,256]{3,2,1,0:T(8,128)S(1)} %get-tuple-element.33.weights, s32[24,24,256]{2,1,0:T(8,128)S(1)} %get-tuple-element.34.labels, s32[3,3,8,128]{3,2,1,0:T(8,128)S(1)} %get-tuple-element.35.asg, ...), custom_call_target="tpu_custom_call" | custom-call | tf_op jit(solution)/shard_map/pallas_call | solution.py:699
  78.6 18.2 %all_to_all.22.values = f32[64,4,128]{2,1,0:T(4,128)S(1)} all-to-all(f32[64,4,128]{2,1,0:T(4,128)S(1)} %shard_map.74), channel_id=1, replica_groups=mesh['gx'=8,'gy'=16,'col'=4] {'gy','col'}, dimensions={0} | all-to-all | bytes 262144 | tf_op jit(solution)/shard_map/all_to_all | solution.py:705
  96.8 1.1 %shard_map.75 = f32[8,24,128]{2,1,0:T(8,128)S(1)} custom-call(f32[64,4,128]{2,1,0:T(4,128)S(1)} %all_to_all.22.values, f32[64,2,128]{2,1,0:T(2,128)S(1)} %all_to_all.20.values.first), custom_call_target="tpu_custom_call" | custom-call | tf_op jit(solution)/shard_map/pallas_call | solution.py:706
  97.9 7.7 %all_to_all.23.images = f32[8,24,128]{2,1,0:T(8,128)S(1)} all-to-all(f32[8,24,128]{2,1,0:T(8,128)S(1)} %shard_map.75), channel_id=1, replica_groups=mesh['gx'=8,'gy'=16,'col'=4] {'gx'}, dimensions={0} | all-to-all | bytes 196608 | tf_op jit(solution)/shard_map/all_to_all | solution.py:709
  105.6 2.6 %shard_map.76 = (f32[8,8,128]{2,1,0:T(8,128)}, f32[1,16]{1,0:T(1,128)}) custom-call(f32[8,16,128]{2,1,0:T(8,128)S(1)} %all_to_all.21.parts, f32[8,24,128]{2,1,0:T(8,128)S(1)} %all_to_all.23.images, f32[6,24,24,256]{3,2,1,0:T(8,128)S(1)} %get-tuple-element.33.weights, s32[24,24,256]{2,1,0:T(8,128)S(1)} %get-tuple-element.34.labels, ...), custom_call_target="tpu_custom_call" | custom-call | tf_op jit(solution)/shard_map/pallas_call | solution.py:710
  (1 shorter events, 0.0 us)
Async XLA Ops:
  1.6 7.0 %collective-permute-start = (f32[5,8,128]{2,1,0:T(8,128)S(1)}, f32[5,8,128]{2,1,0:T(8,128)S(1)}, u32[]{:S(2)}, u32[]{:S(2)}) collective-permute-start(f32[5,8,128]{2,1,0:T(8,128)S(1)} %get-tuple-element.21), channel_id=1, source_target_pairs={{1,0},{2,1},{3,2},{5,4},{6,5},{7,6},{9,8},{10,9},{11,10},{13,12},{... | collective-permute-start | bytes 61448 | tf_op jit(solution)/shard_map/ppermute | solution.py:654
  2.9 6.6 %collective-permute-start.1 = (f32[5,8,128]{2,1,0:T(8,128)S(1)}, f32[5,8,128]{2,1,0:T(8,128)S(1)}, u32[]{:S(2)}, u32[]{:S(2)}) collective-permute-start(f32[5,8,128]{2,1,0:T(8,128)S(1)} %get-tuple-element.22), channel_id=1, source_target_pairs={{0,1},{1,2},{2,3},{4,5},{5,6},{6,7},{8,9},{9,10},{10,11},{12,13},{... | collective-permute-start | bytes 61448 | tf_op jit(solution)/shard_map/ppermute | solution.py:654
  9.5 4.8 %collective-permute-start.2 = (f32[25,8,128]{2,1,0:T(8,128)S(1)}, f32[25,8,128]{2,1,0:T(8,128)S(1)}, u32[]{:S(2)}, u32[]{:S(2)}) collective-permute-start(f32[25,8,128]{2,1,0:T(8,128)S(1)} %get-tuple-element.23), channel_id=1, source_target_pairs={{0,64},{64,128},{128,192},{192,256},{256,320},{320,384},{384,448},... | collective-permute-start | bytes 307208 | tf_op jit(solution)/shard_map/ppermute | solution.py:654
  12.7 5.4 %collective-permute-start.3 = (f32[25,8,128]{2,1,0:T(8,128)S(1)}, f32[25,8,128]{2,1,0:T(8,128)S(1)}, u32[]{:S(2)}, u32[]{:S(2)}) collective-permute-start(f32[25,8,128]{2,1,0:T(8,128)S(1)} %get-tuple-element.25), channel_id=1, source_target_pairs={{64,0},{128,64},{192,128},{256,192},{320,256},{384,320},{448,384},... | collective-permute-start | bytes 307208 | tf_op jit(solution)/shard_map/ppermute | solution.py:654
  18.2 8.1 %collective-permute-start.4 = (f32[53,8,128]{2,1,0:T(8,128)S(1)}, f32[53,8,128]{2,1,0:T(8,128)S(1)}, u32[]{:S(2)}, u32[]{:S(2)}) collective-permute-start(f32[53,8,128]{2,1,0:T(8,128)S(1)} %get-tuple-element.26), channel_id=1, source_target_pairs={{0,4},{4,8},{8,12},{12,16},{16,20},{20,24},{24,28},{28,32},{32,36}... | collective-permute-start | bytes 651272 | tf_op jit(solution)/shard_map/ppermute | solution.py:654
  23.4 5.6 %collective-permute-start.5 = (f32[53,8,128]{2,1,0:T(8,128)S(1)}, f32[53,8,128]{2,1,0:T(8,128)S(1)}, u32[]{:S(2)}, u32[]{:S(2)}) collective-permute-start(f32[53,8,128]{2,1,0:T(8,128)S(1)} %get-tuple-element.27), channel_id=1, source_target_pairs={{0,60},{4,0},{8,4},{12,8},{16,12},{20,16},{24,20},{28,24},{32,28},... | collective-permute-start | bytes 651272 | tf_op jit(solution)/shard_map/ppermute | solution.py:654

commit v12 on v11

--- a/solution.py
+++ b/solution.py
@@ -586,7 +586,8 @@
                 ends[2, q : q + 1, :] = plane[0:1] * -paths[2, q : q + 1, :]
                 ends[3, q : q + 1, :] = plane[B - 1 : B] * -paths[3, q : q + 1, :]
 
-    sweeps(both, weights, 0, 7, after=after, operator_at=4)
+    sweeps(both, weights, 0, 4, after=after, operator_at=4)
+    sweeps(both, weights, 5, 7, size=NP - 10)
     tiles = [own_tile(both.at[0], weights, B + q) * dvals[B + q] for q in range(B)]
     label_tiles = [labels[B + q, r, 0:LZ] for q in range(B)]
     beyond = [labels[2 * B, r, 0:LZ], labels[B - 1, r, 0:LZ]]

time: 109 us -> 109 us (level)
  no operation moved by 1% of the time
where the time goes in v12:
time: 109 us; the launch traced here: 108 us
  blocking collectives  65.4 us (60%)
  starting transfers between devices  17.9 us (16%)
  Pallas kernels  14.9 us (14%)
  waiting for transfers between devices  9.08 us (8%)
    all_to_all x1, blocking collectives, on_device(): bricks = lax.all_to_all(chunk, ('gy', 'col'), 0, 0, tiled=True)  28.6 us
    all_to_all x1, blocking collectives, on_device(): images = lax.all_to_all(chunk, ('gy', 'col'), 0, 0, tiled=True)  18.2 us
    ppermute x6, starting transfers between devices, send(): return lax.ppermute(x, axis, steps(lax.axis_size(axis), by, wrap))  17.9 us
    all_to_all x1, blocking collectives, on_device(): parts = lax.all_to_all(parts, 'gx', 0, 0, tiled=True)  10.9 us
    ppermute x6, waiting for transfers between devices, send(): return lax.ppermute(x, axis, steps(lax.axis_size(axis), by, wrap))  9.08 us
    all_to_all x1, blocking collectives, on_device(): images = lax.all_to_all(images, 'gx', 0, 0, tiled=True)  7.68 us
    pallas_call x1, Pallas kernels, on_device(): call(functools.partial(second_sums, *sizes), sds(n_bricks, 4, LZ), 6, scr...  5.84 us
    pallas_call x1, Pallas kernels, on_device(): call(functools.partial(first_sums, *sizes), [sds(6, NP, *FULL), sds(NP, *...  3.25 us
  transfers between devices with their start and end apart: 6, of which 5 were waited for; matrix products, arithmetic and copies ran while one was open for 0% of the time, Pallas kernels for 0%

profile of v12, /device:TPU:1, one launch (start us, length us, event | category | flops | bytes accessed | tf_op | source)
XLA Modules:
  0.0 108.0 jit_solution(18031726771040414020)
XLA Ops:
  0.6 1.0 shard_map.68
  1.6 1.3 %collective-permute-start = (f32[5,8,128]{2,1,0:T(8,128)S(1)}, f32[5,8,128]{2,1,0:T(8,128)S(1)}, u32[]{:S(2)}, u32[]{:S(2)}) collective-permute-start(f32[5,8,128]{2,1,0:T(8,128)S(1)} %get-tuple-element.21), channel_id=1, source_target_pairs={{1,0},{2,1},{3,2},{5,4},{6,5},{7,6},{9,8},{10,9},{11,10},{13,12},{... | collective-permute-start | bytes 61448 | tf_op jit(solution)/shard_map/ppermute | solution.py:655
  2.9 5.7 %collective-permute-start.1 = (f32[5,8,128]{2,1,0:T(8,128)S(1)}, f32[5,8,128]{2,1,0:T(8,128)S(1)}, u32[]{:S(2)}, u32[]{:S(2)}) collective-permute-start(f32[5,8,128]{2,1,0:T(8,128)S(1)} %get-tuple-element.22), channel_id=1, source_target_pairs={{0,1},{1,2},{2,3},{4,5},{5,6},{6,7},{8,9},{9,10},{10,11},{12,13},{... | collective-permute-start | bytes 61448 | tf_op jit(solution)/shard_map/ppermute | solution.py:655
  8.6 0.0 collective-permute-done.mr
  8.6 0.9 collective-permute-done.1.ml
  9.5 3.2 %collective-permute-start.2 = (f32[25,8,128]{2,1,0:T(8,128)S(1)}, f32[25,8,128]{2,1,0:T(8,128)S(1)}, u32[]{:S(2)}, u32[]{:S(2)}) collective-permute-start(f32[25,8,128]{2,1,0:T(8,128)S(1)} %get-tuple-element.23), channel_id=1, source_target_pairs={{0,64},{64,128},{128,192},{192,256},{256,320},{320,384},{384,448},... | collective-permute-start | bytes 307208 | tf_op jit(solution)/shard_map/ppermute | solution.py:655
  12.7 1.3 %collective-permute-start.3 = (f32[25,8,128]{2,1,0:T(8,128)S(1)}, f32[25,8,128]{2,1,0:T(8,128)S(1)}, u32[]{:S(2)}, u32[]{:S(2)}) collective-permute-start(f32[25,8,128]{2,1,0:T(8,128)S(1)} %get-tuple-element.25), channel_id=1, source_target_pairs={{64,0},{128,64},{192,128},{256,192},{320,256},{384,320},{448,384},... | collective-permute-start | bytes 307208 | tf_op jit(solution)/shard_map/ppermute | solution.py:655
  14.0 0.4 collective-permute-done.2.low
  14.4 3.7 %collective-permute-done.3.high = f32[25,8,128]{2,1,0:T(8,128)S(1)} collective-permute-done((f32[25,8,128]{2,1,0:T(8,128)S(1)}, f32[25,8,128]{2,1,0:T(8,128)S(1)}, u32[]{:S(2)}, u32[]{:S(2)}) %collective-permute-start.3) | collective-permute-done | bytes 102432 | tf_op jit(solution)/shard_map/ppermute | solution.py:655
  18.1 0.1 shard_map.70
  18.2 5.2 %collective-permute-start.4 = (f32[53,8,128]{2,1,0:T(8,128)S(1)}, f32[53,8,128]{2,1,0:T(8,128)S(1)}, u32[]{:S(2)}, u32[]{:S(2)}) collective-permute-start(f32[53,8,128]{2,1,0:T(8,128)S(1)} %get-tuple-element.26), channel_id=1, source_target_pairs={{0,4},{4,8},{8,12},{12,16},{16,20},{20,24},{24,28},{28,32},{32,36}... | collective-permute-start | bytes 651272 | tf_op jit(solution)/shard_map/ppermute | solution.py:655
  23.4 1.3 %collective-permute-start.5 = (f32[53,8,128]{2,1,0:T(8,128)S(1)}, f32[53,8,128]{2,1,0:T(8,128)S(1)}, u32[]{:S(2)}, u32[]{:S(2)}) collective-permute-start(f32[53,8,128]{2,1,0:T(8,128)S(1)} %get-tuple-element.27), channel_id=1, source_target_pairs={{0,60},{4,0},{8,4},{12,8},{16,12},{20,16},{24,20},{28,24},{32,28},... | collective-permute-start | bytes 651272 | tf_op jit(solution)/shard_map/ppermute | solution.py:655
  24.7 0.2 shard_map.71
  24.9 1.3 %collective-permute-done.4.below = f32[53,8,128]{2,1,0:T(8,128)S(1)} collective-permute-done((f32[53,8,128]{2,1,0:T(8,128)S(1)}, f32[53,8,128]{2,1,0:T(8,128)S(1)}, u32[]{:S(2)}, u32[]{:S(2)}) %collective-permute-start.4) | collective-permute-done | bytes 217120 | tf_op jit(solution)/shard_map/ppermute | solution.py:655
  26.2 2.8 %collective-permute-done.5.above = f32[53,8,128]{2,1,0:T(8,128)S(1)} collective-permute-done((f32[53,8,128]{2,1,0:T(8,128)S(1)}, f32[53,8,128]{2,1,0:T(8,128)S(1)}, u32[]{:S(2)}, u32[]{:S(2)}) %collective-permute-start.5) | collective-permute-done | bytes 217120 | tf_op jit(solution)/shard_map/ppermute | solution.py:655
  29.0 3.3 %shard_map.72 = (f32[6,24,24,256]{3,2,1,0:T(8,128)S(1)}, s32[24,24,256]{2,1,0:T(8,128)S(1)}, f32[64,2,128]{2,1,0:T(2,128)S(1)}, f32[24,8,128]{2,1,0:T(8,128)S(1)...) custom-call(f32[25,8,128]{2,1,0:T(8,128)S(1)} %collective-permute-done.2.low, ...), custom_call_target="tpu_custom_call" | custom-call | tf_op jit(solution)/shard_map/pallas_call | solution.py:682
  32.3 28.6 %all_to_all.20.values.first = f32[64,2,128]{2,1,0:T(2,128)S(1)} all-to-all(f32[64,2,128]{2,1,0:T(2,128)S(1)} %get-tuple-element.32), channel_id=1, replica_groups=mesh['gx'=8,'gy'=16,'col'=4] {'gy','col'}, dimensions={0} | all-to-all | bytes 131072 | tf_op jit(solution)/shard_map/all_to_all | solution.py:694
  60.9 0.7 shard_map.73
  61.6 10.9 %all_to_all.21.parts = f32[8,16,128]{2,1,0:T(8,128)S(1)} all-to-all(f32[8,16,128]{2,1,0:T(8,128)S(1)} %shard_map.73), channel_id=1, replica_groups=mesh['gx'=8,'gy'=16,'col'=4] {'gx'}, dimensions={0} | all-to-all | bytes 131072 | tf_op jit(solution)/shard_map/all_to_all | solution.py:698
  72.6 5.8 %shard_map.74 = f32[64,4,128]{2,1,0:T(4,128)S(1)} custom-call(f32[8,16,128]{2,1,0:T(8,128)S(1)} %all_to_all.21.parts, f32[6,24,24,256]{3,2,1,0:T(8,128)S(1)} %get-tuple-element.33.weights, s32[24,24,256]{2,1,0:T(8,128)S(1)} %get-tuple-element.34.labels, s32[3,3,8,128]{3,2,1,0:T(8,128)S(1)} %get-tuple-element.35.asg, ...), custom_call_target="tpu_custom_call" | custom-call | tf_op jit(solution)/shard_map/pallas_call | solution.py:700
  78.4 18.2 %all_to_all.22.values = f32[64,4,128]{2,1,0:T(4,128)S(1)} all-to-all(f32[64,4,128]{2,1,0:T(4,128)S(1)} %shard_map.74), channel_id=1, replica_groups=mesh['gx'=8,'gy'=16,'col'=4] {'gy','col'}, dimensions={0} | all-to-all | bytes 262144 | tf_op jit(solution)/shard_map/all_to_all | solution.py:706
  96.6 1.1 %shard_map.75 = f32[8,24,128]{2,1,0:T(8,128)S(1)} custom-call(f32[64,4,128]{2,1,0:T(4,128)S(1)} %all_to_all.22.values, f32[64,2,128]{2,1,0:T(2,128)S(1)} %all_to_all.20.values.first), custom_call_target="tpu_custom_call" | custom-call | tf_op jit(solution)/shard_map/pallas_call | solution.py:707
  97.7 7.7 %all_to_all.23.images = f32[8,24,128]{2,1,0:T(8,128)S(1)} all-to-all(f32[8,24,128]{2,1,0:T(8,128)S(1)} %shard_map.75), channel_id=1, replica_groups=mesh['gx'=8,'gy'=16,'col'=4] {'gx'}, dimensions={0} | all-to-all | bytes 196608 | tf_op jit(solution)/shard_map/all_to_all | solution.py:710
  105.4 2.6 %shard_map.76 = (f32[8,8,128]{2,1,0:T(8,128)}, f32[1,16]{1,0:T(1,128)}) custom-call(f32[8,16,128]{2,1,0:T(8,128)S(1)} %all_to_all.21.parts, f32[8,24,128]{2,1,0:T(8,128)S(1)} %all_to_all.23.images, f32[6,24,24,256]{3,2,1,0:T(8,128)S(1)} %get-tuple-element.33.weights, s32[24,24,256]{2,1,0:T(8,128)S(1)} %get-tuple-element.34.labels, ...), custom_call_target="tpu_custom_call" | custom-call | tf_op jit(solution)/shard_map/pallas_call | solution.py:711
  (1 shorter events, 0.0 us)
Async XLA Ops:
  1.6 7.0 %collective-permute-start = (f32[5,8,128]{2,1,0:T(8,128)S(1)}, f32[5,8,128]{2,1,0:T(8,128)S(1)}, u32[]{:S(2)}, u32[]{:S(2)}) collective-permute-start(f32[5,8,128]{2,1,0:T(8,128)S(1)} %get-tuple-element.21), channel_id=1, source_target_pairs={{1,0},{2,1},{3,2},{5,4},{6,5},{7,6},{9,8},{10,9},{11,10},{13,12},{... | collective-permute-start | bytes 61448 | tf_op jit(solution)/shard_map/ppermute | solution.py:655
  2.9 6.6 %collective-permute-start.1 = (f32[5,8,128]{2,1,0:T(8,128)S(1)}, f32[5,8,128]{2,1,0:T(8,128)S(1)}, u32[]{:S(2)}, u32[]{:S(2)}) collective-permute-start(f32[5,8,128]{2,1,0:T(8,128)S(1)} %get-tuple-element.22), channel_id=1, source_target_pairs={{0,1},{1,2},{2,3},{4,5},{5,6},{6,7},{8,9},{9,10},{10,11},{12,13},{... | collective-permute-start | bytes 61448 | tf_op jit(solution)/shard_map/ppermute | solution.py:655
  9.5 4.8 %collective-permute-start.2 = (f32[25,8,128]{2,1,0:T(8,128)S(1)}, f32[25,8,128]{2,1,0:T(8,128)S(1)}, u32[]{:S(2)}, u32[]{:S(2)}) collective-permute-start(f32[25,8,128]{2,1,0:T(8,128)S(1)} %get-tuple-element.23), channel_id=1, source_target_pairs={{0,64},{64,128},{128,192},{192,256},{256,320},{320,384},{384,448},... | collective-permute-start | bytes 307208 | tf_op jit(solution)/shard_map/ppermute | solution.py:655
  12.7 5.4 %collective-permute-start.3 = (f32[25,8,128]{2,1,0:T(8,128)S(1)}, f32[25,8,128]{2,1,0:T(8,128)S(1)}, u32[]{:S(2)}, u32[]{:S(2)}) collective-permute-start(f32[25,8,128]{2,1,0:T(8,128)S(1)} %get-tuple-element.25), channel_id=1, source_target_pairs={{64,0},{128,64},{192,128},{256,192},{320,256},{384,320},{448,384},... | collective-permute-start | bytes 307208 | tf_op jit(solution)/shard_map/ppermute | solution.py:655
  18.2 8.1 %collective-permute-start.4 = (f32[53,8,128]{2,1,0:T(8,128)S(1)}, f32[53,8,128]{2,1,0:T(8,128)S(1)}, u32[]{:S(2)}, u32[]{:S(2)}) collective-permute-start(f32[53,8,128]{2,1,0:T(8,128)S(1)} %get-tuple-element.26), channel_id=1, source_target_pairs={{0,4},{4,8},{8,12},{12,16},{16,20},{20,24},{24,28},{28,32},{32,36}... | collective-permute-start | bytes 651272 | tf_op jit(solution)/shard_map/ppermute | solution.py:655
  23.4 5.6 %collective-permute-start.5 = (f32[53,8,128]{2,1,0:T(8,128)S(1)}, f32[53,8,128]{2,1,0:T(8,128)S(1)}, u32[]{:S(2)}, u32[]{:S(2)}) collective-permute-start(f32[53,8,128]{2,1,0:T(8,128)S(1)} %get-tuple-element.27), channel_id=1, source_target_pairs={{0,60},{4,0},{8,4},{12,8},{16,12},{20,16},{24,20},{28,24},{32,28},... | collective-permute-start | bytes 651272 | tf_op jit(solution)/shard_map/ppermute | solution.py:655
